TPU v7x, 128 devices: a whole 4x4x4 slice. The times are simulated.
128 devices in a mesh: dp: 16 (over z, y_hi, core), tensor: 8 (over x, y_lo).
Axes of the slice: x: 4, y: 4 (y_hi: 2, y_lo: 2; y = y_hi * 2 + y_lo), z: 4, core: 2. Of those that a mesh axis runs over, the one named last changes fastest.
Arguments:
- encoded_neighbours: bfloat16 [128, 128, 8192], P('dp'), may hold values from -6 to 6
- kv_weight: bfloat16 [2, 8192, 4096], P(None, 'dp', 'tensor'), may hold values from -0.0625 to 0.0625
- queries: bfloat16 [4096, 4096], P('dp', 'tensor'), may hold values from -480 to 480
- out_weight: bfloat16 [4096, 8192], P('tensor'), may hold values from -0.09375 to 0.09375
- neighbour_ids: int32 [16, 4, 2, 128], P('dp'), may hold values from 0 to 31999, as said below
- slot_map: int32 [128], replicated, may hold values from 0 to 127, as said below
Outputs:
- mixed: bfloat16 [4096, 8192], P('dp', 'tensor')
Inputs may be any that keep to these rules, and one draw needn't show every extreme that they name: `neighbour_ids`: 0 marks padding and only ends a neighbour; each neighbour has at least 32 tokens that are not 0, and every sequence has a neighbour without padding. `slot_map`: A permutation of the neighbours; slots i with equal i // 8 lie on one index of dp, and the 8 neighbours of one sequence lie in 8 different such blocks.
All inputs are finite; a program needn't handle non-finite values.
Results may differ from a plain program's by a relative error of at most 0.008.
The roundings to bfloat16 on the way count: a program that leaves them out, or rounds other values in their place, can miss the bound.
Values may be sent and summed in bfloat16 or wider, within the bound.
No kernel may reach another device: no remote copies, remote signals or barrier semaphores. Data moves between devices by JAX's collectives and lax.ppermute only.
A program may use at most 128 MiB of HBM per device.

v0:
```python
import math

import jax
import jax.numpy as jnp
from jax import lax
from jax.sharding import PartitionSpec as P

HD = 128
M = 64


def attend_stretches(query_rows, key_rows, value_rows, key_valid):
    length, columns = query_rows.shape
    stretches, key_span = key_valid.shape
    head_count = columns // HD
    lead_rows = M - 1
    shifted = jnp.concatenate(
        [query_rows[lead_rows:], jnp.zeros((lead_rows, columns), query_rows.dtype)], axis=0
    )
    query_blocks = shifted.reshape(stretches, M, head_count, HD)
    key_blocks = key_rows.reshape(stretches, key_span, head_count, HD)
    value_blocks = value_rows.reshape(stretches, key_span, head_count, HD)
    scores = jnp.einsum(
        "cmhd,cnhd->chmn", query_blocks, key_blocks, preferred_element_type=jnp.float32
    ) * (1.0 / math.sqrt(HD))
    scores = jnp.where(key_valid[:, None, None, :], scores, -jnp.inf)
    highest = jnp.max(scores, axis=-1, keepdims=True)
    raised = jnp.exp(scores - highest)
    weights = (raised / jnp.sum(raised, axis=-1, keepdims=True)).astype(jnp.bfloat16)
    mixed_heads = jnp.einsum(
        "chmn,cnhd->cmhd", weights, value_blocks, preferred_element_type=jnp.float32
    ).astype(jnp.bfloat16)
    flat_rows = mixed_heads.reshape(stretches * M, columns)
    return jnp.concatenate(
        [jnp.zeros((lead_rows, columns), jnp.bfloat16), flat_rows[: length - lead_rows]], axis=0
    )


def body(encoded_neighbours, kv_weight, queries, out_weight, neighbour_ids, slot_map):
    group_size = lax.axis_size("dp")
    position = lax.axis_index("dp")
    slot_count, span_rows, model_width = encoded_neighbours.shape
    columns = queries.shape[1]
    encoded = encoded_neighbours.reshape(slot_count * span_rows, model_width)
    weight_piece = lax.all_gather(kv_weight, "dp", axis=1, tiled=True)
    key_sums = jnp.dot(encoded, weight_piece[0], preferred_element_type=jnp.float32)
    value_sums = jnp.dot(encoded, weight_piece[1], preferred_element_type=jnp.float32)
    projected = jnp.stack([key_sums.astype(jnp.bfloat16), value_sums.astype(jnp.bfloat16)]).reshape(
        2, slot_count, span_rows, columns
    )
    held_ids = lax.dynamic_slice_in_dim(slot_map, position * slot_count, slot_count)
    owners = held_ids // slot_count
    routing = (owners[None, :] == jnp.arange(group_size, dtype=jnp.int32)[:, None]).astype(
        jnp.bfloat16
    )
    outgoing = jnp.einsum(
        "ds,asrh->adrh", routing, projected, preferred_element_type=jnp.float32
    ).astype(jnp.bfloat16)
    incoming = lax.all_to_all(outgoing, "dp", split_axis=1, concat_axis=1, tiled=True)
    wanted = position * slot_count + jnp.arange(slot_count, dtype=jnp.int32)
    found_mask = slot_map[None, :] == wanted[:, None]
    holder = (
        jnp.sum(
            jnp.where(found_mask, jnp.arange(slot_map.shape[0], dtype=jnp.int32)[None, :], 0),
            axis=1,
        )
        // slot_count
    )
    selector = (holder[:, None] == jnp.arange(group_size, dtype=jnp.int32)[None, :]).astype(
        jnp.bfloat16
    )
    ordered = jnp.einsum(
        "qd,adrh->aqrh", selector, incoming, preferred_element_type=jnp.float32
    ).astype(jnp.bfloat16)
    stretches = slot_count // 2
    ordered = ordered.reshape(2, stretches, 2 * span_rows, columns)
    key_valid = neighbour_ids.reshape(stretches, 2 * span_rows) != 0
    attended = attend_stretches(queries, ordered[0], ordered[1], key_valid)
    partial_value = jnp.dot(attended, out_weight, preferred_element_type=jnp.float32)
    share_cols = partial_value.shape[1] // lax.axis_size("tensor")
    full_sum = lax.psum(partial_value, "tensor")
    result = lax.dynamic_slice_in_dim(
        full_sum, lax.axis_index("tensor") * share_cols, share_cols, 1
    )
    return result.astype(jnp.bfloat16)


def solution(mesh):
    placed = (
        P("dp", None, None),
        P(None, "dp", "tensor"),
        P("dp", "tensor"),
        P("tensor", None),
        P("dp", None, None, None),
        P(),
    )
    return jax.shard_map(
        body, mesh=mesh, in_specs=placed, out_specs=P("dp", "tensor"), check_vma=False
    )
```

profile of v0, /device:TPU:0, one launch (start us, length us, event | category | flops | bytes accessed | tf_op | source)
XLA Modules:
  0.0 566.5 jit_solution(16680682754666074645)
XLA Ops:
  6.5 0.0 all-gather.2.cloned.1.call-start
  6.5 0.7 all-gather.2.cloned.1.call-update
  7.3 0.7 and_select_fusion.1
  8.0 113.7 %all-gather.2.cloned.1.call-done = bf16[2,8192,512]{2,1,0:T(8,128)(2,1)} async-done(((bf16[2,512,512]{2,1,0:T(8,128)(2,1)}), bf16[2,8192,512]{2,1,0:T(8,128)(2,1)}) %all-gather.2.cloned.1.call-update) | async-done | bytes 16777232 | tf_op jit(solution)/shard_map/all_gather | solution.py:45
  121.7 14.8 %fusion.11 = bf16[1024,512]{1,0:T(8,128)(2,1)S(1)} fusion(bf16[1024,8192]{1,0:T(8,128)(2,1)} %bitcast.54, bf16[2,8192,512]{2,1,0:T(8,128)(2,1)} %all-gather.2.cloned.1.call-done), kind=kOutput, calls=%fused_computation.13 | convolution fusion | flops 8590458880 | bytes 26214400 | tf_op jit(solution)/shard_map/dot_general | solution.py:47
  136.5 0.6 copy.24
  137.1 14.8 %fusion.10 = bf16[1024,512]{1,0:T(8,128)(2,1)S(1)} fusion(bf16[1024,8192]{1,0:T(8,128)(2,1)} %bitcast.55, bf16[2,8192,512]{2,1,0:T(8,128)(2,1)} %all-gather.2.cloned.1.call-done), kind=kOutput, calls=%fused_computation.12 | convolution fusion | flops 8590458880 | bytes 26214400 | tf_op jit(solution)/shard_map/dot_general | solution.py:46
  151.9 0.6 copy.23
  152.5 1.4 convert_bitcast_fusion
  153.8 0.0 copy-start.1
  153.8 0.0 copy-start
  153.8 0.0 copy-start.2
  153.9 4.4 copy.25
  158.2 4.7 all-to-all-start
  162.9 0.0 copy-done.1
  163.0 0.0 copy-done
  163.0 0.1 slice.23
  163.1 0.1 reshape.53
  163.2 0.0 copy-done.2
  163.2 0.2 select_reduce_fusion
  163.4 51.2 %all-to-all-done = bf16[2,16,128,512]{3,2,0,1:T(8,128)(2,1)} async-done(((bf16[2,16,128,512]{3,2,0,1:T(8,128)(2,1)}), bf16[2,16,128,512]{3,2,0,1:T(8,128)(2,1)}, u32[]{:S(2)}, u32[]{:S(2)}) %all-to-all-start) | async-done | bytes 4194336 | tf_op jit(solution)/shard_map/all_to_all | solution.py:59
  214.6 4.7 convert_bitcast_fusion.1
  219.3 0.1 fusion.31
  219.4 0.3 copy.27
  219.7 0.3 reshape_squeeze.6
  220.0 0.3 copy.28
  220.3 0.3 reshape_squeeze.7
  220.6 0.5 fusion.14
  221.1 0.4 fusion.32
  221.5 1.9 fusion.15
  223.3 0.2 copy.32
  223.6 9.0 %fusion.20 = f32[256,8192]{1,0:T(8,128)} fusion(bf16[512,8192]{1,0:T(8,128)(2,1)} %param.9, bf16[193,512]{1,0:T(8,128)(2,1)S(1)} %slice.30), kind=kOutput, calls=%fused_computation.27 | convolution fusion | flops 2147483648 | bytes 16974848 | tf_op jit(solution)/shard_map/dot_general | solution.py:79
  232.6 325.2 %all-reduce.3 = bf16[256,8192]{1,0:T(8,128)(2,1)} all-reduce(f32[256,8192]{1,0:T(8,128)} %fusion.20), channel_id=1, replica_groups=mesh['dp'=16,'tensor'=8] {'tensor'}, use_global_device_ids=true, to_apply=%region_3.4 | all-reduce | flops 2097152 | bytes 12582912 | tf_op jit(solution)/shard_map/psum | solution.py:81
  557.8 1.9 dynamic-slice_convert_fusion
  (7 shorter events, 0.1 us)
Async XLA Ops:
  6.5 115.2 %all-gather.2.cloned.1.call-start = ((), (), s32[]{:S(2)}) async-start(), calls=%async_computation.1 | async-start | bytes 17825792 | tf_op jit(solution)/shard_map/all_gather | solution.py:45
  153.8 9.1 %copy-start.1 = (s32[1,4,2,128]{3,2,1,0:T(2,128)S(1)}, s32[1,4,2,128]{3,2,1,0:T(2,128)}, u32[]{:S(2)}) copy-start(s32[1,4,2,128]{3,2,1,0:T(2,128)} %param.10) | copy-start | bytes 12292
  153.8 9.2 %copy-start = (bf16[256,512]{1,0:T(8,128)(2,1)S(1)}, bf16[256,512]{1,0:T(8,128)(2,1)}, u32[]{:S(2)}) copy-start(bf16[256,512]{1,0:T(8,128)(2,1)} %param.8) | copy-start | bytes 786436
  153.8 9.3 %copy-start.2 = (s32[128]{0:T(128)S(1)}, s32[128]{0:T(128)}, u32[]{:S(2)}) copy-start(s32[128]{0:T(128)} %param.11) | copy-start | bytes 1540
  158.2 56.4 %all-to-all-start = ((bf16[2,16,128,512]{3,2,0,1:T(8,128)(2,1)}), bf16[2,16,128,512]{3,2,0,1:T(8,128)(2,1)}, u32[]{:S(2)}, u32[]{:S(2)}) async-start(bf16[2,16,128,512]{3,2,0,1:T(8,128)(2,1)} %copy.25), calls=%async_computation | async-start | bytes 8388608 | tf_op jit(solution)/shard_map/all_to_all | solution.py:59
Sparse Core Ops, SparseCore 0:
  9.8 111.8 all-gather.1
where the time goes:
time: 568 us; the launch traced here: 567 us
  blocking collectives  325 us (57%)
  waiting for transfers between devices  166 us (29%)
  matrix products  46.8 us (8%)
  between operations  13.6 us (2%)
  local copies, waits for them, and re-layouts  9.16 us (2%)
    psum x1, blocking collectives, body(): full_sum = lax.psum(partial_value, 'tensor')  325 us
    all_gather x1, waiting for transfers between devices, body(): weight_piece = lax.all_gather(kv_weight, 'dp', axis=1, tiled=True)  114 us
    all_to_all x1, waiting for transfers between devices, body(): lax.all_to_all(outgoing, 'dp', split_axis=1, concat_axis=1, tiled=True)  51.2 us
    dot_general x1, matrix products, body(): jnp.dot(encoded, weight_piece[0], preferred_element_type=jnp.float32)  14.8 us
    dot_general x1, matrix products, body(): jnp.dot(encoded, weight_piece[1], preferred_element_type=jnp.float32)  14.8 us
  transfers between devices with their start and end apart: 2, of which 2 were waited for; matrix products, arithmetic and copies ran while one was open for 0% of the time, Pallas kernels for 0%

commit v1 on v0

v1 whole, which is shorter than its diff:
```python
import functools
import math

import jax
import jax.numpy as jnp
from jax import lax
from jax.experimental import pallas as pl
from jax.experimental.pallas import tpu as pltpu
from jax.sharding import PartitionSpec as P

HD = 128
M = 64
BF = jnp.bfloat16
F32 = jnp.float32
VMEM_LIMIT = 48 * 1024 * 1024


def dp_pairs(dz, dy, dc):
    pairs = []
    for i in range(16):
        z, y, c = i // 4, (i // 2) % 2, i % 2
        pairs.append((i, ((z + dz) % 4) * 4 + ((y + dy) % 2) * 2 + (c + dc) % 2))
    return pairs


def tensor_pairs(dx, dy):
    pairs = []
    for i in range(8):
        x, y = i // 2, i % 2
        pairs.append((i, ((x + dx) % 4) * 2 + (y + dy) % 2))
    return pairs


Z_UP, Z_DOWN = dp_pairs(1, 0, 0), dp_pairs(-1, 0, 0)
Y_SWAP, CORE_SWAP = dp_pairs(0, 1, 0), dp_pairs(0, 0, 1)


def vmem_specs(count):
    return [pl.BlockSpec(memory_space=pltpu.VMEM)] * count


def project_kernel(blocks, has_total, final, idx, *refs):
    del idx
    rows = refs[:blocks]
    weights = refs[blocks : 2 * blocks]
    rest = refs[2 * blocks :]
    out = rest[-1]
    columns = weights[0].shape[2]
    for side in range(2):
        cols = slice(side * columns, (side + 1) * columns)
        total = rest[0][:, cols] if has_total else None
        for row, weight in zip(rows, weights):
            term = jnp.dot(row[...], weight[side], preferred_element_type=F32)
            total = term if total is None else total + term
        out[:, cols] = total.astype(out.dtype)


def project(encoded, pieces, total, final):
    rows = encoded.shape[0]
    depth, columns = pieces[0][1].shape[1:]
    tile = 256
    blocks = len(pieces)
    idx = jnp.stack([place for place, _ in pieces]).astype(jnp.int32)

    def row_spec(j):
        return pl.BlockSpec((tile, depth), lambda m, i, j=j: (m, i[j]))

    in_specs = [row_spec(j) for j in range(blocks)] + [
        pl.BlockSpec((2, depth, columns), lambda m, i: (0, 0, 0), pipeline_mode=pl.Buffered(1))
    ] * blocks
    operands = [encoded] * blocks + [weight for _, weight in pieces]
    total_spec = pl.BlockSpec((tile, 2 * columns), lambda m, i: (m, 0))
    if total is not None:
        in_specs.append(total_spec)
        operands.append(total)
    return pl.pallas_call(
        functools.partial(project_kernel, blocks, total is not None, final),
        grid_spec=pltpu.PrefetchScalarGridSpec(
            num_scalar_prefetch=1, grid=(rows // tile,), in_specs=in_specs, out_specs=total_spec
        ),
        out_shape=jax.ShapeDtypeStruct((rows, 2 * columns), BF if final else F32),
        compiler_params=pltpu.CompilerParams(vmem_limit_bytes=VMEM_LIMIT),
        cost_estimate=pl.CostEstimate(
            flops=4 * rows * depth * columns * blocks,
            bytes_accessed=2 * blocks * depth * (rows + 2 * columns),
            transcendentals=0,
        ),
        name="project",
    )(idx, *operands)


def pack_kernel(holder, query, valid, out):
    rows = query.shape[0]
    shifted = pltpu.roll(query[...].astype(F32), rows - (M - 1), 0).astype(BF)
    for j in range(valid.shape[0]):
        u = j // 2
        out[holder[j], :M, :] = shifted[u * M : (u + 1) * M]
        out[holder[j], M:, :] = jnp.tile(valid[j : j + 1, :], (16, query.shape[1] // HD)).astype(BF)


def pack_queries(query, valid, holder, groups):
    return pl.pallas_call(
        pack_kernel,
        in_specs=[pl.BlockSpec(memory_space=pltpu.SMEM)] + vmem_specs(2),
        out_specs=pl.BlockSpec(memory_space=pltpu.VMEM),
        out_shape=jax.ShapeDtypeStruct((groups, M + 16, query.shape[1]), BF),
        compiler_params=pltpu.CompilerParams(vmem_limit_bytes=VMEM_LIMIT),
        name="pack_queries",
    )(holder, query, valid)


def attend_kernel(owner, query, keys_values, out):
    del owner
    heads = query.shape[2] // HD
    span = keys_values.shape[0]
    valid = query[0, M : M + 1, :span].astype(F32) > 0.5
    lane = lax.broadcasted_iota(jnp.int32, (M, HD), 1)
    stats = jnp.zeros((M, HD), F32)
    for h in range(heads):
        cols = slice(h * HD, (h + 1) * HD)
        value_cols = slice((heads + h) * HD, (heads + h + 1) * HD)
        scores = lax.dot_general(
            query[0, :M, cols],
            keys_values[:, cols],
            (((1,), (1,)), ((), ())),
            preferred_element_type=F32,
        ) * (1.0 / math.sqrt(HD))
        scores = jnp.where(valid, scores, -jnp.inf)
        highest = jnp.max(scores, axis=1, keepdims=True)
        raised = jnp.exp(scores - highest)
        norm = jnp.sum(raised, axis=1, keepdims=True)
        weights = (raised / norm).astype(BF)
        out[0, :, cols] = jnp.dot(
            weights, keys_values[:, value_cols], preferred_element_type=F32
        ).astype(BF)
        level = highest + jnp.log(norm)
        first = level.astype(BF).astype(F32)
        second = (level - first).astype(BF).astype(F32)
        third = level - first - second
        stats = jnp.where(lane == 3 * h, first, stats)
        stats = jnp.where(lane == 3 * h + 1, second, stats)
        stats = jnp.where(lane == 3 * h + 2, third, stats)
    out[0, :, heads * HD :] = stats.astype(BF)


def attend(owner, query_blocks, keys_values, span):
    groups, query_rows, columns = query_blocks.shape
    slots = keys_values.shape[0] // span
    return pl.pallas_call(
        attend_kernel,
        grid_spec=pltpu.PrefetchScalarGridSpec(
            num_scalar_prefetch=1,
            grid=(slots,),
            in_specs=[
                pl.BlockSpec((1, query_rows, columns), lambda i, owner: (owner[i], 0, 0)),
                pl.BlockSpec((span, 2 * columns), lambda i, owner: (i, 0)),
            ],
            out_specs=pl.BlockSpec((1, M, columns + HD), lambda i, owner: (owner[i], 0, 0)),
        ),
        out_shape=jax.ShapeDtypeStruct((groups, M, columns + HD), BF),
        compiler_params=pltpu.CompilerParams(vmem_limit_bytes=VMEM_LIMIT),
        name="attend",
    )(owner, query_blocks, keys_values)


def combine_kernel(holder, parts, out):
    rows, columns = out.shape
    heads = columns // HD
    flat = []
    for u in range(rows // M):
        first, second = parts[holder[2 * u]], parts[holder[2 * u + 1]]
        levels = [part[:, columns:].astype(F32) for part in (first, second)]
        pieces = []
        for h in range(heads):
            cols = slice(h * HD, (h + 1) * HD)
            one, two = [
                level[:, 3 * h : 3 * h + 1]
                + level[:, 3 * h + 1 : 3 * h + 2]
                + level[:, 3 * h + 2 : 3 * h + 3]
                for level in levels
            ]
            top = jnp.maximum(one, two)
            share_one, share_two = jnp.exp(one - top), jnp.exp(two - top)
            both = share_one + share_two
            pieces.append(
                first[:, cols].astype(F32) * (share_one / both)
                + second[:, cols].astype(F32) * (share_two / both)
            )
        flat.append(jnp.concatenate(pieces, axis=1))
    shifted = pltpu.roll(jnp.concatenate(flat, axis=0), M - 1, 0)
    row = lax.broadcasted_iota(jnp.int32, (rows, columns), 0)
    out[...] = jnp.where(row >= M - 1, shifted, 0.0).astype(BF)


def combine(holder, parts, rows):
    columns = parts.shape[2] - HD
    return pl.pallas_call(
        combine_kernel,
        in_specs=[pl.BlockSpec(memory_space=pltpu.SMEM)] + vmem_specs(1),
        out_specs=pl.BlockSpec(memory_space=pltpu.VMEM),
        out_shape=jax.ShapeDtypeStruct((rows, columns), BF),
        compiler_params=pltpu.CompilerParams(vmem_limit_bytes=VMEM_LIMIT),
        name="combine",
    )(holder, parts)


def mix_kernel(place, *refs):
    attended = refs[:4]
    mine, other, out = refs[4:]
    core = place[5]
    half = mine.shape[1]
    total = None
    for r in range(4):
        for swap, weight in ((0, mine), (1, other)):
            cols = pl.ds(pl.multiple_of(((core + swap) % 2) * half, half), half)
            term = jnp.dot(attended[r][:, cols], weight[place[r]], preferred_element_type=F32)
            total = term if total is None else total + term
    out[...] = total.astype(out.dtype)


def mix(place, attended, mine, other, kind):
    rows, columns = attended[0].shape
    width = mine.shape[2] // 2
    tile = width // 2
    weight_spec = pl.BlockSpec(
        (4, mine.shape[1], tile), lambda j, place: (0, 0, place[4] * 2 + j)
    )
    return pl.pallas_call(
        mix_kernel,
        grid_spec=pltpu.PrefetchScalarGridSpec(
            num_scalar_prefetch=1,
            grid=(2,),
            in_specs=[pl.BlockSpec((rows, columns), lambda j, place: (0, 0))] * 4
            + [weight_spec] * 2,
            out_specs=pl.BlockSpec((rows, tile), lambda j, place: (0, j)),
        ),
        out_shape=jax.ShapeDtypeStruct((rows, width), kind),
        compiler_params=pltpu.CompilerParams(vmem_limit_bytes=VMEM_LIMIT),
        cost_estimate=pl.CostEstimate(
            flops=8 * rows * columns * width, bytes_accessed=8 * columns * width, transcendentals=0
        ),
        name="mix",
    )(place, *attended, mine, other)


def gather_weights(own, position):
    z, y, c = position // 4, (position // 2) % 2, position % 2

    def at(dz, dy, dc):
        return ((z + dz) % 4) * 4 + ((y + dy) % 2) * 2 + (c + dc) % 2

    def send(block, pairs):
        return lax.ppermute(block, "dp", pairs)

    def with_twin(block, dz, dy):
        return [(at(dz, dy, 0), block), (at(dz, dy, 1), send(block, CORE_SWAP))]

    below, above, across = send(own, Z_UP), send(own, Z_DOWN), send(own, Y_SWAP)
    far = send(above, Z_DOWN)
    across_below = send(across, Z_UP)
    across_above = send(above, Y_SWAP)
    across_far = jnp.concatenate(
        [send(across_below[:1], Z_UP), send(across_above[1:], Z_DOWN)], axis=0
    )
    return [
        with_twin(own, 0, 0)
        + with_twin(below, -1, 0)
        + with_twin(above, 1, 0)
        + with_twin(across, 0, 1),
        with_twin(far, 2, 0) + with_twin(across_below, -1, 1) + with_twin(across_above, 1, 1),
        with_twin(across_far, 2, 1),
    ]


def body(encoded_neighbours, kv_weight, queries, out_weight, neighbour_ids, slot_map):
    groups = lax.axis_size("dp")
    position = lax.axis_index("dp")
    tensor_at = lax.axis_index("tensor")
    core, x, y_lo = position % 2, tensor_at // 2, tensor_at % 2
    slot_count, span, model_width = encoded_neighbours.shape
    encoded = encoded_neighbours.reshape(slot_count * span, model_width)

    held = lax.dynamic_slice_in_dim(slot_map, position * slot_count, slot_count)
    owner = held // slot_count
    wanted = position * slot_count + jnp.arange(slot_count, dtype=jnp.int32)
    holder = (
        jnp.sum(
            jnp.where(
                slot_map[None, :] == wanted[:, None],
                jnp.arange(slot_map.shape[0], dtype=jnp.int32)[None, :],
                0,
            ),
            axis=1,
        )
        // slot_count
    )
    valid = (neighbour_ids.reshape(slot_count, span) != 0).astype(F32)
    outgoing = pack_queries(queries, valid, holder, groups)
    query_blocks = lax.all_to_all(outgoing, "dp", 0, 0, tiled=True)

    half = out_weight.shape[0] // 2
    x_size = 4
    pair_width = out_weight.shape[1] // x_size
    own_half = lax.dynamic_slice_in_dim(out_weight, core * half, half, 0)
    own_half = own_half.reshape(half, x_size, pair_width).transpose(1, 0, 2)
    x_groups = [[i * 2 + yl for i in range(x_size)] for yl in range(2)]
    mix_mine = lax.all_to_all(own_half, "tensor", 0, 0, tiled=True, axis_index_groups=x_groups)
    mix_other = lax.ppermute(mix_mine, "dp", CORE_SWAP)

    stages = gather_weights(kv_weight, position)
    total = None
    for at, stage in enumerate(stages):
        total = project(encoded, stage, total, at == len(stages) - 1)

    parts = attend(owner, query_blocks, total, span)
    returned = lax.all_to_all(parts, "dp", 0, 0, tiled=True)
    attended = combine(holder, returned, queries.shape[0])

    near = [
        attended,
        lax.ppermute(attended, "tensor", tensor_pairs(1, 0)),
        lax.ppermute(attended, "tensor", tensor_pairs(-1, 0)),
        lax.ppermute(attended, "tensor", tensor_pairs(2, 0)),
    ]
    places = [x, (x + 3) % 4, (x + 1) % 4, (x + 2) % 4]
    theirs = mix(jnp.stack(places + [1 - y_lo, core]), near, mix_mine, mix_other, BF)
    arrived = lax.ppermute(theirs, "tensor", tensor_pairs(0, 1))
    ours = mix(jnp.stack(places + [y_lo, core]), near, mix_mine, mix_other, F32)
    return (ours + arrived.astype(F32)).astype(BF)


def solution(mesh):
    placed = (
        P("dp", None, None),
        P(None, "dp", "tensor"),
        P("dp", "tensor"),
        P("tensor", None),
        P("dp", None, None, None),
        P(),
    )
    return jax.shard_map(
        body, mesh=mesh, in_specs=placed, out_specs=P("dp", "tensor"), check_vma=False
    )
```

time: 568 us -> 215 us (0.38)
  blocking collectives: 325 us -> 25.4 us
  waiting for transfers between devices: 166 us -> 70.7 us
  Pallas kernels: 0 us -> 54.8 us
  matrix products: 46.8 us -> 0 us
  starting transfers between devices: 4.72 us -> 32 us
  local copies, waits for them, and re-layouts: 9.16 us -> 29.1 us
  between operations: 13.6 us -> 0.33 us
    psum x1 -> x0, blocking collectives: 325 us -> none  [body(): full_sum = lax.psum(partial_value, 'tensor')]
    all_gather x1 -> x0, waiting for transfers between devices: 114 us -> none  [body(): weight_piece = lax.all_gather(kv_weight, 'dp', axis=1, tiled=True)]
    ppermute x0 -> x21, waiting for transfers between devices: none -> 70.7 us  [the longest x16 52.1 us: send(): return lax.ppermute(block, 'dp', pairs)]
    pallas_call x0 -> x8, Pallas kernels: none -> 54.8 us  [the longest x3 32.1 us: project(): pl.pallas_call(functools.partial(project_kernel, blocks, total is not Non...]
    all_to_all x1 -> x2, waiting for transfers between devices: 51.2 us -> 0.01 us  [the longest x1 0.01 us: body(): lax.all_to_all(own_half, 'tensor', 0, 0, tiled=True, axis_index_groups=x_...]
    dot_general x7 -> x0, matrix products: 46.8 us -> none  [the longest x1 14.8 us: body(): jnp.dot(encoded, weight_piece[0], preferred_element_type=jnp.float32)]
    all_to_all x0 -> x1, blocking collectives: none -> 25.4 us  [body(): returned = lax.all_to_all(parts, 'dp', 0, 0, tiled=True)]
    ppermute x0 -> x21, starting transfers between devices: none -> 20.9 us  [the longest x16 14.6 us: send(): return lax.ppermute(block, 'dp', pairs)]
  transfers between devices with their start and end apart: 2 -> 23, of which waited for: 2 -> 11; matrix products, arithmetic and copies ran while one was open for 0% -> 2% of each run, Pallas kernels for 0% -> 24%
where the time goes in v1:
time: 215 us; the launch traced here: 214 us
  waiting for transfers between devices  70.7 us (33%)
  Pallas kernels  54.8 us (25%)
  starting transfers between devices  32 us (15%)
  local copies, waits for them, and re-layouts  29.1 us (14%)
  blocking collectives  25.4 us (12%)
    ppermute x16, waiting for transfers between devices, send(): return lax.ppermute(block, 'dp', pairs)  52.1 us
    pallas_call x3, Pallas kernels, project(): pl.pallas_call(functools.partial(project_kernel, blocks, total is not Non...  32.1 us
    all_to_all x1, blocking collectives, body(): returned = lax.all_to_all(parts, 'dp', 0, 0, tiled=True)  25.4 us
    unnamed x22, local copies, waits for them, and re-layouts  15 us
    ppermute x16, starting transfers between devices, send(): return lax.ppermute(block, 'dp', pairs)  14.6 us
    pallas_call x1, Pallas kernels, attend(): pl.pallas_call(attend_kernel, grid_spec=pltpu.PrefetchScalarGridSpec(num_...  11.7 us
    ppermute x1, waiting for transfers between devices, body(): arrived = lax.ppermute(theirs, 'tensor', tensor_pairs(0, 1))  8.23 us
    pallas_call x2, Pallas kernels, mix(): pl.pallas_call(mix_kernel, grid_spec=pltpu.PrefetchScalarGridSpec(num_sca...  7.91 us
  transfers between devices with their start and end apart: 23, of which 11 were waited for; matrix products, arithmetic and copies ran while one was open for 2% of the time, Pallas kernels for 24%

profile of v1, /device:TPU:0, one launch (start us, length us, event | category | flops | bytes accessed | tf_op | source)
XLA Modules:
  0.0 213.6 jit_solution(9989416842117738472)
XLA Ops:
  0.0 4.6 %constant_dynamic-slice_fusion = bf16[256,8192]{1,0:T(8,128)(2,1)} fusion(bf16[512,8192]{1,0:T(8,128)(2,1)} %param.9, s32[]{:T(128)S(6)} %select_n.190), kind=kLoop, calls=%fused_computation.15 | loop fusion | bytes 8388612 | tf_op jit(solution)/shard_map/dynamic_slice | solution.py:304
  4.6 6.3 %copy.11 = bf16[256,8192]{0,1:T(8,128)(2,1)} copy(bf16[256,8192]{1,0:T(8,128)(2,1)} %constant_dynamic-slice_fusion) | data formatting | bytes 8388608
  11.0 6.4 %copy.10 = bf16[256,4,2048]{2,0,1:T(8,128)(2,1)} copy(bf16[256,4,2048]{0,2,1:T(8,128)(2,1)} %bitcast.45) | data formatting | bytes 8388608 | tf_op jit(solution)/shard_map/reshape | solution.py:305
  17.3 5.0 %all-to-all-start.2 = ((bf16[4,256,2048]{2,1,0:T(8,128)(2,1)}), bf16[4,256,2048]{2,1,0:T(8,128)(2,1)}, u32[]{:S(2)}, u32[]{:S(2)}) async-start(bf16[4,256,2048]{2,1,0:T(8,128)(2,1)} %bitcast.44), calls=%async_computation.2 | async-start | bytes 8388608 | tf_op jit(solution)/shard_map/all_to_all | solution.py:307
  22.3 4.2 %collective-permute-start.3 = (bf16[2,512,512]{2,1,0:T(8,128)(2,1)S(1)}, bf16[2,512,512]{2,1,0:T(8,128)(2,1)}, u32[]{:S(2)}, u32[]{:S(2)}) collective-permute-start(bf16[2,512,512]{2,1,0:T(8,128)(2,1)S(1)} %copy-done), channel_id=1, source_target_pairs={{0,96},{8,104},{16,112},{24,120},{32,0},{40,8},{48,16},{56,24},{64... | collective-permute-start | bytes 3145736 | tf_op jit(solution)/shard_map/ppermute | solution.py:253
  26.5 3.2 %collective-permute-start = (bf16[2,512,512]{2,1,0:T(8,128)(2,1)S(1)}, bf16[2,512,512]{2,1,0:T(8,128)(2,1)}, u32[]{:S(2)}, u32[]{:S(2)}) collective-permute-start(bf16[2,512,512]{2,1,0:T(8,128)(2,1)S(1)} %copy-done), channel_id=1, source_target_pairs={{0,16},{8,24},{16,0},{24,8},{32,48},{40,56},{48,32},{56,40},{64,80... | collective-permute-start | bytes 3145736 | tf_op jit(solution)/shard_map/ppermute | solution.py:253
  29.7 19.2 %collective-permute-done.3.refs_12_ = bf16[2,512,512]{2,1,0:T(8,128)(2,1)} collective-permute-done((bf16[2,512,512]{2,1,0:T(8,128)(2,1)S(1)}, bf16[2,512,512]{2,1,0:T(8,128)(2,1)}, u32[]{:S(2)}, u32[]{:S(2)}) %collective-permute-start.3) | collective-permute-done | bytes 1048608 | tf_op jit(solution)/shard_map/ppermute | solution.py:253
  49.0 3.2 %collective-permute-start.4 = (bf16[2,512,512]{2,1,0:T(8,128)(2,1)}, bf16[2,512,512]{2,1,0:T(8,128)(2,1)S(1)}, u32[]{:S(2)}, u32[]{:S(2)}) collective-permute-start(bf16[2,512,512]{2,1,0:T(8,128)(2,1)} %collective-permute-done.3.refs_12_), channel_id=1, source_target_pairs={{0,16},{8,24},{16,0},{24,8},{32,48},{40,56},{48,32},{56,40},{64,80... | collective-permute-start | bytes 3145736 | tf_op jit(solution)/shard_map/ppermute | solution.py:253
  52.1 1.0 collective-permute-done.refs_14_
  53.1 2.1 %collective-permute-done.12.refs_10_ = bf16[2,512,512]{2,1,0:T(8,128)(2,1)S(1)} collective-permute-done((bf16[2,512,512]{2,1,0:T(8,128)(2,1)S(1)}, bf16[2,512,512]{2,1,0:T(8,128)(2,1)S(1)}, u32[]{:S(2)}, u32[]{:S(2)}) %collective-permute-start.12) | collective-permute-done | bytes 1048608 | tf_op jit(solution)/shard_map/ppermute | solution.py:253
  55.3 1.0 copy-done.2
  56.3 1.0 copy-done.4
  57.3 1.1 collective-permute-start.7
  58.4 16.7 %collective-permute-done.4.refs_10_ = bf16[2,512,512]{2,1,0:T(8,128)(2,1)S(1)} collective-permute-done((bf16[2,512,512]{2,1,0:T(8,128)(2,1)}, bf16[2,512,512]{2,1,0:T(8,128)(2,1)S(1)}, u32[]{:S(2)}, u32[]{:S(2)}) %collective-permute-start.4) | collective-permute-done | bytes 1048608 | tf_op jit(solution)/shard_map/ppermute | solution.py:253
  75.1 3.0 %collective-permute-done.1.refs_8_ = bf16[2,512,512]{2,1,0:T(8,128)(2,1)S(1)} collective-permute-done((bf16[2,512,512]{2,1,0:T(8,128)(2,1)}, bf16[2,512,512]{2,1,0:T(8,128)(2,1)S(1)}, u32[]{:S(2)}, u32[]{:S(2)}) %collective-permute-start.1) | collective-permute-done | bytes 1048608 | tf_op jit(solution)/shard_map/ppermute | solution.py:253
  78.4 0.8 slice.9
  79.2 0.8 slice.8
  80.0 1.7 collective-permute-start.5
  81.8 0.3 collective-permute-start.2
  82.1 0.9 copy-done.6
  83.0 1.7 pack_queries.1
  84.8 6.1 %all-to-all-start = ((bf16[16,80,512]{2,1,0:T(8,128)(2,1)}), bf16[16,80,512]{2,1,0:T(8,128)(2,1)S(1)}, u32[]{:S(2)}, u32[]{:S(2)}) async-start(bf16[16,80,512]{2,1,0:T(8,128)(2,1)} %pack_queries.1), calls=%async_computation | async-start | bytes 2621440 | tf_op jit(solution)/shard_map/all_to_all | solution.py:299
  91.6 7.9 %collective-permute-done.5 = bf16[1,512,512]{2,1,0:T(8,128)(2,1)} collective-permute-done((bf16[1,512,512]{2,1,0:T(8,128)(2,1)}, bf16[1,512,512]{2,1,0:T(8,128)(2,1)}, u32[]{:S(2)}, u32[]{:S(2)}) %collective-permute-start.5) | collective-permute-done | bytes 524320 | tf_op jit(solution)/shard_map/ppermute | solution.py:253
  99.5 2.1 collective-permute-done.2
  101.6 1.1 constant_dynamic-update-slice_fusion.1
  102.7 1.1 constant_dynamic-update-slice_fusion.refs_2_
  103.7 0.6 collective-permute-start.6
  104.3 1.2 copy-done.1
  105.6 1.2 copy-done.3
  106.8 1.2 copy-done.5
  108.0 14.7 %project.3.refs_12_ = f32[1024,1024]{1,0:T(8,128)} custom-call(s32[8]{0:T(128)S(1)} %stack.114.idx, bf16[1024,8192]{1,0:T(8,128)(2,1)} %bitcast.28, bf16[1024,8192]{1,0:T(8,128)(2,1)} %bitcast.29, bf16[1024,8192]{1,0:T(8,128)(2,1)} %bitcast.30, bf16[1024,8192]{1,0:T(8,128)(2,1)} %bitcast.31, bf16[1024,8192]{1,0:T(8,128)(2,1)} %bitcast.32, ...), custom_call_target="tpu_custom_call" | custom-call | flops 8589934592 | bytes 16777216 | tf_op jit(solution)/shard_map/project/pallas_call | solution.py:76
  122.7 0.9 copy-done.7
  123.7 11.8 %project.4.refs_4_ = f32[1024,1024]{1,0:T(8,128)} custom-call(s32[6]{0:T(128)S(1)} %stack.105.idx, bf16[1024,8192]{1,0:T(8,128)(2,1)} %bitcast.36, bf16[1024,8192]{1,0:T(8,128)(2,1)} %bitcast.37, bf16[1024,8192]{1,0:T(8,128)(2,1)} %bitcast.38, bf16[1024,8192]{1,0:T(8,128)(2,1)} %bitcast.39, bf16[1024,8192]{1,0:T(8,128)(2,1)} %bitcast.40, ...), custom_call_target="tpu_custom_call" | custom-call | flops 6442450944 | bytes 12582912 | tf_op jit(solution)/shard_map/project/pallas_call | solution.py:76
  135.4 5.7 %project.5.keys_values = bf16[1024,1024]{1,0:T(8,128)(2,1)S(1)} custom-call(s32[2]{0:T(128)S(1)} %pad_add_fusion.idx, bf16[1024,8192]{1,0:T(8,128)(2,1)} %bitcast.42, bf16[1024,8192]{1,0:T(8,128)(2,1)} %bitcast.43, bf16[2,512,512]{2,1,0:T(8,128)(2,1)S(1)} %constant_dynamic-update-slice_fusion.refs_2_, ...), custom_call_target="tpu_custom_call" | custom-call | flops 2147483648 | bytes 4194304 | tf_op jit(solution)/shard_map/project/pallas_call | solution.py:76
  141.1 11.7 %attend.1 = bf16[16,64,640]{2,1,0:T(8,128)(2,1)S(1)} custom-call(s32[8]{0:T(128)S(1)} %and_select_fusion.owner, bf16[16,80,512]{2,1,0:T(8,128)(2,1)S(1)} %all-to-all-done.query, bf16[1024,1024]{1,0:T(8,128)(2,1)S(1)} %project.5.keys_values), custom_call_target="tpu_custom_call" | custom-call | tf_op jit(solution)/shard_map/attend/pallas_call | solution.py:149
  152.8 25.4 %all_to_all.15.parts = bf16[16,64,640]{2,1,0:T(8,128)(2,1)S(1)} all-to-all(bf16[16,64,640]{2,1,0:T(8,128)(2,1)S(1)} %attend.1), channel_id=1, replica_groups=mesh['dp'=16,'tensor'=8] {'dp'}, dimensions={0} | all-to-all | bytes 2621440 | tf_op jit(solution)/shard_map/all_to_all | solution.py:316
  178.2 1.3 combine.1.refs_0_
  179.6 2.1 collective-permute-start.16
  181.7 1.3 collective-permute-start.17
  183.0 2.2 %collective-permute-start.18 = (bf16[256,512]{1,0:T(8,128)(2,1)S(1)}, bf16[256,512]{1,0:T(8,128)(2,1)S(1)}, u32[]{:S(2)}, u32[]{:S(2)}) collective-permute-start(bf16[256,512]{1,0:T(8,128)(2,1)S(1)} %combine.1.refs_0_), channel_id=1, source_target_pairs={{0,4},{1,5},{2,6},{3,7},{4,0},{5,1},{6,2},{7,3},{8,12},{9,13},{10,... | collective-permute-start | bytes 786440 | tf_op jit(solution)/shard_map/ppermute | solution.py:323
  185.3 3.9 %collective-permute-done.16.refs_1_ = bf16[256,512]{1,0:T(8,128)(2,1)S(1)} collective-permute-done((bf16[256,512]{1,0:T(8,128)(2,1)S(1)}, bf16[256,512]{1,0:T(8,128)(2,1)S(1)}, u32[]{:S(2)}, u32[]{:S(2)}) %collective-permute-start.16) | collective-permute-done | bytes 262176 | tf_op jit(solution)/shard_map/ppermute | solution.py:321
  189.3 1.7 collective-permute-done.17.refs_2_
  191.0 4.8 %collective-permute-done.18.refs_3_ = bf16[256,512]{1,0:T(8,128)(2,1)S(1)} collective-permute-done((bf16[256,512]{1,0:T(8,128)(2,1)S(1)}, bf16[256,512]{1,0:T(8,128)(2,1)S(1)}, u32[]{:S(2)}, u32[]{:S(2)}) %collective-permute-start.18) | collective-permute-done | bytes 262176 | tf_op jit(solution)/shard_map/ppermute | solution.py:323
  195.7 4.3 %mix.3 = bf16[256,1024]{1,0:T(8,128)(2,1)} custom-call(s32[6]{0:T(128)S(1)} %stack.116.place, bf16[256,512]{1,0:T(8,128)(2,1)S(1)} %combine.1.refs_0_, bf16[256,512]{1,0:T(8,128)(2,1)S(1)} %collective-permute-done.16.refs_1_, bf16[256,512]{1,0:T(8,128)(2,1)S(1)} %collective-permute-done.17.refs_2_, bf16[256,512]{1,0:T(8,128)(2,1)S(1)} %collective-permute-done.18.refs_3_, ...), custom_call_target="tpu_custom_call" | custom-call | flops 1073741824 | bytes 4194304 | tf_op jit(solution)/shard_map/mix/pallas_call | solution.py:228
  200.0 0.7 collective-permute-start.20
  200.8 3.6 %mix.2 = f32[256,1024]{1,0:T(8,128)S(1)} custom-call(s32[6]{0:T(128)S(1)} %stack.95.place, bf16[256,512]{1,0:T(8,128)(2,1)S(1)} %combine.1.refs_0_, bf16[256,512]{1,0:T(8,128)(2,1)S(1)} %collective-permute-done.16.refs_1_, bf16[256,512]{1,0:T(8,128)(2,1)S(1)} %collective-permute-done.17.refs_2_, bf16[256,512]{1,0:T(8,128)(2,1)S(1)} %collective-permute-done.18.refs_3_, ...), custom_call_target="tpu_custom_call" | custom-call | flops 1073741824 | bytes 4194304 | tf_op jit(solution)/shard_map/mix/pallas_call | solution.py:228
  204.4 8.2 %collective-permute-done.20 = bf16[256,1024]{1,0:T(8,128)(2,1)S(1)} collective-permute-done((bf16[256,1024]{1,0:T(8,128)(2,1)}, bf16[256,1024]{1,0:T(8,128)(2,1)S(1)}, u32[]{:S(2)}, u32[]{:S(2)}) %collective-permute-start.20) | collective-permute-done | bytes 524320 | tf_op jit(solution)/shard_map/ppermute | solution.py:327
  212.7 0.9 add_convert_fusion
  (45 shorter events, 1.0 us)
Async XLA Ops:
  17.3 5.0 %copy-start = (bf16[2,512,512]{2,1,0:T(8,128)(2,1)S(1)}, bf16[2,512,512]{2,1,0:T(8,128)(2,1)}, u32[]{:S(2)}) copy-start(bf16[2,512,512]{2,1,0:T(8,128)(2,1)} %refs_8_.1) | copy-start | bytes 3145732
  17.3 60.8 %copy-start.9 = (s32[128]{0:T(128)S(1)}, s32[128]{0:T(128)}, u32[]{:S(2)}) copy-start(s32[128]{0:T(128)} %param.11) | copy-start | bytes 1540
  17.3 64.7 %copy-start.8 = (s32[1,4,2,128]{3,2,1,0:T(2,128)S(1)}, s32[1,4,2,128]{3,2,1,0:T(2,128)}, u32[]{:S(2)}) copy-start(s32[1,4,2,128]{3,2,1,0:T(2,128)} %param.10) | copy-start | bytes 12292
  17.3 60.8 %all-to-all-start.2 = ((bf16[4,256,2048]{2,1,0:T(8,128)(2,1)}), bf16[4,256,2048]{2,1,0:T(8,128)(2,1)}, u32[]{:S(2)}, u32[]{:S(2)}) async-start(bf16[4,256,2048]{2,1,0:T(8,128)(2,1)} %bitcast.44), calls=%async_computation.2 | async-start | bytes 8388608 | tf_op jit(solution)/shard_map/all_to_all | solution.py:307
  22.3 26.6 %collective-permute-start.3 = (bf16[2,512,512]{2,1,0:T(8,128)(2,1)S(1)}, bf16[2,512,512]{2,1,0:T(8,128)(2,1)}, u32[]{:S(2)}, u32[]{:S(2)}) collective-permute-start(bf16[2,512,512]{2,1,0:T(8,128)(2,1)S(1)} %copy-done), channel_id=1, source_target_pairs={{0,96},{8,104},{16,112},{24,120},{32,0},{40,8},{48,16},{56,24},{64... | collective-permute-start | bytes 3145736 | tf_op jit(solution)/shard_map/ppermute | solution.py:253
  26.5 26.6 %collective-permute-start = (bf16[2,512,512]{2,1,0:T(8,128)(2,1)S(1)}, bf16[2,512,512]{2,1,0:T(8,128)(2,1)}, u32[]{:S(2)}, u32[]{:S(2)}) collective-permute-start(bf16[2,512,512]{2,1,0:T(8,128)(2,1)S(1)} %copy-done), channel_id=1, source_target_pairs={{0,16},{8,24},{16,0},{24,8},{32,48},{40,56},{48,32},{56,40},{64,80... | collective-permute-start | bytes 3145736 | tf_op jit(solution)/shard_map/ppermute | solution.py:253
  29.7 25.5 %collective-permute-start.12 = (bf16[2,512,512]{2,1,0:T(8,128)(2,1)S(1)}, bf16[2,512,512]{2,1,0:T(8,128)(2,1)S(1)}, u32[]{:S(2)}, u32[]{:S(2)}) collective-permute-start(bf16[2,512,512]{2,1,0:T(8,128)(2,1)S(1)} %copy-done), channel_id=1, source_target_pairs={{0,32},{8,40},{16,48},{24,56},{32,64},{40,72},{48,80},{56,88},{64,... | collective-permute-start | bytes 3145736 | tf_op jit(solution)/shard_map/ppermute | solution.py:253
  29.7 25.6 %collective-permute-start.11 = (bf16[2,512,512]{2,1,0:T(8,128)(2,1)S(1)}, bf16[2,512,512]{2,1,0:T(8,128)(2,1)S(1)}, u32[]{:S(2)}, u32[]{:S(2)}) collective-permute-start(bf16[2,512,512]{2,1,0:T(8,128)(2,1)S(1)} %copy-done), channel_id=1, source_target_pairs={{0,8},{8,0},{16,24},{24,16},{32,40},{40,32},{48,56},{56,48},{64,72... | collective-permute-start | bytes 3145736 | tf_op jit(solution)/shard_map/ppermute | solution.py:253
  49.0 26.2 %collective-permute-start.4 = (bf16[2,512,512]{2,1,0:T(8,128)(2,1)}, bf16[2,512,512]{2,1,0:T(8,128)(2,1)S(1)}, u32[]{:S(2)}, u32[]{:S(2)}) collective-permute-start(bf16[2,512,512]{2,1,0:T(8,128)(2,1)} %collective-permute-done.3.refs_12_), channel_id=1, source_target_pairs={{0,16},{8,24},{16,0},{24,8},{32,48},{40,56},{48,32},{56,40},{64,80... | collective-permute-start | bytes 3145736 | tf_op jit(solution)/shard_map/ppermute | solution.py:253
  53.1 25.0 %collective-permute-start.1 = (bf16[2,512,512]{2,1,0:T(8,128)(2,1)}, bf16[2,512,512]{2,1,0:T(8,128)(2,1)S(1)}, u32[]{:S(2)}, u32[]{:S(2)}) collective-permute-start(bf16[2,512,512]{2,1,0:T(8,128)(2,1)} %collective-permute-done.refs_14_), channel_id=1, source_target_pairs={{0,32},{8,40},{16,48},{24,56},{32,64},{40,72},{48,80},{56,88},{64,... | collective-permute-start | bytes 3145736 | tf_op jit(solution)/shard_map/ppermute | solution.py:253
  53.1 26.9 %collective-permute-start.14 = (bf16[2,512,512]{2,1,0:T(8,128)(2,1)}, bf16[2,512,512]{2,1,0:T(8,128)(2,1)}, u32[]{:S(2)}, u32[]{:S(2)}) collective-permute-start(bf16[2,512,512]{2,1,0:T(8,128)(2,1)} %collective-permute-done.3.refs_12_), channel_id=1, source_target_pairs={{0,8},{8,0},{16,24},{24,16},{32,40},{40,32},{48,56},{56,48},{64,72... | collective-permute-start | bytes 3145736 | tf_op jit(solution)/shard_map/ppermute | solution.py:253
  55.3 1.0 copy-start.2
  55.3 26.5 %collective-permute-start.15 = (bf16[2,512,512]{2,1,0:T(8,128)(2,1)}, bf16[2,512,512]{2,1,0:T(8,128)(2,1)}, u32[]{:S(2)}, u32[]{:S(2)}) collective-permute-start(bf16[2,512,512]{2,1,0:T(8,128)(2,1)} %collective-permute-done.refs_14_), channel_id=1, source_target_pairs={{0,8},{8,0},{16,24},{24,16},{32,40},{40,32},{48,56},{56,48},{64,72... | collective-permute-start | bytes 3145736 | tf_op jit(solution)/shard_map/ppermute | solution.py:253
  56.3 1.0 copy-start.4
  57.3 34.0 %collective-permute-start.7 = (bf16[2,512,512]{2,1,0:T(8,128)(2,1)}, bf16[2,512,512]{2,1,0:T(8,128)(2,1)}, u32[]{:S(2)}, u32[]{:S(2)}) collective-permute-start(bf16[2,512,512]{2,1,0:T(8,128)(2,1)} %collective-permute-done.3.refs_12_), channel_id=1, source_target_pairs={{0,96},{8,104},{16,112},{24,120},{32,0},{40,8},{48,16},{56,24},{64... | collective-permute-start | bytes 3145736 | tf_op jit(solution)/shard_map/ppermute | solution.py:253
  75.1 28.6 %collective-permute-start.13 = (bf16[2,512,512]{2,1,0:T(8,128)(2,1)}, bf16[2,512,512]{2,1,0:T(8,128)(2,1)}, u32[]{:S(2)}, u32[]{:S(2)}) collective-permute-start(bf16[2,512,512]{2,1,0:T(8,128)(2,1)} %copy-done.2), channel_id=1, source_target_pairs={{0,8},{8,0},{16,24},{24,16},{32,40},{40,32},{48,56},{56,48},{64,72... | collective-permute-start | bytes 3145736 | tf_op jit(solution)/shard_map/ppermute | solution.py:253
  78.2 117.6 %collective-permute-start.19 = (bf16[4,256,2048]{2,1,0:T(8,128)(2,1)}, bf16[4,256,2048]{2,1,0:T(8,128)(2,1)}, u32[]{:S(2)}, u32[]{:S(2)}) collective-permute-start(bf16[4,256,2048]{2,1,0:T(8,128)(2,1)} %all-to-all-done.2.refs_4_), channel_id=1, source_target_pairs={{0,8},{8,0},{16,24},{24,16},{32,40},{40,32},{48,56},{56,48},{64,72... | collective-permute-start | bytes 12582920 | tf_op jit(solution)/shard_map/ppermute | solution.py:308
  80.0 19.4 %collective-permute-start.5 = (bf16[1,512,512]{2,1,0:T(8,128)(2,1)}, bf16[1,512,512]{2,1,0:T(8,128)(2,1)}, u32[]{:S(2)}, u32[]{:S(2)}) collective-permute-start(bf16[1,512,512]{2,1,0:T(8,128)(2,1)} %slice.9), channel_id=1, source_target_pairs={{0,96},{8,104},{16,112},{24,120},{32,0},{40,8},{48,16},{56,24},{64... | collective-permute-start | bytes 1572872 | tf_op jit(solution)/shard_map/ppermute | solution.py:253
  81.8 19.8 %collective-permute-start.2 = (bf16[1,512,512]{2,1,0:T(8,128)(2,1)}, bf16[1,512,512]{2,1,0:T(8,128)(2,1)}, u32[]{:S(2)}, u32[]{:S(2)}) collective-permute-start(bf16[1,512,512]{2,1,0:T(8,128)(2,1)} %slice.8), channel_id=1, source_target_pairs={{0,32},{8,40},{16,48},{24,56},{32,64},{40,72},{48,80},{56,88},{64,... | collective-permute-start | bytes 1572872 | tf_op jit(solution)/shard_map/ppermute | solution.py:253
  82.1 1.0 copy-start.6
  84.8 56.4 %all-to-all-start = ((bf16[16,80,512]{2,1,0:T(8,128)(2,1)}), bf16[16,80,512]{2,1,0:T(8,128)(2,1)S(1)}, u32[]{:S(2)}, u32[]{:S(2)}) async-start(bf16[16,80,512]{2,1,0:T(8,128)(2,1)} %pack_queries.1), calls=%async_computation | async-start | bytes 2621440 | tf_op jit(solution)/shard_map/all_to_all | solution.py:299
  91.3 31.4 %collective-permute-start.10 = (bf16[2,512,512]{2,1,0:T(8,128)(2,1)S(1)}, bf16[2,512,512]{2,1,0:T(8,128)(2,1)S(1)}, u32[]{:S(2)}, u32[]{:S(2)}) collective-permute-start(bf16[2,512,512]{2,1,0:T(8,128)(2,1)S(1)} %collective-permute-done.4.refs_10_), channel_id=1, source_target_pairs={{0,8},{8,0},{16,24},{24,16},{32,40},{40,32},{48,56},{56,48},{64,72... | collective-permute-start | bytes 3145736 | tf_op jit(solution)/shard_map/ppermute | solution.py:253
  99.4 23.3 %collective-permute-start.9 = (bf16[2,512,512]{2,1,0:T(8,128)(2,1)S(1)}, bf16[2,512,512]{2,1,0:T(8,128)(2,1)S(1)}, u32[]{:S(2)}, u32[]{:S(2)}) collective-permute-start(bf16[2,512,512]{2,1,0:T(8,128)(2,1)S(1)} %collective-permute-done.1.refs_8_), channel_id=1, source_target_pairs={{0,8},{8,0},{16,24},{24,16},{32,40},{40,32},{48,56},{56,48},{64,72... | collective-permute-start | bytes 3145736 | tf_op jit(solution)/shard_map/ppermute | solution.py:253
  101.6 21.1 %collective-permute-start.8 = (bf16[2,512,512]{2,1,0:T(8,128)(2,1)}, bf16[2,512,512]{2,1,0:T(8,128)(2,1)S(1)}, u32[]{:S(2)}, u32[]{:S(2)}) collective-permute-start(bf16[2,512,512]{2,1,0:T(8,128)(2,1)} %collective-permute-done.7.refs_6_), channel_id=1, source_target_pairs={{0,8},{8,0},{16,24},{24,16},{32,40},{40,32},{48,56},{56,48},{64,72... | collective-permute-start | bytes 3145736 | tf_op jit(solution)/shard_map/ppermute | solution.py:253
  103.7 31.7 %collective-permute-start.6 = (bf16[2,512,512]{2,1,0:T(8,128)(2,1)S(1)}, bf16[2,512,512]{2,1,0:T(8,128)(2,1)S(1)}, u32[]{:S(2)}, u32[]{:S(2)}) collective-permute-start(bf16[2,512,512]{2,1,0:T(8,128)(2,1)S(1)} %constant_dynamic-update-slice_fusion.refs_2_), channel_id=1, source_target_pairs={{0,8},{8,0},{16,24},{24,16},{32,40},{40,32},{48,56},{56,48},{64,72... | collective-permute-start | bytes 3145736 | tf_op jit(solution)/shard_map/ppermute | solution.py:253
  104.3 1.2 copy-start.1
  105.6 1.2 copy-start.3
  106.8 1.2 copy-start.5
  122.7 1.0 copy-start.7
  179.6 9.7 %collective-permute-start.16 = (bf16[256,512]{1,0:T(8,128)(2,1)S(1)}, bf16[256,512]{1,0:T(8,128)(2,1)S(1)}, u32[]{:S(2)}, u32[]{:S(2)}) collective-permute-start(bf16[256,512]{1,0:T(8,128)(2,1)S(1)} %combine.1.refs_0_), channel_id=1, source_target_pairs={{0,2},{1,3},{2,4},{3,5},{4,6},{5,7},{6,0},{7,1},{8,10},{9,11},{10,... | collective-permute-start | bytes 786440 | tf_op jit(solution)/shard_map/ppermute | solution.py:321
  181.7 9.2 %collective-permute-start.17 = (bf16[256,512]{1,0:T(8,128)(2,1)S(1)}, bf16[256,512]{1,0:T(8,128)(2,1)S(1)}, u32[]{:S(2)}, u32[]{:S(2)}) collective-permute-start(bf16[256,512]{1,0:T(8,128)(2,1)S(1)} %combine.1.refs_0_), channel_id=1, source_target_pairs={{0,6},{1,7},{2,0},{3,1},{4,2},{5,3},{6,4},{7,5},{8,14},{9,15},{10,... | collective-permute-start | bytes 786440 | tf_op jit(solution)/shard_map/ppermute | solution.py:322
  183.0 12.7 %collective-permute-start.18 = (bf16[256,512]{1,0:T(8,128)(2,1)S(1)}, bf16[256,512]{1,0:T(8,128)(2,1)S(1)}, u32[]{:S(2)}, u32[]{:S(2)}) collective-permute-start(bf16[256,512]{1,0:T(8,128)(2,1)S(1)} %combine.1.refs_0_), channel_id=1, source_target_pairs={{0,4},{1,5},{2,6},{3,7},{4,0},{5,1},{6,2},{7,3},{8,12},{9,13},{10,... | collective-permute-start | bytes 786440 | tf_op jit(solution)/shard_map/ppermute | solution.py:323
  200.0 12.6 %collective-permute-start.20 = (bf16[256,1024]{1,0:T(8,128)(2,1)}, bf16[256,1024]{1,0:T(8,128)(2,1)S(1)}, u32[]{:S(2)}, u32[]{:S(2)}) collective-permute-start(bf16[256,1024]{1,0:T(8,128)(2,1)} %mix.3), channel_id=1, source_target_pairs={{0,1},{1,0},{2,3},{3,2},{4,5},{5,4},{6,7},{7,6},{8,9},{9,8},{10,11... | collective-permute-start | bytes 1572872 | tf_op jit(solution)/shard_map/ppermute | solution.py:327

commit v2 on v1

--- a/solution.py
+++ b/solution.py
@@ -12,6 +12,7 @@
 M = 64
 BF = jnp.bfloat16
 F32 = jnp.float32
+ATTEND_SLOTS = 2
 VMEM_LIMIT = 48 * 1024 * 1024
 
 
@@ -39,25 +40,33 @@
     return [pl.BlockSpec(memory_space=pltpu.VMEM)] * count
 
 
-def project_kernel(blocks, has_total, final, idx, *refs):
+def project_kernel(sizes, has_total, idx, *refs):
     del idx
+    blocks = len(sizes)
     rows = refs[:blocks]
-    weights = refs[blocks : 2 * blocks]
-    rest = refs[2 * blocks :]
-    out = rest[-1]
-    columns = weights[0].shape[2]
+    weights = []
+    at = blocks
+    for size in sizes:
+        if size == 1:
+            weights.append((refs[at].at[0], refs[at].at[1]))
+        else:
+            weights.append((refs[at].at[0], refs[at + 1].at[0]))
+        at += size
+    out = refs[-1]
+    columns = out.shape[1] // 2
     for side in range(2):
         cols = slice(side * columns, (side + 1) * columns)
-        total = rest[0][:, cols] if has_total else None
+        total = refs[at][:, cols] if has_total else None
         for row, weight in zip(rows, weights):
-            term = jnp.dot(row[...], weight[side], preferred_element_type=F32)
+            term = jnp.dot(row[...], weight[side][...], preferred_element_type=F32)
             total = term if total is None else total + term
         out[:, cols] = total.astype(out.dtype)
 
 
 def project(encoded, pieces, total, final):
     rows = encoded.shape[0]
-    depth, columns = pieces[0][1].shape[1:]
+    arrays = [array for _, weight in pieces for array in weight]
+    depth, columns = arrays[0].shape[1:]
     tile = 256
     blocks = len(pieces)
     idx = jnp.stack([place for place, _ in pieces]).astype(jnp.int32)
@@ -66,15 +75,16 @@
         return pl.BlockSpec((tile, depth), lambda m, i, j=j: (m, i[j]))
 
     in_specs = [row_spec(j) for j in range(blocks)] + [
-        pl.BlockSpec((2, depth, columns), lambda m, i: (0, 0, 0), pipeline_mode=pl.Buffered(1))
-    ] * blocks
-    operands = [encoded] * blocks + [weight for _, weight in pieces]
+        pl.BlockSpec(array.shape, lambda m, i: (0, 0, 0), pipeline_mode=pl.Buffered(1))
+        for array in arrays
+    ]
+    operands = [encoded] * blocks + arrays
     total_spec = pl.BlockSpec((tile, 2 * columns), lambda m, i: (m, 0))
     if total is not None:
         in_specs.append(total_spec)
         operands.append(total)
     return pl.pallas_call(
-        functools.partial(project_kernel, blocks, total is not None, final),
+        functools.partial(project_kernel, [len(w) for _, w in pieces], total is not None),
         grid_spec=pltpu.PrefetchScalarGridSpec(
             num_scalar_prefetch=1, grid=(rows // tile,), in_specs=in_specs, out_specs=total_spec
         ),
@@ -87,6 +97,30 @@
         ),
         name="project",
     )(idx, *operands)
+
+
+def split_kernel(core, rows, out):
+    del core
+    out[0] = rows[...]
+
+
+def split_rows(core, weight, parts):
+    half, width = weight.shape[0] // 2, weight.shape[1] // parts
+    return pl.pallas_call(
+        split_kernel,
+        grid_spec=pltpu.PrefetchScalarGridSpec(
+            num_scalar_prefetch=1,
+            grid=(parts,),
+            in_specs=[pl.BlockSpec((half, width), lambda j, core: (core[0], j))],
+            out_specs=pl.BlockSpec((1, half, width), lambda j, core: (j, 0, 0)),
+        ),
+        out_shape=jax.ShapeDtypeStruct((parts, half, width), weight.dtype),
+        compiler_params=pltpu.CompilerParams(vmem_limit_bytes=VMEM_LIMIT),
+        cost_estimate=pl.CostEstimate(
+            flops=0, bytes_accessed=8 * half * width * parts, transcendentals=0
+        ),
+        name="split_rows",
+    )(core, weight)
 
 
 def pack_kernel(holder, query, valid, out):
@@ -110,52 +144,60 @@
 
 
 def attend_kernel(owner, query, keys_values, out):
-    del owner
     heads = query.shape[2] // HD
-    span = keys_values.shape[0]
-    valid = query[0, M : M + 1, :span].astype(F32) > 0.5
+    span = keys_values.shape[0] // ATTEND_SLOTS
     lane = lax.broadcasted_iota(jnp.int32, (M, HD), 1)
-    stats = jnp.zeros((M, HD), F32)
-    for h in range(heads):
+    pairs = [(i, h) for i in range(ATTEND_SLOTS) for h in range(heads)]
+    places = [owner[pl.program_id(0) * ATTEND_SLOTS + i] for i in range(ATTEND_SLOTS)]
+    scores = {}
+    for i, h in pairs:
         cols = slice(h * HD, (h + 1) * HD)
-        value_cols = slice((heads + h) * HD, (heads + h + 1) * HD)
-        scores = lax.dot_general(
-            query[0, :M, cols],
-            keys_values[:, cols],
+        scores[i, h] = lax.dot_general(
+            query[places[i], :M, cols],
+            keys_values[i * span : (i + 1) * span, cols],
             (((1,), (1,)), ((), ())),
             preferred_element_type=F32,
-        ) * (1.0 / math.sqrt(HD))
-        scores = jnp.where(valid, scores, -jnp.inf)
-        highest = jnp.max(scores, axis=1, keepdims=True)
-        raised = jnp.exp(scores - highest)
+        )
+    valid = [query[place, M : M + 1, :span].astype(F32) > 0.5 for place in places]
+    weights, levels = {}, {}
+    for i, h in pairs:
+        scaled = jnp.where(valid[i], scores[i, h] * (1.0 / math.sqrt(HD)), -jnp.inf)
+        highest = jnp.max(scaled, axis=1, keepdims=True)
+        raised = jnp.exp(scaled - highest)
         norm = jnp.sum(raised, axis=1, keepdims=True)
-        weights = (raised / norm).astype(BF)
-        out[0, :, cols] = jnp.dot(
-            weights, keys_values[:, value_cols], preferred_element_type=F32
+        weights[i, h] = (raised / norm).astype(BF)
+        levels[i, h] = highest + jnp.log(norm)
+    for i, h in pairs:
+        out[places[i], :, h * HD : (h + 1) * HD] = jnp.dot(
+            weights[i, h],
+            keys_values[i * span : (i + 1) * span, (heads + h) * HD : (heads + h + 1) * HD],
+            preferred_element_type=F32,
         ).astype(BF)
-        level = highest + jnp.log(norm)
-        first = level.astype(BF).astype(F32)
-        second = (level - first).astype(BF).astype(F32)
-        third = level - first - second
-        stats = jnp.where(lane == 3 * h, first, stats)
-        stats = jnp.where(lane == 3 * h + 1, second, stats)
-        stats = jnp.where(lane == 3 * h + 2, third, stats)
-    out[0, :, heads * HD :] = stats.astype(BF)
+    for i in range(ATTEND_SLOTS):
+        stats = jnp.zeros((M, HD), F32)
+        for h in range(heads):
+            first = levels[i, h].astype(BF).astype(F32)
+            second = (levels[i, h] - first).astype(BF).astype(F32)
+            third = levels[i, h] - first - second
+            stats = jnp.where(lane == 3 * h, first, stats)
+            stats = jnp.where(lane == 3 * h + 1, second, stats)
+            stats = jnp.where(lane == 3 * h + 2, third, stats)
+        out[places[i], :, heads * HD :] = stats.astype(BF)
 
 
 def attend(owner, query_blocks, keys_values, span):
     groups, query_rows, columns = query_blocks.shape
-    slots = keys_values.shape[0] // span
+    steps = keys_values.shape[0] // (span * ATTEND_SLOTS)
     return pl.pallas_call(
         attend_kernel,
         grid_spec=pltpu.PrefetchScalarGridSpec(
             num_scalar_prefetch=1,
-            grid=(slots,),
+            grid=(steps,),
             in_specs=[
-                pl.BlockSpec((1, query_rows, columns), lambda i, owner: (owner[i], 0, 0)),
-                pl.BlockSpec((span, 2 * columns), lambda i, owner: (i, 0)),
+                pl.BlockSpec((groups, query_rows, columns), lambda i, owner: (0, 0, 0)),
+                pl.BlockSpec((span * ATTEND_SLOTS, 2 * columns), lambda i, owner: (i, 0)),
             ],
-            out_specs=pl.BlockSpec((1, M, columns + HD), lambda i, owner: (owner[i], 0, 0)),
+            out_specs=pl.BlockSpec((groups, M, columns + HD), lambda i, owner: (0, 0, 0)),
         ),
         out_shape=jax.ShapeDtypeStruct((groups, M, columns + HD), BF),
         compiler_params=pltpu.CompilerParams(vmem_limit_bytes=VMEM_LIMIT),
@@ -243,33 +285,46 @@
     )(place, *attended, mine, other)
 
 
-def gather_weights(own, position):
+def project_gathered(encoded, own, own_twin, position, query_blocks, core):
     z, y, c = position // 4, (position // 2) % 2, position % 2
-
-    def at(dz, dy, dc):
-        return ((z + dz) % 4) * 4 + ((y + dy) % 2) * 2 + (c + dc) % 2
 
     def send(block, pairs):
         return lax.ppermute(block, "dp", pairs)
 
-    def with_twin(block, dz, dy):
-        return [(at(dz, dy, 0), block), (at(dz, dy, 1), send(block, CORE_SWAP))]
+    def with_twin(dz, dy, *arrays):
+        def at(dc):
+            return ((z + dz) % 4) * 4 + ((y + dy) % 2) * 2 + (c + dc) % 2
+
+        return [(at(0), arrays), (at(1), tuple(send(array, CORE_SWAP) for array in arrays))]
 
     below, above, across = send(own, Z_UP), send(own, Z_DOWN), send(own, Y_SWAP)
-    far = send(above, Z_DOWN)
-    across_below = send(across, Z_UP)
-    across_above = send(above, Y_SWAP)
-    across_far = jnp.concatenate(
-        [send(across_below[:1], Z_UP), send(across_above[1:], Z_DOWN)], axis=0
-    )
-    return [
-        with_twin(own, 0, 0)
-        + with_twin(below, -1, 0)
-        + with_twin(above, 1, 0)
-        + with_twin(across, 0, 1),
-        with_twin(far, 2, 0) + with_twin(across_below, -1, 1) + with_twin(across_above, 1, 1),
-        with_twin(across_far, 2, 1),
-    ]
+    own_pieces = [(position, (own,)), (position + 1 - 2 * c, (own_twin,))]
+    below, above, across, query_blocks, core = lax.optimization_barrier(
+        (below, above, across, query_blocks, core)
+    )
+    far, across_below, across_above = send(above, Z_DOWN), send(across, Z_UP), send(above, Y_SWAP)
+    total = project(
+        encoded,
+        own_pieces
+        + with_twin(-1, 0, below)
+        + with_twin(1, 0, above)
+        + with_twin(0, 1, across),
+        None,
+        False,
+    )
+    far, across_below, across_above, total = lax.optimization_barrier(
+        (far, across_below, across_above, total)
+    )
+    far_keys, far_values = send(across_below[:1], Z_UP), send(across_above[1:], Z_DOWN)
+    total = project(
+        encoded,
+        with_twin(2, 0, far) + with_twin(-1, 1, across_below) + with_twin(1, 1, across_above),
+        total,
+        False,
+    )
+    far_keys, far_values, total = lax.optimization_barrier((far_keys, far_values, total))
+    last = project(encoded, with_twin(2, 1, far_keys, far_values), total, True)
+    return last, query_blocks, core
 
 
 def body(encoded_neighbours, kv_weight, queries, out_weight, neighbour_ids, slot_map):
@@ -295,24 +350,23 @@
         // slot_count
     )
     valid = (neighbour_ids.reshape(slot_count, span) != 0).astype(F32)
+    own_twin = lax.ppermute(kv_weight, "dp", CORE_SWAP)
+    own_twin, holder = lax.optimization_barrier((own_twin, holder))
     outgoing = pack_queries(queries, valid, holder, groups)
     query_blocks = lax.all_to_all(outgoing, "dp", 0, 0, tiled=True)
 
-    half = out_weight.shape[0] // 2
+    keys_values, query_blocks, later_core = project_gathered(
+        encoded, kv_weight, own_twin, position, query_blocks, jnp.full((1,), core, jnp.int32)
+    )
+
     x_size = 4
-    pair_width = out_weight.shape[1] // x_size
-    own_half = lax.dynamic_slice_in_dim(out_weight, core * half, half, 0)
-    own_half = own_half.reshape(half, x_size, pair_width).transpose(1, 0, 2)
+    own_half = split_rows(later_core, out_weight, x_size)
     x_groups = [[i * 2 + yl for i in range(x_size)] for yl in range(2)]
     mix_mine = lax.all_to_all(own_half, "tensor", 0, 0, tiled=True, axis_index_groups=x_groups)
+    mix_mine, keys_values = lax.optimization_barrier((mix_mine, keys_values))
     mix_other = lax.ppermute(mix_mine, "dp", CORE_SWAP)
 
-    stages = gather_weights(kv_weight, position)
-    total = None
-    for at, stage in enumerate(stages):
-        total = project(encoded, stage, total, at == len(stages) - 1)
-
-    parts = attend(owner, query_blocks, total, span)
+    parts = attend(owner, query_blocks, keys_values, span)
     returned = lax.all_to_all(parts, "dp", 0, 0, tiled=True)
     attended = combine(holder, returned, queries.shape[0])
 

time: 215 us -> 184 us (0.86)
  local copies, waits for them, and re-layouts: 29.1 us -> 10.7 us
  waiting for transfers between devices: 70.7 us -> 59 us
  Pallas kernels: 54.8 us -> 49.7 us
  starting transfers between devices: 32 us -> 35.2 us
    ppermute x16, waiting for transfers between devices: 52.1 us -> 37.9 us  [send(): return lax.ppermute(block, 'dp', pairs)]
    pallas_call x1, Pallas kernels: 11.7 us -> 2.99 us  [attend(): pl.pallas_call(attend_kernel, grid_spec=pltpu.PrefetchScalarGridSpec(num_...]
    reshape x1 -> x0, local copies, waits for them, and re-layouts: 6.35 us -> none  [body(): own_half = own_half.reshape(half, x_size, pair_width).transpose(1, 0, 2)]
    unnamed x22 -> x24, local copies, waits for them, and re-layouts: 15 us -> 10.3 us
    dynamic_slice x1 -> x0, local copies, waits for them, and re-layouts: 4.64 us -> none  [body(): own_half = lax.dynamic_slice_in_dim(out_weight, core * half, half, 0)]
    pallas_call x3 -> x4, Pallas kernels: 32.1 us -> 36.4 us  [the longest x3 33.4 us: project(): pl.pallas_call(functools.partial(project_kernel, [len(w) for _, w in piec...]
    ppermute x1, waiting for transfers between devices: 4.77 us -> 0.96 us  [body(): lax.ppermute(attended, 'tensor', tensor_pairs(2, 0))]
    ppermute x16, starting transfers between devices: 14.6 us -> 17 us  [send(): return lax.ppermute(block, 'dp', pairs)]
  transfers between devices with their start and end apart: 23 -> 24, of which waited for: 11 -> 12; matrix products, arithmetic and copies ran while one was open for 2% -> 1% of each run, Pallas kernels for 24% -> 24%
where the time goes in v2:
time: 184 us; the launch traced here: 183 us
  waiting for transfers between devices  59 us (32%)
  Pallas kernels  49.7 us (27%)
  starting transfers between devices  35.2 us (19%)
  blocking collectives  25.5 us (14%)
  local copies, waits for them, and re-layouts  10.7 us (6%)
  other arithmetic  2.74 us (1%)
    ppermute x16, waiting for transfers between devices, send(): return lax.ppermute(block, 'dp', pairs)  37.9 us
    pallas_call x3, Pallas kernels, project(): pl.pallas_call(functools.partial(project_kernel, [len(w) for _, w in piec...  33.4 us
    all_to_all x1, blocking collectives, body(): returned = lax.all_to_all(parts, 'dp', 0, 0, tiled=True)  25.5 us
    ppermute x16, starting transfers between devices, send(): return lax.ppermute(block, 'dp', pairs)  17 us
    unnamed x24, local copies, waits for them, and re-layouts  10.3 us
    all_to_all x1, starting transfers between devices, body(): query_blocks = lax.all_to_all(outgoing, 'dp', 0, 0, tiled=True)  8.13 us
    ppermute x1, waiting for transfers between devices, body(): arrived = lax.ppermute(theirs, 'tensor', tensor_pairs(0, 1))  8.02 us
    pallas_call x2, Pallas kernels, mix(): pl.pallas_call(mix_kernel, grid_spec=pltpu.PrefetchScalarGridSpec(num_sca...  7.24 us
  transfers between devices with their start and end apart: 24, of which 12 were waited for; matrix products, arithmetic and copies ran while one was open for 1% of the time, Pallas kernels for 24%

profile of v2, /device:TPU:0, one launch (start us, length us, event | category | flops | bytes accessed | tf_op | source)
XLA Modules:
  0.0 183.0 jit_solution(8755042626159507069)
XLA Ops:
  0.0 0.9 select_reduce_fusion
  0.9 0.7 compare_convert_fusion
  1.6 1.2 collective-permute-done.refs_9_
  2.9 1.1 copy-done.9
  4.0 1.7 pack_queries.1
  5.7 8.1 %all-to-all-start = ((bf16[16,80,512]{2,1,0:T(8,128)(2,1)}), bf16[16,80,512]{2,1,0:T(8,128)(2,1)S(1)}, u32[]{:S(2)}, u32[]{:S(2)}) async-start(bf16[16,80,512]{2,1,0:T(8,128)(2,1)} %pack_queries.1), calls=%async_computation | async-start | bytes 2621440 | tf_op jit(solution)/shard_map/all_to_all | solution.py:356
  13.9 2.0 %collective-permute-start.1 = (bf16[2,512,512]{2,1,0:T(8,128)(2,1)S(1)}, bf16[2,512,512]{2,1,0:T(8,128)(2,1)}, u32[]{:S(2)}, u32[]{:S(2)}) collective-permute-start(bf16[2,512,512]{2,1,0:T(8,128)(2,1)S(1)} %copy-done.1), channel_id=1, source_target_pairs={{0,32},{8,40},{16,48},{24,56},{32,64},{40,72},{48,80},{56,88},{64,... | collective-permute-start | bytes 3145736 | tf_op jit(solution)/shard_map/ppermute | solution.py:292
  15.9 1.3 collective-permute-start.2
  17.2 3.4 %collective-permute-start.3 = (bf16[2,512,512]{2,1,0:T(8,128)(2,1)S(1)}, bf16[2,512,512]{2,1,0:T(8,128)(2,1)}, u32[]{:S(2)}, u32[]{:S(2)}) collective-permute-start(bf16[2,512,512]{2,1,0:T(8,128)(2,1)S(1)} %copy-done.1), channel_id=1, source_target_pairs={{0,16},{8,24},{16,0},{24,8},{32,48},{40,56},{48,32},{56,40},{64,80... | collective-permute-start | bytes 3145736 | tf_op jit(solution)/shard_map/ppermute | solution.py:292
  20.6 34.2 %collective-permute-done.1.refs_10_ = bf16[2,512,512]{2,1,0:T(8,128)(2,1)} collective-permute-done((bf16[2,512,512]{2,1,0:T(8,128)(2,1)S(1)}, bf16[2,512,512]{2,1,0:T(8,128)(2,1)}, u32[]{:S(2)}, u32[]{:S(2)}) %collective-permute-start.1) | collective-permute-done | bytes 1048608 | tf_op jit(solution)/shard_map/ppermute | solution.py:292
  55.2 0.5 collective-permute-start.9
  55.7 2.7 %collective-permute-start.4 = (bf16[2,512,512]{2,1,0:T(8,128)(2,1)}, bf16[2,512,512]{2,1,0:T(8,128)(2,1)}, u32[]{:S(2)}, u32[]{:S(2)}) collective-permute-start(bf16[2,512,512]{2,1,0:T(8,128)(2,1)} %collective-permute-done.2.refs_12_), channel_id=1, source_target_pairs={{0,96},{8,104},{16,112},{24,120},{32,0},{40,8},{48,16},{56,24},{64... | collective-permute-start | bytes 3145736 | tf_op jit(solution)/shard_map/ppermute | solution.py:292
  58.4 1.0 collective-permute-start.6
  59.5 1.0 copy-done.10
  60.5 1.5 collective-permute-start.5
  62.1 3.0 %split_rows.1 = bf16[4,256,2048]{2,1,0:T(8,128)(2,1)S(1)} custom-call(s32[1]{0:T(128)} %bitcast.5.core, bf16[512,8192]{1,0:T(8,128)(2,1)} %rows.1), custom_call_target="tpu_custom_call" | custom-call | bytes 16777216 | tf_op jit(solution)/shard_map/split_rows/pallas_call | solution.py:109
  65.1 2.0 %copy-done = bf16[4,256,2048]{2,1,0:T(8,128)(2,1)} copy-done((bf16[4,256,2048]{2,1,0:T(8,128)(2,1)}, bf16[4,256,2048]{2,1,0:T(8,128)(2,1)S(1)}, u32[]{:S(2)}) %copy-start) | copy-done | bytes 4194328
  67.1 4.8 %all-to-all-start.1 = ((bf16[4,256,2048]{2,1,0:T(8,128)(2,1)}), bf16[4,256,2048]{2,1,0:T(8,128)(2,1)}, u32[]{:S(2)}, u32[]{:S(2)}) async-start(bf16[4,256,2048]{2,1,0:T(8,128)(2,1)} %copy-done), calls=%async_computation.1 | async-start | bytes 8388608 | tf_op jit(solution)/shard_map/all_to_all | solution.py:365
  72.0 1.2 copy-done.2
  73.2 1.2 copy-done.4
  74.4 15.0 %project.3.refs_12_ = f32[1024,1024]{1,0:T(8,128)} custom-call(s32[8]{0:T(128)S(1)} %stack.107.idx, bf16[1024,8192]{1,0:T(8,128)(2,1)} %bitcast.26, bf16[1024,8192]{1,0:T(8,128)(2,1)} %bitcast.27, bf16[1024,8192]{1,0:T(8,128)(2,1)} %bitcast.28, bf16[1024,8192]{1,0:T(8,128)(2,1)} %bitcast.29, bf16[1024,8192]{1,0:T(8,128)(2,1)} %bitcast.30, ...), custom_call_target="tpu_custom_call" | custom-call | flops 8589934592 | bytes 16777216 | tf_op jit(solution)/shard_map/project/pallas_call | solution.py:86
  89.5 0.5 collective-permute-start.13
  90.3 1.5 collective-permute-start.10
  91.7 1.8 collective-permute-start.11
  93.8 1.5 collective-permute-done.14.refs_11_
  95.3 12.4 %project.4.refs_6_ = f32[1024,1024]{1,0:T(8,128)} custom-call(s32[6]{0:T(128)S(1)} %stack.114.idx, bf16[1024,8192]{1,0:T(8,128)(2,1)} %bitcast.34, bf16[1024,8192]{1,0:T(8,128)(2,1)} %bitcast.35, bf16[1024,8192]{1,0:T(8,128)(2,1)} %bitcast.36, bf16[1024,8192]{1,0:T(8,128)(2,1)} %bitcast.37, bf16[1024,8192]{1,0:T(8,128)(2,1)} %bitcast.38, ...), custom_call_target="tpu_custom_call" | custom-call | flops 6442450944 | bytes 12582912 | tf_op jit(solution)/shard_map/project/pallas_call | solution.py:86
  107.9 0.4 collective-permute-start.16
  108.3 1.5 collective-permute-done.15.refs_4_
  109.9 0.8 copy-done.5
  110.7 0.8 copy-done.7
  111.5 1.0 copy-done.6
  112.6 1.0 copy-done.8
  113.6 6.0 %project.5.keys_values = bf16[1024,1024]{1,0:T(8,128)(2,1)S(1)} custom-call(s32[2]{0:T(128)S(1)} %pad_add_fusion.idx, bf16[1024,8192]{1,0:T(8,128)(2,1)} %bitcast.40, bf16[1024,8192]{1,0:T(8,128)(2,1)} %bitcast.41, bf16[1,512,512]{2,1,0:T(8,128)(2,1)} %collective-permute-done.10.refs_2_, bf16[1,512,512]{2,1,0:T(8,128)(2,1)} %collective-permute-done.11.refs_3_, ...), custom_call_target="tpu_custom_call" | custom-call | flops 2147483648 | bytes 4194304 | tf_op jit(solution)/shard_map/project/pallas_call | solution.py:86
  119.6 1.5 all-to-all-done.1.refs_4_
  121.2 3.0 %attend.1 = bf16[16,64,640]{2,1,0:T(8,128)(2,1)S(1)} custom-call(s32[8]{0:T(128)S(1)} %and_select_fusion.owner, bf16[16,80,512]{2,1,0:T(8,128)(2,1)S(1)} %all-to-all-done.query, bf16[1024,1024]{1,0:T(8,128)(2,1)S(1)} %project.5.keys_values), custom_call_target="tpu_custom_call" | custom-call | tf_op jit(solution)/shard_map/attend/pallas_call | solution.py:191
  124.2 25.5 %all_to_all.15.parts = bf16[16,64,640]{2,1,0:T(8,128)(2,1)S(1)} all-to-all(bf16[16,64,640]{2,1,0:T(8,128)(2,1)S(1)} %attend.1), channel_id=1, replica_groups=mesh['dp'=16,'tensor'=8] {'dp'}, dimensions={0} | all-to-all | bytes 2621440 | tf_op jit(solution)/shard_map/all_to_all | solution.py:370
  149.7 1.3 combine.1.refs_0_
  151.0 0.9 collective-permute-start.17
  151.9 2.4 %collective-permute-start.18 = (bf16[256,512]{1,0:T(8,128)(2,1)S(1)}, bf16[256,512]{1,0:T(8,128)(2,1)S(1)}, u32[]{:S(2)}, u32[]{:S(2)}) collective-permute-start(bf16[256,512]{1,0:T(8,128)(2,1)S(1)} %combine.1.refs_0_), channel_id=1, source_target_pairs={{0,6},{1,7},{2,0},{3,1},{4,2},{5,3},{6,4},{7,5},{8,14},{9,15},{10,... | collective-permute-start | bytes 786440 | tf_op jit(solution)/shard_map/ppermute | solution.py:376
  154.3 1.1 collective-permute-start.19
  155.5 5.7 %collective-permute-done.17.refs_1_ = bf16[256,512]{1,0:T(8,128)(2,1)S(1)} collective-permute-done((bf16[256,512]{1,0:T(8,128)(2,1)S(1)}, bf16[256,512]{1,0:T(8,128)(2,1)S(1)}, u32[]{:S(2)}, u32[]{:S(2)}) %collective-permute-start.17) | collective-permute-done | bytes 262176 | tf_op jit(solution)/shard_map/ppermute | solution.py:375
  161.3 3.7 %collective-permute-done.18.refs_2_ = bf16[256,512]{1,0:T(8,128)(2,1)S(1)} collective-permute-done((bf16[256,512]{1,0:T(8,128)(2,1)S(1)}, bf16[256,512]{1,0:T(8,128)(2,1)S(1)}, u32[]{:S(2)}, u32[]{:S(2)}) %collective-permute-start.18) | collective-permute-done | bytes 262176 | tf_op jit(solution)/shard_map/ppermute | solution.py:376
  165.0 1.0 collective-permute-done.19.refs_3_
  165.9 3.6 %mix.3 = bf16[256,1024]{1,0:T(8,128)(2,1)S(1)} custom-call(s32[6]{0:T(128)S(1)} %stack.116.place, bf16[256,512]{1,0:T(8,128)(2,1)S(1)} %combine.1.refs_0_, bf16[256,512]{1,0:T(8,128)(2,1)S(1)} %collective-permute-done.17.refs_1_, bf16[256,512]{1,0:T(8,128)(2,1)S(1)} %collective-permute-done.18.refs_2_, bf16[256,512]{1,0:T(8,128)(2,1)S(1)} %collective-permute-done.19.refs_3_, ...), custom_call_target="tpu_custom_call" | custom-call | flops 1073741824 | bytes 4194304 | tf_op jit(solution)/shard_map/mix/pallas_call | solution.py:270
  169.5 0.8 collective-permute-start.21
  170.4 3.6 %mix.2 = f32[256,1024]{1,0:T(8,128)S(1)} custom-call(s32[6]{0:T(128)S(1)} %stack.95.place, bf16[256,512]{1,0:T(8,128)(2,1)S(1)} %combine.1.refs_0_, bf16[256,512]{1,0:T(8,128)(2,1)S(1)} %collective-permute-done.17.refs_1_, bf16[256,512]{1,0:T(8,128)(2,1)S(1)} %collective-permute-done.18.refs_2_, bf16[256,512]{1,0:T(8,128)(2,1)S(1)} %collective-permute-done.19.refs_3_, ...), custom_call_target="tpu_custom_call" | custom-call | flops 1073741824 | bytes 4194304 | tf_op jit(solution)/shard_map/mix/pallas_call | solution.py:270
  174.0 8.0 %collective-permute-done.21 = bf16[256,1024]{1,0:T(8,128)(2,1)S(1)} collective-permute-done((bf16[256,1024]{1,0:T(8,128)(2,1)S(1)}, bf16[256,1024]{1,0:T(8,128)(2,1)S(1)}, u32[]{:S(2)}, u32[]{:S(2)}) %collective-permute-start.21) | collective-permute-done | bytes 524320 | tf_op jit(solution)/shard_map/ppermute | solution.py:381
  182.0 1.0 add_convert_fusion
  (47 shorter events, 1.7 us)
Async XLA Ops:
  0.0 13.9 %copy-start.1 = (bf16[2,512,512]{2,1,0:T(8,128)(2,1)S(1)}, bf16[2,512,512]{2,1,0:T(8,128)(2,1)}, u32[]{:S(2)}) copy-start(bf16[2,512,512]{2,1,0:T(8,128)(2,1)} %refs_8_.1) | copy-start | bytes 3145732
  0.0 2.9 %collective-permute-start = (bf16[2,512,512]{2,1,0:T(8,128)(2,1)}, bf16[2,512,512]{2,1,0:T(8,128)(2,1)S(1)}, u32[]{:S(2)}, u32[]{:S(2)}) collective-permute-start(bf16[2,512,512]{2,1,0:T(8,128)(2,1)} %refs_8_.1), channel_id=1, source_target_pairs={{0,8},{8,0},{16,24},{24,16},{32,40},{40,32},{48,56},{56,48},{64,72... | collective-permute-start | bytes 3145736 | tf_op jit(solution)/shard_map/ppermute | solution.py:353
  2.9 56.5 %copy-start.3 = (bf16[2,512,512]{2,1,0:T(8,128)(2,1)}, bf16[2,512,512]{2,1,0:T(8,128)(2,1)S(1)}, u32[]{:S(2)}) copy-start(bf16[2,512,512]{2,1,0:T(8,128)(2,1)S(1)} %collective-permute-done.refs_9_) | copy-start | bytes 3145732
  2.9 1.1 copy-start.9
  5.7 49.4 %all-to-all-start = ((bf16[16,80,512]{2,1,0:T(8,128)(2,1)}), bf16[16,80,512]{2,1,0:T(8,128)(2,1)S(1)}, u32[]{:S(2)}, u32[]{:S(2)}) async-start(bf16[16,80,512]{2,1,0:T(8,128)(2,1)} %pack_queries.1), calls=%async_computation | async-start | bytes 2621440 | tf_op jit(solution)/shard_map/all_to_all | solution.py:356
  13.9 41.0 %collective-permute-start.1 = (bf16[2,512,512]{2,1,0:T(8,128)(2,1)S(1)}, bf16[2,512,512]{2,1,0:T(8,128)(2,1)}, u32[]{:S(2)}, u32[]{:S(2)}) collective-permute-start(bf16[2,512,512]{2,1,0:T(8,128)(2,1)S(1)} %copy-done.1), channel_id=1, source_target_pairs={{0,32},{8,40},{16,48},{24,56},{32,64},{40,72},{48,80},{56,88},{64,... | collective-permute-start | bytes 3145736 | tf_op jit(solution)/shard_map/ppermute | solution.py:292
  15.9 39.0 %collective-permute-start.2 = (bf16[2,512,512]{2,1,0:T(8,128)(2,1)S(1)}, bf16[2,512,512]{2,1,0:T(8,128)(2,1)}, u32[]{:S(2)}, u32[]{:S(2)}) collective-permute-start(bf16[2,512,512]{2,1,0:T(8,128)(2,1)S(1)} %copy-done.1), channel_id=1, source_target_pairs={{0,96},{8,104},{16,112},{24,120},{32,0},{40,8},{48,16},{56,24},{64... | collective-permute-start | bytes 3145736 | tf_op jit(solution)/shard_map/ppermute | solution.py:292
  17.2 38.0 %collective-permute-start.3 = (bf16[2,512,512]{2,1,0:T(8,128)(2,1)S(1)}, bf16[2,512,512]{2,1,0:T(8,128)(2,1)}, u32[]{:S(2)}, u32[]{:S(2)}) collective-permute-start(bf16[2,512,512]{2,1,0:T(8,128)(2,1)S(1)} %copy-done.1), channel_id=1, source_target_pairs={{0,16},{8,24},{16,0},{24,8},{32,48},{40,56},{48,32},{56,40},{64,80... | collective-permute-start | bytes 3145736 | tf_op jit(solution)/shard_map/ppermute | solution.py:292
  55.1 4.3 %collective-permute-start.8 = (bf16[2,512,512]{2,1,0:T(8,128)(2,1)}, bf16[2,512,512]{2,1,0:T(8,128)(2,1)S(1)}, u32[]{:S(2)}, u32[]{:S(2)}) collective-permute-start(bf16[2,512,512]{2,1,0:T(8,128)(2,1)} %collective-permute-done.2.refs_12_), channel_id=1, source_target_pairs={{0,8},{8,0},{16,24},{24,16},{32,40},{40,32},{48,56},{56,48},{64,72... | collective-permute-start | bytes 3145736 | tf_op jit(solution)/shard_map/ppermute | solution.py:292
  55.2 16.8 %collective-permute-start.9 = (bf16[2,512,512]{2,1,0:T(8,128)(2,1)}, bf16[2,512,512]{2,1,0:T(8,128)(2,1)}, u32[]{:S(2)}, u32[]{:S(2)}) collective-permute-start(bf16[2,512,512]{2,1,0:T(8,128)(2,1)} %collective-permute-done.3.refs_14_), channel_id=1, source_target_pairs={{0,8},{8,0},{16,24},{24,16},{32,40},{40,32},{48,56},{56,48},{64,72... | collective-permute-start | bytes 3145736 | tf_op jit(solution)/shard_map/ppermute | solution.py:292
  55.7 16.3 %collective-permute-start.7 = (bf16[2,512,512]{2,1,0:T(8,128)(2,1)}, bf16[2,512,512]{2,1,0:T(8,128)(2,1)}, u32[]{:S(2)}, u32[]{:S(2)}) collective-permute-start(bf16[2,512,512]{2,1,0:T(8,128)(2,1)} %collective-permute-done.1.refs_10_), channel_id=1, source_target_pairs={{0,8},{8,0},{16,24},{24,16},{32,40},{40,32},{48,56},{56,48},{64,72... | collective-permute-start | bytes 3145736 | tf_op jit(solution)/shard_map/ppermute | solution.py:292
  55.7 33.7 %collective-permute-start.4 = (bf16[2,512,512]{2,1,0:T(8,128)(2,1)}, bf16[2,512,512]{2,1,0:T(8,128)(2,1)}, u32[]{:S(2)}, u32[]{:S(2)}) collective-permute-start(bf16[2,512,512]{2,1,0:T(8,128)(2,1)} %collective-permute-done.2.refs_12_), channel_id=1, source_target_pairs={{0,96},{8,104},{16,112},{24,120},{32,0},{40,8},{48,16},{56,24},{64... | collective-permute-start | bytes 3145736 | tf_op jit(solution)/shard_map/ppermute | solution.py:292
  58.4 31.0 %collective-permute-start.6 = (bf16[2,512,512]{2,1,0:T(8,128)(2,1)}, bf16[2,512,512]{2,1,0:T(8,128)(2,1)S(1)}, u32[]{:S(2)}, u32[]{:S(2)}) collective-permute-start(bf16[2,512,512]{2,1,0:T(8,128)(2,1)} %collective-permute-done.2.refs_12_), channel_id=1, source_target_pairs={{0,16},{8,24},{16,0},{24,8},{32,48},{40,56},{48,32},{56,40},{64,80... | collective-permute-start | bytes 3145736 | tf_op jit(solution)/shard_map/ppermute | solution.py:292
  59.5 1.0 copy-start.10
  60.5 28.9 %collective-permute-start.5 = (bf16[2,512,512]{2,1,0:T(8,128)(2,1)}, bf16[2,512,512]{2,1,0:T(8,128)(2,1)S(1)}, u32[]{:S(2)}, u32[]{:S(2)}) collective-permute-start(bf16[2,512,512]{2,1,0:T(8,128)(2,1)} %collective-permute-done.3.refs_14_), channel_id=1, source_target_pairs={{0,32},{8,40},{16,48},{24,56},{32,64},{40,72},{48,80},{56,88},{64,... | collective-permute-start | bytes 3145736 | tf_op jit(solution)/shard_map/ppermute | solution.py:292
  65.1 2.0 %copy-start = (bf16[4,256,2048]{2,1,0:T(8,128)(2,1)}, bf16[4,256,2048]{2,1,0:T(8,128)(2,1)S(1)}, u32[]{:S(2)}) copy-start(bf16[4,256,2048]{2,1,0:T(8,128)(2,1)S(1)} %split_rows.1) | copy-start | bytes 12582916
  67.1 54.0 %all-to-all-start.1 = ((bf16[4,256,2048]{2,1,0:T(8,128)(2,1)}), bf16[4,256,2048]{2,1,0:T(8,128)(2,1)}, u32[]{:S(2)}, u32[]{:S(2)}) async-start(bf16[4,256,2048]{2,1,0:T(8,128)(2,1)} %copy-done), calls=%async_computation.1 | async-start | bytes 8388608 | tf_op jit(solution)/shard_map/all_to_all | solution.py:365
  72.0 1.2 copy-start.2
  73.2 1.2 copy-start.4
  89.4 4.2 %collective-permute-start.12 = (bf16[2,512,512]{2,1,0:T(8,128)(2,1)}, bf16[2,512,512]{2,1,0:T(8,128)(2,1)}, u32[]{:S(2)}, u32[]{:S(2)}) collective-permute-start(bf16[2,512,512]{2,1,0:T(8,128)(2,1)} %collective-permute-done.4.refs_6_), channel_id=1, source_target_pairs={{0,8},{8,0},{16,24},{24,16},{32,40},{40,32},{48,56},{56,48},{64,72... | collective-permute-start | bytes 3145736 | tf_op jit(solution)/shard_map/ppermute | solution.py:292
  89.5 4.3 %collective-permute-start.13 = (bf16[2,512,512]{2,1,0:T(8,128)(2,1)S(1)}, bf16[2,512,512]{2,1,0:T(8,128)(2,1)}, u32[]{:S(2)}, u32[]{:S(2)}) collective-permute-start(bf16[2,512,512]{2,1,0:T(8,128)(2,1)S(1)} %collective-permute-done.5.refs_8_), channel_id=1, source_target_pairs={{0,8},{8,0},{16,24},{24,16},{32,40},{40,32},{48,56},{56,48},{64,72... | collective-permute-start | bytes 3145736 | tf_op jit(solution)/shard_map/ppermute | solution.py:292
  90.0 5.3 %collective-permute-start.14 = (bf16[2,512,512]{2,1,0:T(8,128)(2,1)S(1)}, bf16[2,512,512]{2,1,0:T(8,128)(2,1)}, u32[]{:S(2)}, u32[]{:S(2)}) collective-permute-start(bf16[2,512,512]{2,1,0:T(8,128)(2,1)S(1)} %collective-permute-done.6.refs_10_), channel_id=1, source_target_pairs={{0,8},{8,0},{16,24},{24,16},{32,40},{40,32},{48,56},{56,48},{64,72... | collective-permute-start | bytes 3145736 | tf_op jit(solution)/shard_map/ppermute | solution.py:292
  90.3 17.4 %collective-permute-start.10 = (bf16[1,512,512]{2,1,0:T(8,128)(2,1)S(1)}, bf16[1,512,512]{2,1,0:T(8,128)(2,1)}, u32[]{:S(2)}, u32[]{:S(2)}) collective-permute-start(bf16[1,512,512]{2,1,0:T(8,128)(2,1)S(1)} %slice.6), channel_id=1, source_target_pairs={{0,32},{8,40},{16,48},{24,56},{32,64},{40,72},{48,80},{56,88},{64,... | collective-permute-start | bytes 1572872 | tf_op jit(solution)/shard_map/ppermute | solution.py:292
  91.7 15.9 %collective-permute-start.11 = (bf16[1,512,512]{2,1,0:T(8,128)(2,1)S(1)}, bf16[1,512,512]{2,1,0:T(8,128)(2,1)}, u32[]{:S(2)}, u32[]{:S(2)}) collective-permute-start(bf16[1,512,512]{2,1,0:T(8,128)(2,1)S(1)} %slice.7), channel_id=1, source_target_pairs={{0,96},{8,104},{16,112},{24,120},{32,0},{40,8},{48,16},{56,24},{64... | collective-permute-start | bytes 1572872 | tf_op jit(solution)/shard_map/ppermute | solution.py:292
  107.7 2.2 %collective-permute-start.15 = (bf16[1,512,512]{2,1,0:T(8,128)(2,1)}, bf16[1,512,512]{2,1,0:T(8,128)(2,1)S(1)}, u32[]{:S(2)}, u32[]{:S(2)}) collective-permute-start(bf16[1,512,512]{2,1,0:T(8,128)(2,1)} %collective-permute-done.10.refs_2_), channel_id=1, source_target_pairs={{0,8},{8,0},{16,24},{24,16},{32,40},{40,32},{48,56},{56,48},{64,72... | collective-permute-start | bytes 1572872 | tf_op jit(solution)/shard_map/ppermute | solution.py:292
  107.9 2.8 %collective-permute-start.16 = (bf16[1,512,512]{2,1,0:T(8,128)(2,1)}, bf16[1,512,512]{2,1,0:T(8,128)(2,1)S(1)}, u32[]{:S(2)}, u32[]{:S(2)}) collective-permute-start(bf16[1,512,512]{2,1,0:T(8,128)(2,1)} %collective-permute-done.11.refs_3_), channel_id=1, source_target_pairs={{0,8},{8,0},{16,24},{24,16},{32,40},{40,32},{48,56},{56,48},{64,72... | collective-permute-start | bytes 1572872 | tf_op jit(solution)/shard_map/ppermute | solution.py:292
  108.3 12.8 %copy-start.11 = (s32[128]{0:T(128)S(1)}, s32[128]{0:T(128)}, u32[]{:S(2)}) copy-start(s32[128]{0:T(128)} %param.11) | copy-start | bytes 1540
  109.9 0.8 copy-start.5
  110.7 0.8 copy-start.7
  111.5 1.0 copy-start.6
  112.6 1.0 copy-start.8
  121.1 44.8 %collective-permute-start.20 = (bf16[4,256,2048]{2,1,0:T(8,128)(2,1)}, bf16[4,256,2048]{2,1,0:T(8,128)(2,1)}, u32[]{:S(2)}, u32[]{:S(2)}) collective-permute-start(bf16[4,256,2048]{2,1,0:T(8,128)(2,1)} %all-to-all-done.1.refs_4_), channel_id=1, source_target_pairs={{0,8},{8,0},{16,24},{24,16},{32,40},{40,32},{48,56},{56,48},{64,72... | collective-permute-start | bytes 12582920 | tf_op jit(solution)/shard_map/ppermute | solution.py:367
  151.0 10.3 %collective-permute-start.17 = (bf16[256,512]{1,0:T(8,128)(2,1)S(1)}, bf16[256,512]{1,0:T(8,128)(2,1)S(1)}, u32[]{:S(2)}, u32[]{:S(2)}) collective-permute-start(bf16[256,512]{1,0:T(8,128)(2,1)S(1)} %combine.1.refs_0_), channel_id=1, source_target_pairs={{0,2},{1,3},{2,4},{3,5},{4,6},{5,7},{6,0},{7,1},{8,10},{9,11},{10,... | collective-permute-start | bytes 786440 | tf_op jit(solution)/shard_map/ppermute | solution.py:375
  151.9 13.0 %collective-permute-start.18 = (bf16[256,512]{1,0:T(8,128)(2,1)S(1)}, bf16[256,512]{1,0:T(8,128)(2,1)S(1)}, u32[]{:S(2)}, u32[]{:S(2)}) collective-permute-start(bf16[256,512]{1,0:T(8,128)(2,1)S(1)} %combine.1.refs_0_), channel_id=1, source_target_pairs={{0,6},{1,7},{2,0},{3,1},{4,2},{5,3},{6,4},{7,5},{8,14},{9,15},{10,... | collective-permute-start | bytes 786440 | tf_op jit(solution)/shard_map/ppermute | solution.py:376
  154.3 11.6 %collective-permute-start.19 = (bf16[256,512]{1,0:T(8,128)(2,1)S(1)}, bf16[256,512]{1,0:T(8,128)(2,1)S(1)}, u32[]{:S(2)}, u32[]{:S(2)}) collective-permute-start(bf16[256,512]{1,0:T(8,128)(2,1)S(1)} %combine.1.refs_0_), channel_id=1, source_target_pairs={{0,4},{1,5},{2,6},{3,7},{4,0},{5,1},{6,2},{7,3},{8,12},{9,13},{10,... | collective-permute-start | bytes 786440 | tf_op jit(solution)/shard_map/ppermute | solution.py:377
  169.5 12.5 %collective-permute-start.21 = (bf16[256,1024]{1,0:T(8,128)(2,1)S(1)}, bf16[256,1024]{1,0:T(8,128)(2,1)S(1)}, u32[]{:S(2)}, u32[]{:S(2)}) collective-permute-start(bf16[256,1024]{1,0:T(8,128)(2,1)S(1)} %mix.3), channel_id=1, source_target_pairs={{0,1},{1,0},{2,3},{3,2},{4,5},{5,4},{6,7},{7,6},{8,9},{9,8},{10,11... | collective-permute-start | bytes 1572872 | tf_op jit(solution)/shard_map/ppermute | solution.py:381

commit v3 on v2

v3 whole, which is shorter than its diff:
```python
import functools
import math

import jax
import jax.numpy as jnp
from jax import lax
from jax.experimental import pallas as pl
from jax.experimental.pallas import tpu as pltpu
from jax.sharding import PartitionSpec as P

HD = 128
M = 64
BF = jnp.bfloat16
F32 = jnp.float32
ATTEND_SLOTS = 2
VMEM_LIMIT = 48 * 1024 * 1024


def dp_pairs(dz, dy, dc):
    pairs = []
    for i in range(16):
        z, y, c = i // 4, (i // 2) % 2, i % 2
        pairs.append((i, ((z + dz) % 4) * 4 + ((y + dy) % 2) * 2 + (c + dc) % 2))
    return pairs


def tensor_pairs(dx, dy):
    pairs = []
    for i in range(8):
        x, y = i // 2, i % 2
        pairs.append((i, ((x + dx) % 4) * 2 + (y + dy) % 2))
    return pairs


Z_UP, Z_DOWN = dp_pairs(1, 0, 0), dp_pairs(-1, 0, 0)
Y_SWAP, CORE_SWAP = dp_pairs(0, 1, 0), dp_pairs(0, 0, 1)


def vmem_specs(count):
    return [pl.BlockSpec(memory_space=pltpu.VMEM)] * count


def add_terms(sizes, rows, weight_refs, total, out):
    weights = []
    at = 0
    for size in sizes:
        if size == 1:
            weights.append((weight_refs[at].at[0], weight_refs[at].at[1]))
        else:
            weights.append((weight_refs[at].at[0], weight_refs[at + 1].at[0]))
        at += size
    columns = out.shape[1] // 2
    for side in range(2):
        cols = slice(side * columns, (side + 1) * columns)
        value = None if total is None else total[:, cols]
        for row, weight in zip(rows, weights):
            term = jnp.dot(row[...], weight[side][...], preferred_element_type=F32)
            value = term if value is None else value + term
        out[:, cols] = value.astype(out.dtype)


def project_kernel(sizes, has_total, idx, *refs):
    del idx
    blocks = len(sizes)
    rows, weights = refs[:blocks], refs[blocks : blocks + sum(sizes)]
    add_terms(sizes, rows, weights, refs[-2] if has_total else None, refs[-1])


def project_operands(encoded, pieces, tile):
    arrays = [array for _, weight in pieces for array in weight]
    depth = arrays[0].shape[1]
    specs = [
        pl.BlockSpec((tile, depth), lambda m, i, j=j: (m, i[j])) for j in range(len(pieces))
    ] + [
        pl.BlockSpec(array.shape, lambda m, i: (0, 0, 0), pipeline_mode=pl.Buffered(1))
        for array in arrays
    ]
    return specs, [encoded] * len(pieces) + arrays


def project(encoded, pieces, total):
    rows = encoded.shape[0]
    depth, columns = pieces[0][1][0].shape[1:]
    tile = 256
    in_specs, operands = project_operands(encoded, pieces, tile)
    total_spec = pl.BlockSpec((tile, 2 * columns), lambda m, i: (m, 0))
    if total is not None:
        in_specs.append(total_spec)
        operands.append(total)
    return pl.pallas_call(
        functools.partial(project_kernel, [len(w) for _, w in pieces], total is not None),
        grid_spec=pltpu.PrefetchScalarGridSpec(
            num_scalar_prefetch=1, grid=(rows // tile,), in_specs=in_specs, out_specs=total_spec
        ),
        out_shape=jax.ShapeDtypeStruct((rows, 2 * columns), F32),
        compiler_params=pltpu.CompilerParams(vmem_limit_bytes=VMEM_LIMIT),
        cost_estimate=pl.CostEstimate(
            flops=4 * rows * depth * columns * len(pieces),
            bytes_accessed=2 * len(pieces) * depth * (rows + 2 * columns),
            transcendentals=0,
        ),
        name="project",
    )(jnp.stack([place for place, _ in pieces]).astype(jnp.int32), *operands)


def split_kernel(place, *refs):
    del place
    count = len(refs) // 2
    for source, target in zip(refs[:count], refs[count:]):
        target[...] = source[...]


def split_rows(core, places, weight):
    parts = len(places)
    half, width = weight.shape[0] // 2, weight.shape[1] // parts
    tile = half // 4
    return pl.pallas_call(
        split_kernel,
        grid_spec=pltpu.PrefetchScalarGridSpec(
            num_scalar_prefetch=1,
            grid=(4,),
            in_specs=[
                pl.BlockSpec((tile, width), lambda m, place, r=r: (place[parts] * 4 + m, place[r]))
                for r in range(parts)
            ],
            out_specs=[pl.BlockSpec((tile, width), lambda m, place: (m, 0))] * parts,
        ),
        out_shape=[jax.ShapeDtypeStruct((half, width), weight.dtype)] * parts,
        compiler_params=pltpu.CompilerParams(vmem_limit_bytes=VMEM_LIMIT),
        cost_estimate=pl.CostEstimate(
            flops=0, bytes_accessed=half * width // 8, transcendentals=0
        ),
        name="split_rows",
    )(jnp.stack(places + [core]), *[weight] * parts)


def pack_kernel(holder, query, valid, out):
    rows = query.shape[0]
    shifted = pltpu.roll(query[...].astype(F32), rows - (M - 1), 0).astype(BF)
    for j in range(valid.shape[0]):
        u = j // 2
        out[holder[j], :M, :] = shifted[u * M : (u + 1) * M]
        out[holder[j], M:, :] = jnp.tile(valid[j : j + 1, :], (16, query.shape[1] // HD)).astype(BF)


def pack_queries(query, valid, holder, groups):
    return pl.pallas_call(
        pack_kernel,
        in_specs=[pl.BlockSpec(memory_space=pltpu.SMEM)] + vmem_specs(2),
        out_specs=pl.BlockSpec(memory_space=pltpu.VMEM),
        out_shape=jax.ShapeDtypeStruct((groups, M + 16, query.shape[1]), BF),
        compiler_params=pltpu.CompilerParams(vmem_limit_bytes=VMEM_LIMIT),
        name="pack_queries",
    )(holder, query, valid)


def attend_kernel(sizes, idx, *refs):
    blocks = len(sizes)
    rows, weights = refs[:blocks], refs[blocks : blocks + sum(sizes)]
    total, query, out, keys_values = refs[-4:]
    add_terms(sizes, rows, weights, total, keys_values)
    heads = query.shape[2] // HD
    span = keys_values.shape[0] // ATTEND_SLOTS
    lane = lax.broadcasted_iota(jnp.int32, (M, HD), 1)
    pairs = [(i, h) for i in range(ATTEND_SLOTS) for h in range(heads)]
    places = [idx[blocks + pl.program_id(0) * ATTEND_SLOTS + i] for i in range(ATTEND_SLOTS)]
    scores = {}
    for i, h in pairs:
        cols = slice(h * HD, (h + 1) * HD)
        scores[i, h] = lax.dot_general(
            query[places[i], :M, cols],
            keys_values[i * span : (i + 1) * span, cols],
            (((1,), (1,)), ((), ())),
            preferred_element_type=F32,
        )
    valid = [query[place, M : M + 1, :span].astype(F32) > 0.5 for place in places]
    shares, levels = {}, {}
    for i, h in pairs:
        scaled = jnp.where(valid[i], scores[i, h] * (1.0 / math.sqrt(HD)), -jnp.inf)
        highest = jnp.max(scaled, axis=1, keepdims=True)
        raised = jnp.exp(scaled - highest)
        norm = jnp.sum(raised, axis=1, keepdims=True)
        shares[i, h] = (raised / norm).astype(BF)
        levels[i, h] = highest + jnp.log(norm)
    for i, h in pairs:
        out[places[i], :, h * HD : (h + 1) * HD] = jnp.dot(
            shares[i, h],
            keys_values[i * span : (i + 1) * span, (heads + h) * HD : (heads + h + 1) * HD],
            preferred_element_type=F32,
        ).astype(BF)
    for i in range(ATTEND_SLOTS):
        stats = jnp.zeros((M, HD), F32)
        for h in range(heads):
            first = levels[i, h].astype(BF).astype(F32)
            second = (levels[i, h] - first).astype(BF).astype(F32)
            third = levels[i, h] - first - second
            stats = jnp.where(lane == 3 * h, first, stats)
            stats = jnp.where(lane == 3 * h + 1, second, stats)
            stats = jnp.where(lane == 3 * h + 2, third, stats)
        out[places[i], :, heads * HD :] = stats.astype(BF)


def attend(encoded, pieces, total, owner, query_blocks):
    groups, query_rows, columns = query_blocks.shape
    rows = encoded.shape[0]
    tile = rows // owner.shape[0] * ATTEND_SLOTS
    in_specs, operands = project_operands(encoded, pieces, tile)
    places = jnp.concatenate([jnp.stack([place for place, _ in pieces]).astype(jnp.int32), owner])
    return pl.pallas_call(
        functools.partial(attend_kernel, [len(w) for _, w in pieces]),
        grid_spec=pltpu.PrefetchScalarGridSpec(
            num_scalar_prefetch=1,
            grid=(rows // tile,),
            in_specs=in_specs
            + [
                pl.BlockSpec((tile, 2 * columns), lambda m, i: (m, 0)),
                pl.BlockSpec((groups, query_rows, columns), lambda m, i: (0, 0, 0)),
            ],
            out_specs=pl.BlockSpec((groups, M, columns + HD), lambda m, i: (0, 0, 0)),
            scratch_shapes=[pltpu.VMEM((tile, 2 * columns), BF)],
        ),
        out_shape=jax.ShapeDtypeStruct((groups, M, columns + HD), BF),
        compiler_params=pltpu.CompilerParams(vmem_limit_bytes=VMEM_LIMIT),
        name="attend",
    )(places, *operands, total, query_blocks)


def combine_kernel(holder, parts, out):
    rows, columns = out.shape
    heads = columns // HD
    flat = []
    for u in range(rows // M):
        first, second = parts[holder[2 * u]], parts[holder[2 * u + 1]]
        levels = [part[:, columns:].astype(F32) for part in (first, second)]
        pieces = []
        for h in range(heads):
            cols = slice(h * HD, (h + 1) * HD)
            one, two = [
                level[:, 3 * h : 3 * h + 1]
                + level[:, 3 * h + 1 : 3 * h + 2]
                + level[:, 3 * h + 2 : 3 * h + 3]
                for level in levels
            ]
            top = jnp.maximum(one, two)
            share_one, share_two = jnp.exp(one - top), jnp.exp(two - top)
            both = share_one + share_two
            pieces.append(
                first[:, cols].astype(F32) * (share_one / both)
                + second[:, cols].astype(F32) * (share_two / both)
            )
        flat.append(jnp.concatenate(pieces, axis=1))
    shifted = pltpu.roll(jnp.concatenate(flat, axis=0), M - 1, 0)
    row = lax.broadcasted_iota(jnp.int32, (rows, columns), 0)
    out[...] = jnp.where(row >= M - 1, shifted, 0.0).astype(BF)


def combine(holder, parts, rows):
    columns = parts.shape[2] - HD
    return pl.pallas_call(
        combine_kernel,
        in_specs=[pl.BlockSpec(memory_space=pltpu.SMEM)] + vmem_specs(1),
        out_specs=pl.BlockSpec(memory_space=pltpu.VMEM),
        out_shape=jax.ShapeDtypeStruct((rows, columns), BF),
        compiler_params=pltpu.CompilerParams(vmem_limit_bytes=VMEM_LIMIT),
        name="combine",
    )(holder, parts)


def mix_kernel(place, *refs):
    attended, mine, other, out = refs[:4], refs[4:8], refs[8:12], refs[12]
    core = place[1]
    half = mine[0].shape[0]
    total = None
    for r in range(4):
        for swap, weight in ((0, mine[r]), (1, other[r])):
            cols = pl.ds(pl.multiple_of(((core + swap) % 2) * half, half), half)
            term = jnp.dot(attended[r][:, cols], weight[...], preferred_element_type=F32)
            total = term if total is None else total + term
    out[...] = total.astype(out.dtype)


def mix(place, attended, mine, other, kind):
    rows, columns = attended[0].shape
    half, width = mine[0].shape[0], mine[0].shape[1] // 2
    tile = width // 2
    weight_spec = pl.BlockSpec((half, tile), lambda j, place: (0, place[0] * 2 + j))
    return pl.pallas_call(
        mix_kernel,
        grid_spec=pltpu.PrefetchScalarGridSpec(
            num_scalar_prefetch=1,
            grid=(2,),
            in_specs=[pl.BlockSpec((rows, columns), lambda j, place: (0, 0))] * 4
            + [weight_spec] * 8,
            out_specs=pl.BlockSpec((rows, tile), lambda j, place: (0, j)),
        ),
        out_shape=jax.ShapeDtypeStruct((rows, width), kind),
        compiler_params=pltpu.CompilerParams(vmem_limit_bytes=VMEM_LIMIT),
        cost_estimate=pl.CostEstimate(
            flops=8 * rows * columns * width, bytes_accessed=8 * columns * width, transcendentals=0
        ),
        name="mix",
    )(place, *attended, *mine, *other)


def body(encoded_neighbours, kv_weight, queries, out_weight, neighbour_ids, slot_map):
    groups = lax.axis_size("dp")
    position = lax.axis_index("dp")
    tensor_at = lax.axis_index("tensor")
    z, y, core = position // 4, (position // 2) % 2, position % 2
    x, y_lo = tensor_at // 2, tensor_at % 2
    slot_count, span, model_width = encoded_neighbours.shape
    encoded = encoded_neighbours.reshape(slot_count * span, model_width)
    held = lax.dynamic_slice_in_dim(slot_map, position * slot_count, slot_count)
    owner = held // slot_count
    wanted = position * slot_count + jnp.arange(slot_count, dtype=jnp.int32)
    holder = (
        jnp.sum(
            jnp.where(
                slot_map[None, :] == wanted[:, None],
                jnp.arange(slot_map.shape[0], dtype=jnp.int32)[None, :],
                0,
            ),
            axis=1,
        )
        // slot_count
    )
    valid = (neighbour_ids.reshape(slot_count, span) != 0).astype(F32)

    def send(block, pairs):
        return lax.ppermute(block, "dp", pairs)

    def across_x(block, step):
        return lax.ppermute(block, "tensor", tensor_pairs(step, 0))

    def with_twin(dz, dy, *arrays):
        def at(dc):
            return ((z + dz) % 4) * 4 + ((y + dy) % 2) * 2 + (core + dc) % 2

        return [(at(0), arrays), (at(1), tuple(send(array, CORE_SWAP) for array in arrays))]

    own = kv_weight
    below, above, across = send(own, Z_UP), send(own, Z_DOWN), send(own, Y_SWAP)
    mix_own, to_next, to_last, to_far = split_rows(
        core, [x, (x + 1) % 4, (x + 3) % 4, (x + 2) % 4], out_weight
    )
    total = project(encoded, with_twin(0, 0, own), None)
    below, above, across, total, to_next = lax.optimization_barrier(
        (below, above, across, total, to_next)
    )

    far, across_below, across_above = send(above, Z_DOWN), send(across, Z_UP), send(above, Y_SWAP)
    mix_last = across_x(to_next, 1)
    total = project(
        encoded,
        with_twin(-1, 0, below) + with_twin(1, 0, above) + with_twin(0, 1, across),
        total,
    )
    total, late_holder = lax.optimization_barrier((total, holder))
    outgoing = pack_queries(queries, valid, late_holder, groups)
    query_blocks = lax.all_to_all(outgoing, "dp", 0, 0, tiled=True)
    far, across_below, across_above, total, mix_last, to_last, outgoing = lax.optimization_barrier(
        (far, across_below, across_above, total, mix_last, to_last, outgoing)
    )

    far_keys, far_values = send(across_below[:1], Z_UP), send(across_above[1:], Z_DOWN)
    mix_next = across_x(to_last, -1)
    total = project(
        encoded,
        with_twin(2, 0, far) + with_twin(-1, 1, across_below) + with_twin(1, 1, across_above),
        total,
    )
    far_keys, far_values, total, mix_next, to_far = lax.optimization_barrier(
        (far_keys, far_values, total, mix_next, to_far)
    )

    mix_far = across_x(to_far, 2)
    parts = attend(encoded, with_twin(2, 1, far_keys, far_values), total, owner, query_blocks)
    returned = lax.all_to_all(parts, "dp", 0, 0, tiled=True)
    attended = combine(holder, returned, queries.shape[0])

    near = [attended, across_x(attended, 1), across_x(attended, -1), across_x(attended, 2)]
    mine = [mix_own, mix_last, mix_next, mix_far]
    other = [send(block, CORE_SWAP) for block in mine]
    theirs = mix(jnp.stack([1 - y_lo, core]), near, mine, other, BF)
    arrived = lax.ppermute(theirs, "tensor", tensor_pairs(0, 1))
    ours = mix(jnp.stack([y_lo, core]), near, mine, other, F32)
    return (ours + arrived.astype(F32)).astype(BF)


def solution(mesh):
    placed = (
        P("dp", None, None),
        P(None, "dp", "tensor"),
        P("dp", "tensor"),
        P("tensor", None),
        P("dp", None, None, None),
        P(),
    )
    return jax.shard_map(
        body, mesh=mesh, in_specs=placed, out_specs=P("dp", "tensor"), check_vma=False
    )
```

time: 184 us -> 176 us (0.957)
  blocking collectives: 25.5 us -> 0 us
  waiting for transfers between devices: 59 us -> 72.1 us
  Pallas kernels: 49.7 us -> 56.7 us
  local copies, waits for them, and re-layouts: 10.7 us -> 5.6 us
  starting transfers between devices: 35.2 us -> 38.5 us
    all_to_all x1 -> x0, blocking collectives: 25.5 us -> none  [body(): returned = lax.all_to_all(parts, 'dp', 0, 0, tiled=True)]
    ppermute x5 -> x6, waiting for transfers between devices: 11.6 us -> 27.3 us  [across_x(): return lax.ppermute(block, 'tensor', tensor_pairs(step, 0))]
    ppermute x16 -> x21, waiting for transfers between devices: 37.9 us -> 24.7 us  [send(): return lax.ppermute(block, 'dp', pairs)]
    all_to_all x1, waiting for transfers between devices: 1.45 us -> 12.2 us  [body(): returned = lax.all_to_all(parts, 'dp', 0, 0, tiled=True)]
    unnamed x24 -> x14, local copies, waits for them, and re-layouts: 10.3 us -> 3.19 us
    pallas_call x1, Pallas kernels: 2.99 us -> 8.72 us  [attend(): pl.pallas_call(functools.partial(attend_kernel, [len(w) for _, w in piece...]
    ppermute x5 -> x6, starting transfers between devices: 4.43 us -> 8.6 us  [across_x(): return lax.ppermute(block, 'tensor', tensor_pairs(step, 0))]
    all_to_all x1, starting transfers between devices: 8.13 us -> 5.26 us  [body(): query_blocks = lax.all_to_all(outgoing, 'dp', 0, 0, tiled=True)]
  transfers between devices with their start and end apart: 24 -> 30, of which waited for: 12 -> 12; matrix products, arithmetic and copies ran while one was open for 1% -> 2% of each run, Pallas kernels for 24% -> 30%
where the time goes in v3:
time: 176 us; the launch traced here: 175 us
  waiting for transfers between devices  72.1 us (41%)
  Pallas kernels  56.7 us (32%)
  starting transfers between devices  38.5 us (22%)
  local copies, waits for them, and re-layouts  5.6 us (3%)
    pallas_call x3, Pallas kernels, project(): pl.pallas_call(functools.partial(project_kernel, [len(w) for _, w in piec...  32.1 us
    ppermute x6, waiting for transfers between devices, across_x(): return lax.ppermute(block, 'tensor', tensor_pairs(step, 0))  27.3 us
    ppermute x21, waiting for transfers between devices, send(): return lax.ppermute(block, 'dp', pairs)  24.7 us
    ppermute x21, starting transfers between devices, send(): return lax.ppermute(block, 'dp', pairs)  18.6 us
    all_to_all x1, waiting for transfers between devices, body(): returned = lax.all_to_all(parts, 'dp', 0, 0, tiled=True)  12.2 us
    pallas_call x1, Pallas kernels, attend(): pl.pallas_call(functools.partial(attend_kernel, [len(w) for _, w in piece...  8.72 us
    ppermute x6, starting transfers between devices, across_x(): return lax.ppermute(block, 'tensor', tensor_pairs(step, 0))  8.6 us
    ppermute x1, waiting for transfers between devices, body(): arrived = lax.ppermute(theirs, 'tensor', tensor_pairs(0, 1))  7.98 us
  transfers between devices with their start and end apart: 30, of which 12 were waited for; matrix products, arithmetic and copies ran while one was open for 2% of the time, Pallas kernels for 30%

profile of v3, /device:TPU:0, one launch (start us, length us, event | category | flops | bytes accessed | tf_op | source)
XLA Modules:
  0.0 174.8 jit_solution(831770747050830617)
XLA Ops:
  0.0 2.0 %collective-permute-start = (bf16[2,512,512]{2,1,0:T(8,128)(2,1)}, bf16[2,512,512]{2,1,0:T(8,128)(2,1)S(1)}, u32[]{:S(2)}, u32[]{:S(2)}) collective-permute-start(bf16[2,512,512]{2,1,0:T(8,128)(2,1)} %refs_2_.2), channel_id=1, source_target_pairs={{0,32},{8,40},{16,48},{24,56},{32,64},{40,72},{48,80},{56,88},{64,... | collective-permute-start | bytes 3145736 | tf_op jit(solution)/shard_map/ppermute | solution.py:330
  2.0 2.2 %collective-permute-start.1 = (bf16[2,512,512]{2,1,0:T(8,128)(2,1)}, bf16[2,512,512]{2,1,0:T(8,128)(2,1)S(1)}, u32[]{:S(2)}, u32[]{:S(2)}) collective-permute-start(bf16[2,512,512]{2,1,0:T(8,128)(2,1)} %refs_2_.2), channel_id=1, source_target_pairs={{0,96},{8,104},{16,112},{24,120},{32,0},{40,8},{48,16},{56,24},{64... | collective-permute-start | bytes 3145736 | tf_op jit(solution)/shard_map/ppermute | solution.py:330
  4.2 3.2 %collective-permute-start.2 = (bf16[2,512,512]{2,1,0:T(8,128)(2,1)}, bf16[2,512,512]{2,1,0:T(8,128)(2,1)}, u32[]{:S(2)}, u32[]{:S(2)}) collective-permute-start(bf16[2,512,512]{2,1,0:T(8,128)(2,1)} %refs_2_.2), channel_id=1, source_target_pairs={{0,16},{8,24},{16,0},{24,8},{32,48},{40,56},{48,32},{56,40},{64,80... | collective-permute-start | bytes 3145736 | tf_op jit(solution)/shard_map/ppermute | solution.py:330
  7.5 4.7 %split_rows.1 = (bf16[256,2048]{1,0:T(8,128)(2,1)S(1)}, bf16[256,2048]{1,0:T(8,128)(2,1)S(1)}, bf16[256,2048]{1,0:T(8,128)(2,1)}, bf16[256,2048]{1,0:T(8,128)(2,1)}) custom-call(s32[5]{0:T(128)S(1)} %stack.101.place, bf16[512,8192]{1,0:T(8,128)(2,1)} %refs_3_.1, bf16[512,8192]{1,0:T(8,128)(2,1)} %refs_3_.1, bf16[512,8192]{1,0:T(8,128)(2,1)} %refs_3_.1, ...), custom_call_target="tpu_custom_call" | custom-call | bytes 65536 | tf_op jit(solution)/shard_map/split_rows/pallas_call | solution.py:117
  12.2 1.0 copy-done.4
  13.3 6.6 %project.3.refs_12_ = f32[1024,1024]{1,0:T(8,128)} custom-call(s32[2]{0:T(128)S(1)} %pad_add_fusion.2.idx, bf16[1024,8192]{1,0:T(8,128)(2,1)} %bitcast.26, bf16[1024,8192]{1,0:T(8,128)(2,1)} %bitcast.27, bf16[2,512,512]{2,1,0:T(8,128)(2,1)S(1)} %copy-done.2, bf16[2,512,512]{2,1,0:T(8,128)(2,1)} %collective-permute-done.3.refs_3_), custom_call_target="tpu_custom_call" | custom-call | flops 2147483648 | bytes 4194304 | tf_op jit(solution)/shard_map/project/pallas_call | solution.py:90
  19.9 8.2 %collective-permute-done.refs_6_ = bf16[2,512,512]{2,1,0:T(8,128)(2,1)S(1)} collective-permute-done((bf16[2,512,512]{2,1,0:T(8,128)(2,1)}, bf16[2,512,512]{2,1,0:T(8,128)(2,1)S(1)}, u32[]{:S(2)}, u32[]{:S(2)}) %collective-permute-start) | collective-permute-done | bytes 1048608 | tf_op jit(solution)/shard_map/ppermute | solution.py:330
  28.2 3.1 %collective-permute-done.2.refs_10_ = bf16[2,512,512]{2,1,0:T(8,128)(2,1)} collective-permute-done((bf16[2,512,512]{2,1,0:T(8,128)(2,1)}, bf16[2,512,512]{2,1,0:T(8,128)(2,1)}, u32[]{:S(2)}, u32[]{:S(2)}) %collective-permute-start.2) | collective-permute-done | bytes 1048608 | tf_op jit(solution)/shard_map/ppermute | solution.py:330
  31.3 1.0 copy-done
  32.2 0.5 collective-permute-start.8
  33.0 1.8 %collective-permute-start.4 = (bf16[2,512,512]{2,1,0:T(8,128)(2,1)S(1)}, bf16[2,512,512]{2,1,0:T(8,128)(2,1)}, u32[]{:S(2)}, u32[]{:S(2)}) collective-permute-start(bf16[2,512,512]{2,1,0:T(8,128)(2,1)S(1)} %collective-permute-done.1.refs_8_), channel_id=1, source_target_pairs={{0,96},{8,104},{16,112},{24,120},{32,0},{40,8},{48,16},{56,24},{64... | collective-permute-start | bytes 3145736 | tf_op jit(solution)/shard_map/ppermute | solution.py:330
  34.8 0.3 collective-permute-start.5
  35.1 3.2 %collective-permute-start.6 = (bf16[2,512,512]{2,1,0:T(8,128)(2,1)S(1)}, bf16[2,512,512]{2,1,0:T(8,128)(2,1)}, u32[]{:S(2)}, u32[]{:S(2)}) collective-permute-start(bf16[2,512,512]{2,1,0:T(8,128)(2,1)S(1)} %collective-permute-done.1.refs_8_), channel_id=1, source_target_pairs={{0,16},{8,24},{16,0},{24,8},{32,48},{40,56},{48,32},{56,40},{64,80... | collective-permute-start | bytes 3145736 | tf_op jit(solution)/shard_map/ppermute | solution.py:330
  38.3 1.5 collective-permute-start.10
  39.8 1.2 copy-done.1
  41.0 12.4 %project.4.refs_12_ = f32[1024,1024]{1,0:T(8,128)} custom-call(s32[6]{0:T(128)S(1)} %stack.108.idx, bf16[1024,8192]{1,0:T(8,128)(2,1)} %bitcast.28, bf16[1024,8192]{1,0:T(8,128)(2,1)} %bitcast.29, bf16[1024,8192]{1,0:T(8,128)(2,1)} %bitcast.30, bf16[1024,8192]{1,0:T(8,128)(2,1)} %bitcast.31, bf16[1024,8192]{1,0:T(8,128)(2,1)} %bitcast.32, ...), custom_call_target="tpu_custom_call" | custom-call | flops 6442450944 | bytes 12582912 | tf_op jit(solution)/shard_map/project/pallas_call | solution.py:90
  53.5 1.7 pack_queries.1
  55.2 9.3 %collective-permute-done.10.refs_5_ = bf16[256,2048]{1,0:T(8,128)(2,1)S(1)} collective-permute-done((bf16[256,2048]{1,0:T(8,128)(2,1)}, bf16[256,2048]{1,0:T(8,128)(2,1)S(1)}, u32[]{:S(2)}, u32[]{:S(2)}) %collective-permute-start.10) | collective-permute-done | bytes 1048608 | tf_op jit(solution)/shard_map/ppermute | solution.py:333
  64.5 0.5 collective-permute-start.14
  65.1 1.5 collective-permute-start.16
  66.7 5.3 %all-to-all-start = ((bf16[16,80,512]{2,1,0:T(8,128)(2,1)}), bf16[16,80,512]{2,1,0:T(8,128)(2,1)S(1)}, u32[]{:S(2)}, u32[]{:S(2)}) async-start(bf16[16,80,512]{2,1,0:T(8,128)(2,1)} %pack_queries.1), calls=%async_computation | async-start | bytes 2621440 | tf_op jit(solution)/shard_map/all_to_all | solution.py:360
  72.1 1.1 slice.6
  73.2 1.1 slice.7
  74.2 2.0 %collective-permute-start.11 = (bf16[1,512,512]{2,1,0:T(8,128)(2,1)S(1)}, bf16[1,512,512]{2,1,0:T(8,128)(2,1)}, u32[]{:S(2)}, u32[]{:S(2)}) collective-permute-start(bf16[1,512,512]{2,1,0:T(8,128)(2,1)S(1)} %slice.6), channel_id=1, source_target_pairs={{0,32},{8,40},{16,48},{24,56},{32,64},{40,72},{48,80},{56,88},{64,... | collective-permute-start | bytes 1572872 | tf_op jit(solution)/shard_map/ppermute | solution.py:330
  76.2 1.4 collective-permute-start.12
  77.6 13.1 %project.5.refs_6_ = f32[1024,1024]{1,0:T(8,128)} custom-call(s32[6]{0:T(128)S(1)} %stack.115.idx, bf16[1024,8192]{1,0:T(8,128)(2,1)} %bitcast.34, bf16[1024,8192]{1,0:T(8,128)(2,1)} %bitcast.35, bf16[1024,8192]{1,0:T(8,128)(2,1)} %bitcast.36, bf16[1024,8192]{1,0:T(8,128)(2,1)} %bitcast.37, bf16[1024,8192]{1,0:T(8,128)(2,1)} %bitcast.38, ...), custom_call_target="tpu_custom_call" | custom-call | flops 6442450944 | bytes 12582912 | tf_op jit(solution)/shard_map/project/pallas_call | solution.py:90
  90.7 11.0 %collective-permute-done.11.refs_2_ = bf16[1,512,512]{2,1,0:T(8,128)(2,1)} collective-permute-done((bf16[1,512,512]{2,1,0:T(8,128)(2,1)S(1)}, bf16[1,512,512]{2,1,0:T(8,128)(2,1)}, u32[]{:S(2)}, u32[]{:S(2)}) %collective-permute-start.11) | collective-permute-done | bytes 524320 | tf_op jit(solution)/shard_map/ppermute | solution.py:330
  101.7 0.8 collective-permute-start.22
  102.5 0.5 collective-permute-start.18
  103.2 1.6 collective-permute-done.17.refs_4_
  104.7 0.7 collective-permute-done.18.refs_5_
  105.5 8.7 %attend.1 = bf16[16,64,640]{2,1,0:T(8,128)(2,1)} custom-call(s32[10]{0:T(128)S(1)} %pad_add_fusion.1.idx, bf16[1024,8192]{1,0:T(8,128)(2,1)} %bitcast.40, bf16[1024,8192]{1,0:T(8,128)(2,1)} %bitcast.41, bf16[1,512,512]{2,1,0:T(8,128)(2,1)} %collective-permute-done.11.refs_2_, bf16[1,512,512]{2,1,0:T(8,128)(2,1)} %collective-permute-done.12.refs_3_, ...), custom_call_target="tpu_custom_call" | custom-call | tf_op jit(solution)/shard_map/attend/pallas_call | solution.py:209
  114.2 5.3 %all-to-all-start.1 = ((bf16[16,64,640]{2,1,0:T(8,128)(2,1)}), bf16[16,64,640]{2,1,0:T(8,128)(2,1)S(1)}, u32[]{:S(2)}, u32[]{:S(2)}) async-start(bf16[16,64,640]{2,1,0:T(8,128)(2,1)} %attend.1), calls=%async_computation.1 | async-start | bytes 2621440 | tf_op jit(solution)/shard_map/all_to_all | solution.py:378
  119.5 0.4 collective-permute-start.23
  120.4 7.8 %collective-permute-done.22.refs_7_ = bf16[256,2048]{1,0:T(8,128)(2,1)} collective-permute-done((bf16[256,2048]{1,0:T(8,128)(2,1)}, bf16[256,2048]{1,0:T(8,128)(2,1)}, u32[]{:S(2)}, u32[]{:S(2)}) %collective-permute-start.22) | collective-permute-done | bytes 1048608 | tf_op jit(solution)/shard_map/ppermute | solution.py:333
  128.2 12.2 %all-to-all-done.1.parts = bf16[16,64,640]{2,1,0:T(8,128)(2,1)S(1)} async-done(((bf16[16,64,640]{2,1,0:T(8,128)(2,1)}), bf16[16,64,640]{2,1,0:T(8,128)(2,1)S(1)}, u32[]{:S(2)}, u32[]{:S(2)}) %all-to-all-start.1) | async-done | bytes 1310752 | tf_op jit(solution)/shard_map/all_to_all | solution.py:378
  140.4 2.0 %combine.1.refs_0_ = bf16[256,512]{1,0:T(8,128)(2,1)} custom-call(s32[8]{0:T(128)S(1)} %and_select_fusion.1.holder, bf16[16,64,640]{2,1,0:T(8,128)(2,1)S(1)} %all-to-all-done.1.parts), custom_call_target="tpu_custom_call" | custom-call | tf_op jit(solution)/shard_map/combine/pallas_call | solution.py:259
  142.4 0.9 collective-permute-start.19
  143.3 2.4 %collective-permute-start.20 = (bf16[256,512]{1,0:T(8,128)(2,1)}, bf16[256,512]{1,0:T(8,128)(2,1)S(1)}, u32[]{:S(2)}, u32[]{:S(2)}) collective-permute-start(bf16[256,512]{1,0:T(8,128)(2,1)} %combine.1.refs_0_), channel_id=1, source_target_pairs={{0,6},{1,7},{2,0},{3,1},{4,2},{5,3},{6,4},{7,5},{8,14},{9,15},{10,... | collective-permute-start | bytes 786440 | tf_op jit(solution)/shard_map/ppermute | solution.py:333
  145.7 1.5 collective-permute-start.21
  147.3 5.5 %collective-permute-done.19.refs_1_ = bf16[256,512]{1,0:T(8,128)(2,1)S(1)} collective-permute-done((bf16[256,512]{1,0:T(8,128)(2,1)}, bf16[256,512]{1,0:T(8,128)(2,1)S(1)}, u32[]{:S(2)}, u32[]{:S(2)}) %collective-permute-start.19) | collective-permute-done | bytes 262176 | tf_op jit(solution)/shard_map/ppermute | solution.py:333
  152.8 3.9 %collective-permute-done.20.refs_2_ = bf16[256,512]{1,0:T(8,128)(2,1)S(1)} collective-permute-done((bf16[256,512]{1,0:T(8,128)(2,1)}, bf16[256,512]{1,0:T(8,128)(2,1)S(1)}, u32[]{:S(2)}, u32[]{:S(2)}) %collective-permute-start.20) | collective-permute-done | bytes 262176 | tf_op jit(solution)/shard_map/ppermute | solution.py:333
  156.6 0.9 collective-permute-done.21.refs_3_
  157.5 3.7 %mix.3 = bf16[256,1024]{1,0:T(8,128)(2,1)S(1)} custom-call(s32[2]{0:T(128)S(1)} %pad_add_fusion.3.place, bf16[256,512]{1,0:T(8,128)(2,1)} %combine.1.refs_0_, bf16[256,512]{1,0:T(8,128)(2,1)S(1)} %collective-permute-done.19.refs_1_, bf16[256,512]{1,0:T(8,128)(2,1)S(1)} %collective-permute-done.20.refs_2_, ...), custom_call_target="tpu_custom_call" | custom-call | flops 1073741824 | bytes 4194304 | tf_op jit(solution)/shard_map/mix/pallas_call | solution.py:287
  161.2 0.8 collective-permute-start.27
  162.1 3.7 %mix.2 = f32[256,1024]{1,0:T(8,128)S(1)} custom-call(s32[2]{0:T(128)S(1)} %pad_add_fusion.place, bf16[256,512]{1,0:T(8,128)(2,1)} %combine.1.refs_0_, bf16[256,512]{1,0:T(8,128)(2,1)S(1)} %collective-permute-done.19.refs_1_, bf16[256,512]{1,0:T(8,128)(2,1)S(1)} %collective-permute-done.20.refs_2_, bf16[256,512]{1,0:T(8,128)(2,1)S(1)} %collective-permute-done.21.refs_3_, ...), custom_call_target="tpu_custom_call" | custom-call | flops 1073741824 | bytes 4194304 | tf_op jit(solution)/shard_map/mix/pallas_call | solution.py:287
  165.8 8.0 %collective-permute-done.27 = bf16[256,1024]{1,0:T(8,128)(2,1)S(1)} collective-permute-done((bf16[256,1024]{1,0:T(8,128)(2,1)S(1)}, bf16[256,1024]{1,0:T(8,128)(2,1)S(1)}, u32[]{:S(2)}, u32[]{:S(2)}) %collective-permute-start.27) | collective-permute-done | bytes 524320 | tf_op jit(solution)/shard_map/ppermute | solution.py:385
  173.8 1.0 add_convert_fusion
  (50 shorter events, 1.6 us)
Async XLA Ops:
  0.0 13.3 %collective-permute-start.3 = (bf16[2,512,512]{2,1,0:T(8,128)(2,1)}, bf16[2,512,512]{2,1,0:T(8,128)(2,1)}, u32[]{:S(2)}, u32[]{:S(2)}) collective-permute-start(bf16[2,512,512]{2,1,0:T(8,128)(2,1)} %refs_2_.2), channel_id=1, source_target_pairs={{0,8},{8,0},{16,24},{24,16},{32,40},{40,32},{48,56},{56,48},{64,72... | collective-permute-start | bytes 3145736 | tf_op jit(solution)/shard_map/ppermute | solution.py:330
  0.0 28.2 %collective-permute-start = (bf16[2,512,512]{2,1,0:T(8,128)(2,1)}, bf16[2,512,512]{2,1,0:T(8,128)(2,1)S(1)}, u32[]{:S(2)}, u32[]{:S(2)}) collective-permute-start(bf16[2,512,512]{2,1,0:T(8,128)(2,1)} %refs_2_.2), channel_id=1, source_target_pairs={{0,32},{8,40},{16,48},{24,56},{32,64},{40,72},{48,80},{56,88},{64,... | collective-permute-start | bytes 3145736 | tf_op jit(solution)/shard_map/ppermute | solution.py:330
  2.0 26.2 %collective-permute-start.1 = (bf16[2,512,512]{2,1,0:T(8,128)(2,1)}, bf16[2,512,512]{2,1,0:T(8,128)(2,1)S(1)}, u32[]{:S(2)}, u32[]{:S(2)}) collective-permute-start(bf16[2,512,512]{2,1,0:T(8,128)(2,1)} %refs_2_.2), channel_id=1, source_target_pairs={{0,96},{8,104},{16,112},{24,120},{32,0},{40,8},{48,16},{56,24},{64... | collective-permute-start | bytes 3145736 | tf_op jit(solution)/shard_map/ppermute | solution.py:330
  4.2 27.1 %collective-permute-start.2 = (bf16[2,512,512]{2,1,0:T(8,128)(2,1)}, bf16[2,512,512]{2,1,0:T(8,128)(2,1)}, u32[]{:S(2)}, u32[]{:S(2)}) collective-permute-start(bf16[2,512,512]{2,1,0:T(8,128)(2,1)} %refs_2_.2), channel_id=1, source_target_pairs={{0,16},{8,24},{16,0},{24,8},{32,48},{40,56},{48,32},{56,40},{64,80... | collective-permute-start | bytes 3145736 | tf_op jit(solution)/shard_map/ppermute | solution.py:330
  7.5 5.8 %copy-start.2 = (bf16[2,512,512]{2,1,0:T(8,128)(2,1)S(1)}, bf16[2,512,512]{2,1,0:T(8,128)(2,1)}, u32[]{:S(2)}) copy-start(bf16[2,512,512]{2,1,0:T(8,128)(2,1)} %refs_2_.2) | copy-start | bytes 3145732
  12.2 1.0 copy-start.4
  13.3 19.5 %copy-start.6 = (s32[128]{0:T(128)S(1)}, s32[128]{0:T(128)}, u32[]{:S(2)}) copy-start(s32[128]{0:T(128)} %param.11) | copy-start | bytes 1540
  13.3 26.5 %copy-start.5 = (s32[1,4,2,128]{3,2,1,0:T(2,128)S(1)}, s32[1,4,2,128]{3,2,1,0:T(2,128)}, u32[]{:S(2)}) copy-start(s32[1,4,2,128]{3,2,1,0:T(2,128)} %param.10) | copy-start | bytes 12292
  31.3 3.9 %collective-permute-start.7 = (bf16[2,512,512]{2,1,0:T(8,128)(2,1)S(1)}, bf16[2,512,512]{2,1,0:T(8,128)(2,1)}, u32[]{:S(2)}, u32[]{:S(2)}) collective-permute-start(bf16[2,512,512]{2,1,0:T(8,128)(2,1)S(1)} %collective-permute-done.refs_6_), channel_id=1, source_target_pairs={{0,8},{8,0},{16,24},{24,16},{32,40},{40,32},{48,56},{56,48},{64,72... | collective-permute-start | bytes 3145736 | tf_op jit(solution)/shard_map/ppermute | solution.py:330
  31.3 1.0 copy-start
  32.2 6.1 %collective-permute-start.8 = (bf16[2,512,512]{2,1,0:T(8,128)(2,1)S(1)}, bf16[2,512,512]{2,1,0:T(8,128)(2,1)}, u32[]{:S(2)}, u32[]{:S(2)}) collective-permute-start(bf16[2,512,512]{2,1,0:T(8,128)(2,1)S(1)} %collective-permute-done.1.refs_8_), channel_id=1, source_target_pairs={{0,8},{8,0},{16,24},{24,16},{32,40},{40,32},{48,56},{56,48},{64,72... | collective-permute-start | bytes 3145736 | tf_op jit(solution)/shard_map/ppermute | solution.py:330
  32.7 7.1 %collective-permute-start.9 = (bf16[2,512,512]{2,1,0:T(8,128)(2,1)}, bf16[2,512,512]{2,1,0:T(8,128)(2,1)}, u32[]{:S(2)}, u32[]{:S(2)}) collective-permute-start(bf16[2,512,512]{2,1,0:T(8,128)(2,1)} %collective-permute-done.2.refs_10_), channel_id=1, source_target_pairs={{0,8},{8,0},{16,24},{24,16},{32,40},{40,32},{48,56},{56,48},{64,72... | collective-permute-start | bytes 3145736 | tf_op jit(solution)/shard_map/ppermute | solution.py:330
  33.0 31.4 %collective-permute-start.4 = (bf16[2,512,512]{2,1,0:T(8,128)(2,1)S(1)}, bf16[2,512,512]{2,1,0:T(8,128)(2,1)}, u32[]{:S(2)}, u32[]{:S(2)}) collective-permute-start(bf16[2,512,512]{2,1,0:T(8,128)(2,1)S(1)} %collective-permute-done.1.refs_8_), channel_id=1, source_target_pairs={{0,96},{8,104},{16,112},{24,120},{32,0},{40,8},{48,16},{56,24},{64... | collective-permute-start | bytes 3145736 | tf_op jit(solution)/shard_map/ppermute | solution.py:330
  34.8 29.6 %collective-permute-start.5 = (bf16[2,512,512]{2,1,0:T(8,128)(2,1)}, bf16[2,512,512]{2,1,0:T(8,128)(2,1)}, u32[]{:S(2)}, u32[]{:S(2)}) collective-permute-start(bf16[2,512,512]{2,1,0:T(8,128)(2,1)} %collective-permute-done.2.refs_10_), channel_id=1, source_target_pairs={{0,32},{8,40},{16,48},{24,56},{32,64},{40,72},{48,80},{56,88},{64,... | collective-permute-start | bytes 3145736 | tf_op jit(solution)/shard_map/ppermute | solution.py:330
  35.1 29.3 %collective-permute-start.6 = (bf16[2,512,512]{2,1,0:T(8,128)(2,1)S(1)}, bf16[2,512,512]{2,1,0:T(8,128)(2,1)}, u32[]{:S(2)}, u32[]{:S(2)}) collective-permute-start(bf16[2,512,512]{2,1,0:T(8,128)(2,1)S(1)} %collective-permute-done.1.refs_8_), channel_id=1, source_target_pairs={{0,16},{8,24},{16,0},{24,8},{32,48},{40,56},{48,32},{56,40},{64,80... | collective-permute-start | bytes 3145736 | tf_op jit(solution)/shard_map/ppermute | solution.py:330
  38.3 26.2 %collective-permute-start.10 = (bf16[256,2048]{1,0:T(8,128)(2,1)}, bf16[256,2048]{1,0:T(8,128)(2,1)S(1)}, u32[]{:S(2)}, u32[]{:S(2)}) collective-permute-start(bf16[256,2048]{1,0:T(8,128)(2,1)} %copy-done.4), channel_id=1, source_target_pairs={{0,2},{1,3},{2,4},{3,5},{4,6},{5,7},{6,0},{7,1},{8,10},{9,11},{10,... | collective-permute-start | bytes 3145736 | tf_op jit(solution)/shard_map/ppermute | solution.py:333
  39.8 1.2 copy-start.1
  41.0 12.4 %copy-start.3 = (bf16[256,512]{1,0:T(8,128)(2,1)S(1)}, bf16[256,512]{1,0:T(8,128)(2,1)}, u32[]{:S(2)}) copy-start(bf16[256,512]{1,0:T(8,128)(2,1)} %query.1) | copy-start | bytes 786436
  64.5 11.7 %collective-permute-start.13 = (bf16[2,512,512]{2,1,0:T(8,128)(2,1)}, bf16[2,512,512]{2,1,0:T(8,128)(2,1)}, u32[]{:S(2)}, u32[]{:S(2)}) collective-permute-start(bf16[2,512,512]{2,1,0:T(8,128)(2,1)} %collective-permute-done.4.refs_6_), channel_id=1, source_target_pairs={{0,8},{8,0},{16,24},{24,16},{32,40},{40,32},{48,56},{56,48},{64,72... | collective-permute-start | bytes 3145736 | tf_op jit(solution)/shard_map/ppermute | solution.py:330
  64.5 13.0 %collective-permute-start.14 = (bf16[2,512,512]{2,1,0:T(8,128)(2,1)}, bf16[2,512,512]{2,1,0:T(8,128)(2,1)}, u32[]{:S(2)}, u32[]{:S(2)}) collective-permute-start(bf16[2,512,512]{2,1,0:T(8,128)(2,1)} %collective-permute-done.5.refs_8_), channel_id=1, source_target_pairs={{0,8},{8,0},{16,24},{24,16},{32,40},{40,32},{48,56},{56,48},{64,72... | collective-permute-start | bytes 3145736 | tf_op jit(solution)/shard_map/ppermute | solution.py:330
  65.0 12.5 %collective-permute-start.15 = (bf16[2,512,512]{2,1,0:T(8,128)(2,1)}, bf16[2,512,512]{2,1,0:T(8,128)(2,1)}, u32[]{:S(2)}, u32[]{:S(2)}) collective-permute-start(bf16[2,512,512]{2,1,0:T(8,128)(2,1)} %collective-permute-done.6.refs_10_), channel_id=1, source_target_pairs={{0,8},{8,0},{16,24},{24,16},{32,40},{40,32},{48,56},{56,48},{64,72... | collective-permute-start | bytes 3145736 | tf_op jit(solution)/shard_map/ppermute | solution.py:330
  65.1 36.6 %collective-permute-start.16 = (bf16[256,2048]{1,0:T(8,128)(2,1)}, bf16[256,2048]{1,0:T(8,128)(2,1)}, u32[]{:S(2)}, u32[]{:S(2)}) collective-permute-start(bf16[256,2048]{1,0:T(8,128)(2,1)} %get-tuple-element.40), channel_id=1, source_target_pairs={{0,6},{1,7},{2,0},{3,1},{4,2},{5,3},{6,4},{7,5},{8,14},{9,15},{10,... | collective-permute-start | bytes 3145736 | tf_op jit(solution)/shard_map/ppermute | solution.py:333
  66.7 36.5 %all-to-all-start = ((bf16[16,80,512]{2,1,0:T(8,128)(2,1)}), bf16[16,80,512]{2,1,0:T(8,128)(2,1)S(1)}, u32[]{:S(2)}, u32[]{:S(2)}) async-start(bf16[16,80,512]{2,1,0:T(8,128)(2,1)} %pack_queries.1), calls=%async_computation | async-start | bytes 2621440 | tf_op jit(solution)/shard_map/all_to_all | solution.py:360
  74.2 27.4 %collective-permute-start.11 = (bf16[1,512,512]{2,1,0:T(8,128)(2,1)S(1)}, bf16[1,512,512]{2,1,0:T(8,128)(2,1)}, u32[]{:S(2)}, u32[]{:S(2)}) collective-permute-start(bf16[1,512,512]{2,1,0:T(8,128)(2,1)S(1)} %slice.6), channel_id=1, source_target_pairs={{0,32},{8,40},{16,48},{24,56},{32,64},{40,72},{48,80},{56,88},{64,... | collective-permute-start | bytes 1572872 | tf_op jit(solution)/shard_map/ppermute | solution.py:330
  76.2 25.5 %collective-permute-start.12 = (bf16[1,512,512]{2,1,0:T(8,128)(2,1)S(1)}, bf16[1,512,512]{2,1,0:T(8,128)(2,1)}, u32[]{:S(2)}, u32[]{:S(2)}) collective-permute-start(bf16[1,512,512]{2,1,0:T(8,128)(2,1)S(1)} %slice.7), channel_id=1, source_target_pairs={{0,96},{8,104},{16,112},{24,120},{32,0},{40,8},{48,16},{56,24},{64... | collective-permute-start | bytes 1572872 | tf_op jit(solution)/shard_map/ppermute | solution.py:330
  101.7 26.5 %collective-permute-start.22 = (bf16[256,2048]{1,0:T(8,128)(2,1)}, bf16[256,2048]{1,0:T(8,128)(2,1)}, u32[]{:S(2)}, u32[]{:S(2)}) collective-permute-start(bf16[256,2048]{1,0:T(8,128)(2,1)} %get-tuple-element.48), channel_id=1, source_target_pairs={{0,4},{1,5},{2,6},{3,7},{4,0},{5,1},{6,2},{7,3},{8,12},{9,13},{10,... | collective-permute-start | bytes 3145736 | tf_op jit(solution)/shard_map/ppermute | solution.py:333
  102.5 2.3 %collective-permute-start.17 = (bf16[1,512,512]{2,1,0:T(8,128)(2,1)}, bf16[1,512,512]{2,1,0:T(8,128)(2,1)}, u32[]{:S(2)}, u32[]{:S(2)}) collective-permute-start(bf16[1,512,512]{2,1,0:T(8,128)(2,1)} %collective-permute-done.11.refs_2_), channel_id=1, source_target_pairs={{0,8},{8,0},{16,24},{24,16},{32,40},{40,32},{48,56},{56,48},{64,72... | collective-permute-start | bytes 1572872 | tf_op jit(solution)/shard_map/ppermute | solution.py:330
  102.5 3.0 %collective-permute-start.18 = (bf16[1,512,512]{2,1,0:T(8,128)(2,1)}, bf16[1,512,512]{2,1,0:T(8,128)(2,1)}, u32[]{:S(2)}, u32[]{:S(2)}) collective-permute-start(bf16[1,512,512]{2,1,0:T(8,128)(2,1)} %collective-permute-done.12.refs_3_), channel_id=1, source_target_pairs={{0,8},{8,0},{16,24},{24,16},{32,40},{40,32},{48,56},{56,48},{64,72... | collective-permute-start | bytes 1572872 | tf_op jit(solution)/shard_map/ppermute | solution.py:330
  114.2 26.2 %all-to-all-start.1 = ((bf16[16,64,640]{2,1,0:T(8,128)(2,1)}), bf16[16,64,640]{2,1,0:T(8,128)(2,1)S(1)}, u32[]{:S(2)}, u32[]{:S(2)}) async-start(bf16[16,64,640]{2,1,0:T(8,128)(2,1)} %attend.1), calls=%async_computation.1 | async-start | bytes 2621440 | tf_op jit(solution)/shard_map/all_to_all | solution.py:378
  119.5 23.8 %collective-permute-start.23 = (bf16[256,2048]{1,0:T(8,128)(2,1)S(1)}, bf16[256,2048]{1,0:T(8,128)(2,1)}, u32[]{:S(2)}, u32[]{:S(2)}) collective-permute-start(bf16[256,2048]{1,0:T(8,128)(2,1)S(1)} %get-tuple-element.45.refs_4_), channel_id=1, source_target_pairs={{0,8},{8,0},{16,24},{24,16},{32,40},{40,32},{48,56},{56,48},{64,72... | collective-permute-start | bytes 3145736 | tf_op jit(solution)/shard_map/ppermute | solution.py:330
  119.9 25.7 %collective-permute-start.24 = (bf16[256,2048]{1,0:T(8,128)(2,1)S(1)}, bf16[256,2048]{1,0:T(8,128)(2,1)}, u32[]{:S(2)}, u32[]{:S(2)}) collective-permute-start(bf16[256,2048]{1,0:T(8,128)(2,1)S(1)} %collective-permute-done.10.refs_5_), channel_id=1, source_target_pairs={{0,8},{8,0},{16,24},{24,16},{32,40},{40,32},{48,56},{56,48},{64,72... | collective-permute-start | bytes 3145736 | tf_op jit(solution)/shard_map/ppermute | solution.py:330
  120.2 27.1 %collective-permute-start.25 = (bf16[256,2048]{1,0:T(8,128)(2,1)}, bf16[256,2048]{1,0:T(8,128)(2,1)}, u32[]{:S(2)}, u32[]{:S(2)}) collective-permute-start(bf16[256,2048]{1,0:T(8,128)(2,1)} %collective-permute-done.16.refs_6_), channel_id=1, source_target_pairs={{0,8},{8,0},{16,24},{24,16},{32,40},{40,32},{48,56},{56,48},{64,72... | collective-permute-start | bytes 3145736 | tf_op jit(solution)/shard_map/ppermute | solution.py:330
  128.2 29.3 %collective-permute-start.26 = (bf16[256,2048]{1,0:T(8,128)(2,1)}, bf16[256,2048]{1,0:T(8,128)(2,1)}, u32[]{:S(2)}, u32[]{:S(2)}) collective-permute-start(bf16[256,2048]{1,0:T(8,128)(2,1)} %collective-permute-done.22.refs_7_), channel_id=1, source_target_pairs={{0,8},{8,0},{16,24},{24,16},{32,40},{40,32},{48,56},{56,48},{64,72... | collective-permute-start | bytes 3145736 | tf_op jit(solution)/shard_map/ppermute | solution.py:330
  142.4 10.4 %collective-permute-start.19 = (bf16[256,512]{1,0:T(8,128)(2,1)}, bf16[256,512]{1,0:T(8,128)(2,1)S(1)}, u32[]{:S(2)}, u32[]{:S(2)}) collective-permute-start(bf16[256,512]{1,0:T(8,128)(2,1)} %combine.1.refs_0_), channel_id=1, source_target_pairs={{0,2},{1,3},{2,4},{3,5},{4,6},{5,7},{6,0},{7,1},{8,10},{9,11},{10,... | collective-permute-start | bytes 786440 | tf_op jit(solution)/shard_map/ppermute | solution.py:333
  143.3 13.3 %collective-permute-start.20 = (bf16[256,512]{1,0:T(8,128)(2,1)}, bf16[256,512]{1,0:T(8,128)(2,1)S(1)}, u32[]{:S(2)}, u32[]{:S(2)}) collective-permute-start(bf16[256,512]{1,0:T(8,128)(2,1)} %combine.1.refs_0_), channel_id=1, source_target_pairs={{0,6},{1,7},{2,0},{3,1},{4,2},{5,3},{6,4},{7,5},{8,14},{9,15},{10,... | collective-permute-start | bytes 786440 | tf_op jit(solution)/shard_map/ppermute | solution.py:333
  145.7 11.9 %collective-permute-start.21 = (bf16[256,512]{1,0:T(8,128)(2,1)}, bf16[256,512]{1,0:T(8,128)(2,1)S(1)}, u32[]{:S(2)}, u32[]{:S(2)}) collective-permute-start(bf16[256,512]{1,0:T(8,128)(2,1)} %combine.1.refs_0_), channel_id=1, source_target_pairs={{0,4},{1,5},{2,6},{3,7},{4,0},{5,1},{6,2},{7,3},{8,12},{9,13},{10,... | collective-permute-start | bytes 786440 | tf_op jit(solution)/shard_map/ppermute | solution.py:333
  161.2 12.6 %collective-permute-start.27 = (bf16[256,1024]{1,0:T(8,128)(2,1)S(1)}, bf16[256,1024]{1,0:T(8,128)(2,1)S(1)}, u32[]{:S(2)}, u32[]{:S(2)}) collective-permute-start(bf16[256,1024]{1,0:T(8,128)(2,1)S(1)} %mix.3), channel_id=1, source_target_pairs={{0,1},{1,0},{2,3},{3,2},{4,5},{5,4},{6,7},{7,6},{8,9},{9,8},{10,11... | collective-permute-start | bytes 1572872 | tf_op jit(solution)/shard_map/ppermute | solution.py:385

commit v4 on v3

--- a/solution.py
+++ b/solution.py
@@ -137,10 +137,14 @@
 def pack_kernel(holder, query, valid, out):
     rows = query.shape[0]
     shifted = pltpu.roll(query[...].astype(F32), rows - (M - 1), 0).astype(BF)
+    heads = query.shape[1] // HD
     for j in range(valid.shape[0]):
         u = j // 2
-        out[holder[j], :M, :] = shifted[u * M : (u + 1) * M]
-        out[holder[j], M:, :] = jnp.tile(valid[j : j + 1, :], (16, query.shape[1] // HD)).astype(BF)
+        for h in range(heads):
+            out[holder[j], h * M : (h + 1) * M, :] = shifted[
+                u * M : (u + 1) * M, h * HD : (h + 1) * HD
+            ]
+        out[holder[j], heads * M :, :] = jnp.tile(valid[j : j + 1, :], (16, 1)).astype(BF)
 
 
 def pack_queries(query, valid, holder, groups):
@@ -148,7 +152,7 @@
         pack_kernel,
         in_specs=[pl.BlockSpec(memory_space=pltpu.SMEM)] + vmem_specs(2),
         out_specs=pl.BlockSpec(memory_space=pltpu.VMEM),
-        out_shape=jax.ShapeDtypeStruct((groups, M + 16, query.shape[1]), BF),
+        out_shape=jax.ShapeDtypeStruct((groups, query.shape[1] // HD * M + 16, HD), BF),
         compiler_params=pltpu.CompilerParams(vmem_limit_bytes=VMEM_LIMIT),
         name="pack_queries",
     )(holder, query, valid)
@@ -159,7 +163,7 @@
     rows, weights = refs[:blocks], refs[blocks : blocks + sum(sizes)]
     total, query, out, keys_values = refs[-4:]
     add_terms(sizes, rows, weights, total, keys_values)
-    heads = query.shape[2] // HD
+    heads = keys_values.shape[1] // (2 * HD)
     span = keys_values.shape[0] // ATTEND_SLOTS
     lane = lax.broadcasted_iota(jnp.int32, (M, HD), 1)
     pairs = [(i, h) for i in range(ATTEND_SLOTS) for h in range(heads)]
@@ -168,12 +172,12 @@
     for i, h in pairs:
         cols = slice(h * HD, (h + 1) * HD)
         scores[i, h] = lax.dot_general(
-            query[places[i], :M, cols],
+            query[places[i], h * M : (h + 1) * M, :],
             keys_values[i * span : (i + 1) * span, cols],
             (((1,), (1,)), ((), ())),
             preferred_element_type=F32,
         )
-    valid = [query[place, M : M + 1, :span].astype(F32) > 0.5 for place in places]
+    valid = [query[place, heads * M : heads * M + 1, :span].astype(F32) > 0.5 for place in places]
     shares, levels = {}, {}
     for i, h in pairs:
         scaled = jnp.where(valid[i], scores[i, h] * (1.0 / math.sqrt(HD)), -jnp.inf)
@@ -183,7 +187,7 @@
         shares[i, h] = (raised / norm).astype(BF)
         levels[i, h] = highest + jnp.log(norm)
     for i, h in pairs:
-        out[places[i], :, h * HD : (h + 1) * HD] = jnp.dot(
+        out[places[i], h * M : (h + 1) * M, :] = jnp.dot(
             shares[i, h],
             keys_values[i * span : (i + 1) * span, (heads + h) * HD : (heads + h + 1) * HD],
             preferred_element_type=F32,
@@ -194,14 +198,14 @@
             first = levels[i, h].astype(BF).astype(F32)
             second = (levels[i, h] - first).astype(BF).astype(F32)
             third = levels[i, h] - first - second
-            stats = jnp.where(lane == 3 * h, first, stats)
-            stats = jnp.where(lane == 3 * h + 1, second, stats)
-            stats = jnp.where(lane == 3 * h + 2, third, stats)
-        out[places[i], :, heads * HD :] = stats.astype(BF)
+            stats = jnp.where(lane == h, first, stats)
+            stats = jnp.where(lane == heads + h, second, stats)
+            stats = jnp.where(lane == 2 * heads + h, third, stats)
+        square = jnp.concatenate([stats, jnp.zeros((HD - M, HD), F32)], axis=0)
+        out[places[i], heads * M :, :] = square.T[:16].astype(BF)
 
 
 def attend(encoded, pieces, total, owner, query_blocks):
-    groups, query_rows, columns = query_blocks.shape
     rows = encoded.shape[0]
     tile = rows // owner.shape[0] * ATTEND_SLOTS
     in_specs, operands = project_operands(encoded, pieces, tile)
@@ -213,13 +217,13 @@
             grid=(rows // tile,),
             in_specs=in_specs
             + [
-                pl.BlockSpec((tile, 2 * columns), lambda m, i: (m, 0)),
-                pl.BlockSpec((groups, query_rows, columns), lambda m, i: (0, 0, 0)),
+                pl.BlockSpec((tile, total.shape[1]), lambda m, i: (m, 0)),
+                pl.BlockSpec(query_blocks.shape, lambda m, i: (0, 0, 0)),
             ],
-            out_specs=pl.BlockSpec((groups, M, columns + HD), lambda m, i: (0, 0, 0)),
-            scratch_shapes=[pltpu.VMEM((tile, 2 * columns), BF)],
-        ),
-        out_shape=jax.ShapeDtypeStruct((groups, M, columns + HD), BF),
+            out_specs=pl.BlockSpec(query_blocks.shape, lambda m, i: (0, 0, 0)),
+            scratch_shapes=[pltpu.VMEM((tile, total.shape[1]), BF)],
+        ),
+        out_shape=jax.ShapeDtypeStruct(query_blocks.shape, BF),
         compiler_params=pltpu.CompilerParams(vmem_limit_bytes=VMEM_LIMIT),
         name="attend",
     )(places, *operands, total, query_blocks)
@@ -227,35 +231,36 @@
 
 def combine_kernel(holder, parts, out):
     rows, columns = out.shape
-    heads = columns // HD
+    heads, stretches = columns // HD, rows // M
+    shares = []
+    for u in range(stretches):
+        levels = []
+        for n in range(2):
+            stats = parts[holder[2 * u + n], heads * M :, :].astype(F32)
+            levels.append(stats[:heads] + stats[heads : 2 * heads] + stats[2 * heads : 3 * heads])
+        top = jnp.maximum(levels[0], levels[1])
+        raised = [jnp.exp(level - top) for level in levels]
+        both = raised[0] + raised[1]
+        shares += [raised[0] / both, raised[1] / both]
+    used = 2 * stretches * heads
+    share_columns = jnp.concatenate(shares + [jnp.zeros((HD - used, HD), F32)], axis=0).T
     flat = []
-    for u in range(rows // M):
-        first, second = parts[holder[2 * u]], parts[holder[2 * u + 1]]
-        levels = [part[:, columns:].astype(F32) for part in (first, second)]
+    for u in range(stretches):
         pieces = []
         for h in range(heads):
-            cols = slice(h * HD, (h + 1) * HD)
-            one, two = [
-                level[:, 3 * h : 3 * h + 1]
-                + level[:, 3 * h + 1 : 3 * h + 2]
-                + level[:, 3 * h + 2 : 3 * h + 3]
-                for level in levels
-            ]
-            top = jnp.maximum(one, two)
-            share_one, share_two = jnp.exp(one - top), jnp.exp(two - top)
-            both = share_one + share_two
-            pieces.append(
-                first[:, cols].astype(F32) * (share_one / both)
-                + second[:, cols].astype(F32) * (share_two / both)
-            )
+            terms = []
+            for n in range(2):
+                at = (2 * u + n) * heads + h
+                part = parts[holder[2 * u + n], h * M : (h + 1) * M, :].astype(F32)
+                terms.append(part * share_columns[:M, at : at + 1])
+            pieces.append(terms[0] + terms[1])
         flat.append(jnp.concatenate(pieces, axis=1))
     shifted = pltpu.roll(jnp.concatenate(flat, axis=0), M - 1, 0)
     row = lax.broadcasted_iota(jnp.int32, (rows, columns), 0)
     out[...] = jnp.where(row >= M - 1, shifted, 0.0).astype(BF)
 
 
-def combine(holder, parts, rows):
-    columns = parts.shape[2] - HD
+def combine(holder, parts, rows, columns):
     return pl.pallas_call(
         combine_kernel,
         in_specs=[pl.BlockSpec(memory_space=pltpu.SMEM)] + vmem_specs(1),
@@ -369,14 +374,14 @@
         with_twin(2, 0, far) + with_twin(-1, 1, across_below) + with_twin(1, 1, across_above),
         total,
     )
-    far_keys, far_values, total, mix_next, to_far = lax.optimization_barrier(
-        (far_keys, far_values, total, mix_next, to_far)
+    far_keys, far_values, total, mix_next, to_far, query_blocks = lax.optimization_barrier(
+        (far_keys, far_values, total, mix_next, to_far, query_blocks)
     )
 
     mix_far = across_x(to_far, 2)
     parts = attend(encoded, with_twin(2, 1, far_keys, far_values), total, owner, query_blocks)
     returned = lax.all_to_all(parts, "dp", 0, 0, tiled=True)
-    attended = combine(holder, returned, queries.shape[0])
+    attended = combine(holder, returned, *queries.shape)
 
     near = [attended, across_x(attended, 1), across_x(attended, -1), across_x(attended, 2)]
     mine = [mix_own, mix_last, mix_next, mix_far]

time: 176 us -> 171 us (0.972)
  waiting for transfers between devices: 72.1 us -> 68.8 us
where the time goes in v4:
time: 171 us; the launch traced here: 170 us
  waiting for transfers between devices  68.8 us (40%)
  Pallas kernels  55.2 us (32%)
  starting transfers between devices  38.7 us (23%)
  local copies, waits for them, and re-layouts  5.59 us (3%)
    pallas_call x3, Pallas kernels, project(): pl.pallas_call(functools.partial(project_kernel, [len(w) for _, w in piec...  32.1 us
    ppermute x6, waiting for transfers between devices, across_x(): return lax.ppermute(block, 'tensor', tensor_pairs(step, 0))  27.1 us
    ppermute x21, waiting for transfers between devices, send(): return lax.ppermute(block, 'dp', pairs)  23 us
    ppermute x21, starting transfers between devices, send(): return lax.ppermute(block, 'dp', pairs)  18.6 us
    all_to_all x1, waiting for transfers between devices, body(): returned = lax.all_to_all(parts, 'dp', 0, 0, tiled=True)  10.6 us
    ppermute x6, starting transfers between devices, across_x(): return lax.ppermute(block, 'tensor', tensor_pairs(step, 0))  8.74 us
    pallas_call x1, Pallas kernels, attend(): pl.pallas_call(functools.partial(attend_kernel, [len(w) for _, w in piece...  8.65 us
    ppermute x1, waiting for transfers between devices, body(): arrived = lax.ppermute(theirs, 'tensor', tensor_pairs(0, 1))  8.07 us
  transfers between devices with their start and end apart: 30, of which 12 were waited for; matrix products, arithmetic and copies ran while one was open for 2% of the time, Pallas kernels for 30%

profile of v4, /device:TPU:0, one launch (start us, length us, event | category | flops | bytes accessed | tf_op | source)
XLA Modules:
  0.0 169.9 jit_solution(15733206068000314239)
XLA Ops:
  0.0 2.0 %collective-permute-start = (bf16[2,512,512]{2,1,0:T(8,128)(2,1)}, bf16[2,512,512]{2,1,0:T(8,128)(2,1)S(1)}, u32[]{:S(2)}, u32[]{:S(2)}) collective-permute-start(bf16[2,512,512]{2,1,0:T(8,128)(2,1)} %refs_2_.2), channel_id=1, source_target_pairs={{0,32},{8,40},{16,48},{24,56},{32,64},{40,72},{48,80},{56,88},{64,... | collective-permute-start | bytes 3145736 | tf_op jit(solution)/shard_map/ppermute | solution.py:335
  2.0 2.2 %collective-permute-start.1 = (bf16[2,512,512]{2,1,0:T(8,128)(2,1)}, bf16[2,512,512]{2,1,0:T(8,128)(2,1)S(1)}, u32[]{:S(2)}, u32[]{:S(2)}) collective-permute-start(bf16[2,512,512]{2,1,0:T(8,128)(2,1)} %refs_2_.2), channel_id=1, source_target_pairs={{0,96},{8,104},{16,112},{24,120},{32,0},{40,8},{48,16},{56,24},{64... | collective-permute-start | bytes 3145736 | tf_op jit(solution)/shard_map/ppermute | solution.py:335
  4.2 3.2 %collective-permute-start.2 = (bf16[2,512,512]{2,1,0:T(8,128)(2,1)}, bf16[2,512,512]{2,1,0:T(8,128)(2,1)}, u32[]{:S(2)}, u32[]{:S(2)}) collective-permute-start(bf16[2,512,512]{2,1,0:T(8,128)(2,1)} %refs_2_.2), channel_id=1, source_target_pairs={{0,16},{8,24},{16,0},{24,8},{32,48},{40,56},{48,32},{56,40},{64,80... | collective-permute-start | bytes 3145736 | tf_op jit(solution)/shard_map/ppermute | solution.py:335
  7.5 4.6 %split_rows.1 = (bf16[256,2048]{1,0:T(8,128)(2,1)S(1)}, bf16[256,2048]{1,0:T(8,128)(2,1)S(1)}, bf16[256,2048]{1,0:T(8,128)(2,1)}, bf16[256,2048]{1,0:T(8,128)(2,1)S(1)}) custom-call(s32[5]{0:T(128)S(1)} %stack.101.place, bf16[512,8192]{1,0:T(8,128)(2,1)} %refs_3_.1, bf16[512,8192]{1,0:T(8,128)(2,1)} %refs_3_.1, bf16[512,8192]{1,0:T(8,128)(2,1)} %refs_3_.1, ...), custom_call_target="tpu_custom_call" | custom-call | bytes 65536 | tf_op jit(solution)/shard_map/split_rows/pallas_call | solution.py:117
  12.1 1.0 copy-done.5
  13.1 6.6 %project.3.refs_12_ = f32[1024,1024]{1,0:T(8,128)} custom-call(s32[2]{0:T(128)S(1)} %pad_add_fusion.2.idx, bf16[1024,8192]{1,0:T(8,128)(2,1)} %bitcast.26, bf16[1024,8192]{1,0:T(8,128)(2,1)} %bitcast.27, bf16[2,512,512]{2,1,0:T(8,128)(2,1)S(1)} %copy-done.2, bf16[2,512,512]{2,1,0:T(8,128)(2,1)} %collective-permute-done.3.refs_3_), custom_call_target="tpu_custom_call" | custom-call | flops 2147483648 | bytes 4194304 | tf_op jit(solution)/shard_map/project/pallas_call | solution.py:90
  19.8 8.4 %collective-permute-done.refs_6_ = bf16[2,512,512]{2,1,0:T(8,128)(2,1)S(1)} collective-permute-done((bf16[2,512,512]{2,1,0:T(8,128)(2,1)}, bf16[2,512,512]{2,1,0:T(8,128)(2,1)S(1)}, u32[]{:S(2)}, u32[]{:S(2)}) %collective-permute-start) | collective-permute-done | bytes 1048608 | tf_op jit(solution)/shard_map/ppermute | solution.py:335
  28.2 3.1 %collective-permute-done.2.refs_10_ = bf16[2,512,512]{2,1,0:T(8,128)(2,1)} collective-permute-done((bf16[2,512,512]{2,1,0:T(8,128)(2,1)}, bf16[2,512,512]{2,1,0:T(8,128)(2,1)}, u32[]{:S(2)}, u32[]{:S(2)}) %collective-permute-start.2) | collective-permute-done | bytes 1048608 | tf_op jit(solution)/shard_map/ppermute | solution.py:335
  31.3 1.0 copy-done
  32.2 0.5 collective-permute-start.8
  33.0 1.8 %collective-permute-start.4 = (bf16[2,512,512]{2,1,0:T(8,128)(2,1)S(1)}, bf16[2,512,512]{2,1,0:T(8,128)(2,1)}, u32[]{:S(2)}, u32[]{:S(2)}) collective-permute-start(bf16[2,512,512]{2,1,0:T(8,128)(2,1)S(1)} %collective-permute-done.1.refs_8_), channel_id=1, source_target_pairs={{0,96},{8,104},{16,112},{24,120},{32,0},{40,8},{48,16},{56,24},{64... | collective-permute-start | bytes 3145736 | tf_op jit(solution)/shard_map/ppermute | solution.py:335
  35.1 3.2 %collective-permute-start.6 = (bf16[2,512,512]{2,1,0:T(8,128)(2,1)S(1)}, bf16[2,512,512]{2,1,0:T(8,128)(2,1)}, u32[]{:S(2)}, u32[]{:S(2)}) collective-permute-start(bf16[2,512,512]{2,1,0:T(8,128)(2,1)S(1)} %collective-permute-done.1.refs_8_), channel_id=1, source_target_pairs={{0,16},{8,24},{16,0},{24,8},{32,48},{40,56},{48,32},{56,40},{64,80... | collective-permute-start | bytes 3145736 | tf_op jit(solution)/shard_map/ppermute | solution.py:335
  38.3 1.5 collective-permute-start.10
  39.8 1.2 copy-done.1
  41.0 12.4 %project.4.refs_12_ = f32[1024,1024]{1,0:T(8,128)} custom-call(s32[6]{0:T(128)S(1)} %stack.108.idx, bf16[1024,8192]{1,0:T(8,128)(2,1)} %bitcast.28, bf16[1024,8192]{1,0:T(8,128)(2,1)} %bitcast.29, bf16[1024,8192]{1,0:T(8,128)(2,1)} %bitcast.30, bf16[1024,8192]{1,0:T(8,128)(2,1)} %bitcast.31, bf16[1024,8192]{1,0:T(8,128)(2,1)} %bitcast.32, ...), custom_call_target="tpu_custom_call" | custom-call | flops 6442450944 | bytes 12582912 | tf_op jit(solution)/shard_map/project/pallas_call | solution.py:90
  53.4 1.6 pack_queries.1
  55.1 9.3 %collective-permute-done.10.refs_5_ = bf16[256,2048]{1,0:T(8,128)(2,1)S(1)} collective-permute-done((bf16[256,2048]{1,0:T(8,128)(2,1)}, bf16[256,2048]{1,0:T(8,128)(2,1)S(1)}, u32[]{:S(2)}, u32[]{:S(2)}) %collective-permute-start.10) | collective-permute-done | bytes 1048608 | tf_op jit(solution)/shard_map/ppermute | solution.py:338
  64.5 0.5 collective-permute-start.14
  65.1 1.5 collective-permute-start.16
  66.7 5.3 %all-to-all-start = ((bf16[16,272,128]{2,1,0:T(8,128)(2,1)}), bf16[16,272,128]{2,1,0:T(8,128)(2,1)S(1)}, u32[]{:S(2)}, u32[]{:S(2)}) async-start(bf16[16,272,128]{2,1,0:T(8,128)(2,1)} %pack_queries.1), calls=%async_computation | async-start | bytes 2228224 | tf_op jit(solution)/shard_map/all_to_all | solution.py:365
  72.1 1.1 slice.6
  73.2 1.1 slice.7
  74.2 2.0 %collective-permute-start.11 = (bf16[1,512,512]{2,1,0:T(8,128)(2,1)S(1)}, bf16[1,512,512]{2,1,0:T(8,128)(2,1)}, u32[]{:S(2)}, u32[]{:S(2)}) collective-permute-start(bf16[1,512,512]{2,1,0:T(8,128)(2,1)S(1)} %slice.6), channel_id=1, source_target_pairs={{0,32},{8,40},{16,48},{24,56},{32,64},{40,72},{48,80},{56,88},{64,... | collective-permute-start | bytes 1572872 | tf_op jit(solution)/shard_map/ppermute | solution.py:335
  76.2 1.4 collective-permute-start.12
  77.6 13.1 %project.5.refs_6_ = f32[1024,1024]{1,0:T(8,128)} custom-call(s32[6]{0:T(128)S(1)} %stack.115.idx, bf16[1024,8192]{1,0:T(8,128)(2,1)} %bitcast.34, bf16[1024,8192]{1,0:T(8,128)(2,1)} %bitcast.35, bf16[1024,8192]{1,0:T(8,128)(2,1)} %bitcast.36, bf16[1024,8192]{1,0:T(8,128)(2,1)} %bitcast.37, bf16[1024,8192]{1,0:T(8,128)(2,1)} %bitcast.38, ...), custom_call_target="tpu_custom_call" | custom-call | flops 6442450944 | bytes 12582912 | tf_op jit(solution)/shard_map/project/pallas_call | solution.py:90
  90.7 8.9 %collective-permute-done.11.refs_2_ = bf16[1,512,512]{2,1,0:T(8,128)(2,1)} collective-permute-done((bf16[1,512,512]{2,1,0:T(8,128)(2,1)S(1)}, bf16[1,512,512]{2,1,0:T(8,128)(2,1)}, u32[]{:S(2)}, u32[]{:S(2)}) %collective-permute-start.11) | collective-permute-done | bytes 524320 | tf_op jit(solution)/shard_map/ppermute | solution.py:335
  99.6 0.9 collective-permute-start.22
  100.5 0.5 collective-permute-start.18
  101.1 0.5 collective-permute-start.24
  101.7 1.1 collective-permute-done.17.refs_4_
  102.7 1.5 collective-permute-done.18.refs_5_
  104.2 8.7 %attend.1 = bf16[16,272,128]{2,1,0:T(8,128)(2,1)} custom-call(s32[10]{0:T(128)S(1)} %pad_add_fusion.1.idx, bf16[1024,8192]{1,0:T(8,128)(2,1)} %bitcast.40, bf16[1024,8192]{1,0:T(8,128)(2,1)} %bitcast.41, bf16[1,512,512]{2,1,0:T(8,128)(2,1)} %collective-permute-done.11.refs_2_, bf16[1,512,512]{2,1,0:T(8,128)(2,1)} %collective-permute-done.12.refs_3_, ...), custom_call_target="tpu_custom_call" | custom-call | tf_op jit(solution)/shard_map/attend/pallas_call | solution.py:213
  112.9 5.2 %all-to-all-start.1 = ((bf16[16,272,128]{2,1,0:T(8,128)(2,1)}), bf16[16,272,128]{2,1,0:T(8,128)(2,1)S(1)}, u32[]{:S(2)}, u32[]{:S(2)}) async-start(bf16[16,272,128]{2,1,0:T(8,128)(2,1)} %attend.1), calls=%async_computation.1 | async-start | bytes 2228224 | tf_op jit(solution)/shard_map/all_to_all | solution.py:383
  118.1 0.4 collective-permute-start.25
  118.5 7.7 %collective-permute-done.22.refs_7_ = bf16[256,2048]{1,0:T(8,128)(2,1)} collective-permute-done((bf16[256,2048]{1,0:T(8,128)(2,1)}, bf16[256,2048]{1,0:T(8,128)(2,1)}, u32[]{:S(2)}, u32[]{:S(2)}) %collective-permute-start.22) | collective-permute-done | bytes 1048608 | tf_op jit(solution)/shard_map/ppermute | solution.py:338
  126.2 10.6 %all-to-all-done.1.parts = bf16[16,272,128]{2,1,0:T(8,128)(2,1)S(1)} async-done(((bf16[16,272,128]{2,1,0:T(8,128)(2,1)}), bf16[16,272,128]{2,1,0:T(8,128)(2,1)S(1)}, u32[]{:S(2)}, u32[]{:S(2)}) %all-to-all-start.1) | async-done | bytes 1114144 | tf_op jit(solution)/shard_map/all_to_all | solution.py:383
  136.8 1.0 combine.1.refs_0_
  137.8 1.0 collective-permute-start.19
  138.8 2.4 %collective-permute-start.20 = (bf16[256,512]{1,0:T(8,128)(2,1)S(1)}, bf16[256,512]{1,0:T(8,128)(2,1)S(1)}, u32[]{:S(2)}, u32[]{:S(2)}) collective-permute-start(bf16[256,512]{1,0:T(8,128)(2,1)S(1)} %combine.1.refs_0_), channel_id=1, source_target_pairs={{0,6},{1,7},{2,0},{3,1},{4,2},{5,3},{6,4},{7,5},{8,14},{9,15},{10,... | collective-permute-start | bytes 786440 | tf_op jit(solution)/shard_map/ppermute | solution.py:338
  141.1 1.5 collective-permute-start.21
  142.7 5.3 %collective-permute-done.19.refs_1_ = bf16[256,512]{1,0:T(8,128)(2,1)S(1)} collective-permute-done((bf16[256,512]{1,0:T(8,128)(2,1)S(1)}, bf16[256,512]{1,0:T(8,128)(2,1)S(1)}, u32[]{:S(2)}, u32[]{:S(2)}) %collective-permute-start.19) | collective-permute-done | bytes 262176 | tf_op jit(solution)/shard_map/ppermute | solution.py:338
  148.0 3.8 %collective-permute-done.20.refs_2_ = bf16[256,512]{1,0:T(8,128)(2,1)S(1)} collective-permute-done((bf16[256,512]{1,0:T(8,128)(2,1)S(1)}, bf16[256,512]{1,0:T(8,128)(2,1)S(1)}, u32[]{:S(2)}, u32[]{:S(2)}) %collective-permute-start.20) | collective-permute-done | bytes 262176 | tf_op jit(solution)/shard_map/ppermute | solution.py:338
  151.8 1.0 collective-permute-done.21.refs_3_
  152.8 3.6 %mix.3 = bf16[256,1024]{1,0:T(8,128)(2,1)S(1)} custom-call(s32[2]{0:T(128)S(1)} %pad_add_fusion.3.place, bf16[256,512]{1,0:T(8,128)(2,1)S(1)} %combine.1.refs_0_, bf16[256,512]{1,0:T(8,128)(2,1)S(1)} %collective-permute-done.19.refs_1_, bf16[256,512]{1,0:T(8,128)(2,1)S(1)} %collective-permute-done.20.refs_2_, ...), custom_call_target="tpu_custom_call" | custom-call | flops 1073741824 | bytes 4194304 | tf_op jit(solution)/shard_map/mix/pallas_call | solution.py:292
  156.4 0.8 collective-permute-start.27
  157.3 3.6 %mix.2 = f32[256,1024]{1,0:T(8,128)S(1)} custom-call(s32[2]{0:T(128)S(1)} %pad_add_fusion.place, bf16[256,512]{1,0:T(8,128)(2,1)S(1)} %combine.1.refs_0_, bf16[256,512]{1,0:T(8,128)(2,1)S(1)} %collective-permute-done.19.refs_1_, bf16[256,512]{1,0:T(8,128)(2,1)S(1)} %collective-permute-done.20.refs_2_, bf16[256,512]{1,0:T(8,128)(2,1)S(1)} %collective-permute-done.21.refs_3_, ...), custom_call_target="tpu_custom_call" | custom-call | flops 1073741824 | bytes 4194304 | tf_op jit(solution)/shard_map/mix/pallas_call | solution.py:292
  160.9 8.1 %collective-permute-done.27 = bf16[256,1024]{1,0:T(8,128)(2,1)S(1)} collective-permute-done((bf16[256,1024]{1,0:T(8,128)(2,1)S(1)}, bf16[256,1024]{1,0:T(8,128)(2,1)S(1)}, u32[]{:S(2)}, u32[]{:S(2)}) %collective-permute-start.27) | collective-permute-done | bytes 524320 | tf_op jit(solution)/shard_map/ppermute | solution.py:390
  169.0 1.0 add_convert_fusion
  (52 shorter events, 1.4 us)
Async XLA Ops:
  0.0 13.1 %collective-permute-start.3 = (bf16[2,512,512]{2,1,0:T(8,128)(2,1)}, bf16[2,512,512]{2,1,0:T(8,128)(2,1)}, u32[]{:S(2)}, u32[]{:S(2)}) collective-permute-start(bf16[2,512,512]{2,1,0:T(8,128)(2,1)} %refs_2_.2), channel_id=1, source_target_pairs={{0,8},{8,0},{16,24},{24,16},{32,40},{40,32},{48,56},{56,48},{64,72... | collective-permute-start | bytes 3145736 | tf_op jit(solution)/shard_map/ppermute | solution.py:335
  0.0 28.2 %collective-permute-start = (bf16[2,512,512]{2,1,0:T(8,128)(2,1)}, bf16[2,512,512]{2,1,0:T(8,128)(2,1)S(1)}, u32[]{:S(2)}, u32[]{:S(2)}) collective-permute-start(bf16[2,512,512]{2,1,0:T(8,128)(2,1)} %refs_2_.2), channel_id=1, source_target_pairs={{0,32},{8,40},{16,48},{24,56},{32,64},{40,72},{48,80},{56,88},{64,... | collective-permute-start | bytes 3145736 | tf_op jit(solution)/shard_map/ppermute | solution.py:335
  2.0 26.2 %collective-permute-start.1 = (bf16[2,512,512]{2,1,0:T(8,128)(2,1)}, bf16[2,512,512]{2,1,0:T(8,128)(2,1)S(1)}, u32[]{:S(2)}, u32[]{:S(2)}) collective-permute-start(bf16[2,512,512]{2,1,0:T(8,128)(2,1)} %refs_2_.2), channel_id=1, source_target_pairs={{0,96},{8,104},{16,112},{24,120},{32,0},{40,8},{48,16},{56,24},{64... | collective-permute-start | bytes 3145736 | tf_op jit(solution)/shard_map/ppermute | solution.py:335
  4.2 27.1 %collective-permute-start.2 = (bf16[2,512,512]{2,1,0:T(8,128)(2,1)}, bf16[2,512,512]{2,1,0:T(8,128)(2,1)}, u32[]{:S(2)}, u32[]{:S(2)}) collective-permute-start(bf16[2,512,512]{2,1,0:T(8,128)(2,1)} %refs_2_.2), channel_id=1, source_target_pairs={{0,16},{8,24},{16,0},{24,8},{32,48},{40,56},{48,32},{56,40},{64,80... | collective-permute-start | bytes 3145736 | tf_op jit(solution)/shard_map/ppermute | solution.py:335
  7.5 5.6 %copy-start.2 = (bf16[2,512,512]{2,1,0:T(8,128)(2,1)S(1)}, bf16[2,512,512]{2,1,0:T(8,128)(2,1)}, u32[]{:S(2)}) copy-start(bf16[2,512,512]{2,1,0:T(8,128)(2,1)} %refs_2_.2) | copy-start | bytes 3145732
  12.1 1.0 copy-start.5
  12.1 7.7 %copy-start.4 = (bf16[256,2048]{1,0:T(8,128)(2,1)}, bf16[256,2048]{1,0:T(8,128)(2,1)S(1)}, u32[]{:S(2)}) copy-start(bf16[256,2048]{1,0:T(8,128)(2,1)S(1)} %get-tuple-element.50) | copy-start | bytes 3145732
  13.1 19.7 %copy-start.7 = (s32[128]{0:T(128)S(1)}, s32[128]{0:T(128)}, u32[]{:S(2)}) copy-start(s32[128]{0:T(128)} %param.11) | copy-start | bytes 1540
  13.1 26.7 %copy-start.6 = (s32[1,4,2,128]{3,2,1,0:T(2,128)S(1)}, s32[1,4,2,128]{3,2,1,0:T(2,128)}, u32[]{:S(2)}) copy-start(s32[1,4,2,128]{3,2,1,0:T(2,128)} %param.10) | copy-start | bytes 12292
  31.3 3.8 %collective-permute-start.7 = (bf16[2,512,512]{2,1,0:T(8,128)(2,1)S(1)}, bf16[2,512,512]{2,1,0:T(8,128)(2,1)}, u32[]{:S(2)}, u32[]{:S(2)}) collective-permute-start(bf16[2,512,512]{2,1,0:T(8,128)(2,1)S(1)} %collective-permute-done.refs_6_), channel_id=1, source_target_pairs={{0,8},{8,0},{16,24},{24,16},{32,40},{40,32},{48,56},{56,48},{64,72... | collective-permute-start | bytes 3145736 | tf_op jit(solution)/shard_map/ppermute | solution.py:335
  31.3 1.0 copy-start
  32.2 6.1 %collective-permute-start.8 = (bf16[2,512,512]{2,1,0:T(8,128)(2,1)S(1)}, bf16[2,512,512]{2,1,0:T(8,128)(2,1)}, u32[]{:S(2)}, u32[]{:S(2)}) collective-permute-start(bf16[2,512,512]{2,1,0:T(8,128)(2,1)S(1)} %collective-permute-done.1.refs_8_), channel_id=1, source_target_pairs={{0,8},{8,0},{16,24},{24,16},{32,40},{40,32},{48,56},{56,48},{64,72... | collective-permute-start | bytes 3145736 | tf_op jit(solution)/shard_map/ppermute | solution.py:335
  32.7 7.1 %collective-permute-start.9 = (bf16[2,512,512]{2,1,0:T(8,128)(2,1)}, bf16[2,512,512]{2,1,0:T(8,128)(2,1)}, u32[]{:S(2)}, u32[]{:S(2)}) collective-permute-start(bf16[2,512,512]{2,1,0:T(8,128)(2,1)} %collective-permute-done.2.refs_10_), channel_id=1, source_target_pairs={{0,8},{8,0},{16,24},{24,16},{32,40},{40,32},{48,56},{56,48},{64,72... | collective-permute-start | bytes 3145736 | tf_op jit(solution)/shard_map/ppermute | solution.py:335
  33.0 31.4 %collective-permute-start.4 = (bf16[2,512,512]{2,1,0:T(8,128)(2,1)S(1)}, bf16[2,512,512]{2,1,0:T(8,128)(2,1)}, u32[]{:S(2)}, u32[]{:S(2)}) collective-permute-start(bf16[2,512,512]{2,1,0:T(8,128)(2,1)S(1)} %collective-permute-done.1.refs_8_), channel_id=1, source_target_pairs={{0,96},{8,104},{16,112},{24,120},{32,0},{40,8},{48,16},{56,24},{64... | collective-permute-start | bytes 3145736 | tf_op jit(solution)/shard_map/ppermute | solution.py:335
  34.8 29.6 %collective-permute-start.5 = (bf16[2,512,512]{2,1,0:T(8,128)(2,1)}, bf16[2,512,512]{2,1,0:T(8,128)(2,1)}, u32[]{:S(2)}, u32[]{:S(2)}) collective-permute-start(bf16[2,512,512]{2,1,0:T(8,128)(2,1)} %collective-permute-done.2.refs_10_), channel_id=1, source_target_pairs={{0,32},{8,40},{16,48},{24,56},{32,64},{40,72},{48,80},{56,88},{64,... | collective-permute-start | bytes 3145736 | tf_op jit(solution)/shard_map/ppermute | solution.py:335
  35.1 29.3 %collective-permute-start.6 = (bf16[2,512,512]{2,1,0:T(8,128)(2,1)S(1)}, bf16[2,512,512]{2,1,0:T(8,128)(2,1)}, u32[]{:S(2)}, u32[]{:S(2)}) collective-permute-start(bf16[2,512,512]{2,1,0:T(8,128)(2,1)S(1)} %collective-permute-done.1.refs_8_), channel_id=1, source_target_pairs={{0,16},{8,24},{16,0},{24,8},{32,48},{40,56},{48,32},{56,40},{64,80... | collective-permute-start | bytes 3145736 | tf_op jit(solution)/shard_map/ppermute | solution.py:335
  38.3 26.2 %collective-permute-start.10 = (bf16[256,2048]{1,0:T(8,128)(2,1)}, bf16[256,2048]{1,0:T(8,128)(2,1)S(1)}, u32[]{:S(2)}, u32[]{:S(2)}) collective-permute-start(bf16[256,2048]{1,0:T(8,128)(2,1)} %copy-done.5), channel_id=1, source_target_pairs={{0,2},{1,3},{2,4},{3,5},{4,6},{5,7},{6,0},{7,1},{8,10},{9,11},{10,... | collective-permute-start | bytes 3145736 | tf_op jit(solution)/shard_map/ppermute | solution.py:338
  39.8 1.2 copy-start.1
  41.0 12.4 %copy-start.3 = (bf16[256,512]{1,0:T(8,128)(2,1)S(1)}, bf16[256,512]{1,0:T(8,128)(2,1)}, u32[]{:S(2)}) copy-start(bf16[256,512]{1,0:T(8,128)(2,1)} %query.1) | copy-start | bytes 786436
  64.5 11.7 %collective-permute-start.13 = (bf16[2,512,512]{2,1,0:T(8,128)(2,1)}, bf16[2,512,512]{2,1,0:T(8,128)(2,1)}, u32[]{:S(2)}, u32[]{:S(2)}) collective-permute-start(bf16[2,512,512]{2,1,0:T(8,128)(2,1)} %collective-permute-done.4.refs_6_), channel_id=1, source_target_pairs={{0,8},{8,0},{16,24},{24,16},{32,40},{40,32},{48,56},{56,48},{64,72... | collective-permute-start | bytes 3145736 | tf_op jit(solution)/shard_map/ppermute | solution.py:335
  64.5 13.0 %collective-permute-start.14 = (bf16[2,512,512]{2,1,0:T(8,128)(2,1)}, bf16[2,512,512]{2,1,0:T(8,128)(2,1)}, u32[]{:S(2)}, u32[]{:S(2)}) collective-permute-start(bf16[2,512,512]{2,1,0:T(8,128)(2,1)} %collective-permute-done.5.refs_8_), channel_id=1, source_target_pairs={{0,8},{8,0},{16,24},{24,16},{32,40},{40,32},{48,56},{56,48},{64,72... | collective-permute-start | bytes 3145736 | tf_op jit(solution)/shard_map/ppermute | solution.py:335
  65.0 12.5 %collective-permute-start.15 = (bf16[2,512,512]{2,1,0:T(8,128)(2,1)}, bf16[2,512,512]{2,1,0:T(8,128)(2,1)}, u32[]{:S(2)}, u32[]{:S(2)}) collective-permute-start(bf16[2,512,512]{2,1,0:T(8,128)(2,1)} %collective-permute-done.6.refs_10_), channel_id=1, source_target_pairs={{0,8},{8,0},{16,24},{24,16},{32,40},{40,32},{48,56},{56,48},{64,72... | collective-permute-start | bytes 3145736 | tf_op jit(solution)/shard_map/ppermute | solution.py:335
  65.1 34.4 %collective-permute-start.16 = (bf16[256,2048]{1,0:T(8,128)(2,1)}, bf16[256,2048]{1,0:T(8,128)(2,1)}, u32[]{:S(2)}, u32[]{:S(2)}) collective-permute-start(bf16[256,2048]{1,0:T(8,128)(2,1)} %get-tuple-element.41), channel_id=1, source_target_pairs={{0,6},{1,7},{2,0},{3,1},{4,2},{5,3},{6,4},{7,5},{8,14},{9,15},{10,... | collective-permute-start | bytes 3145736 | tf_op jit(solution)/shard_map/ppermute | solution.py:338
  66.7 32.9 %all-to-all-start = ((bf16[16,272,128]{2,1,0:T(8,128)(2,1)}), bf16[16,272,128]{2,1,0:T(8,128)(2,1)S(1)}, u32[]{:S(2)}, u32[]{:S(2)}) async-start(bf16[16,272,128]{2,1,0:T(8,128)(2,1)} %pack_queries.1), calls=%async_computation | async-start | bytes 2228224 | tf_op jit(solution)/shard_map/all_to_all | solution.py:365
  74.2 25.3 %collective-permute-start.11 = (bf16[1,512,512]{2,1,0:T(8,128)(2,1)S(1)}, bf16[1,512,512]{2,1,0:T(8,128)(2,1)}, u32[]{:S(2)}, u32[]{:S(2)}) collective-permute-start(bf16[1,512,512]{2,1,0:T(8,128)(2,1)S(1)} %slice.6), channel_id=1, source_target_pairs={{0,32},{8,40},{16,48},{24,56},{32,64},{40,72},{48,80},{56,88},{64,... | collective-permute-start | bytes 1572872 | tf_op jit(solution)/shard_map/ppermute | solution.py:335
  76.2 23.4 %collective-permute-start.12 = (bf16[1,512,512]{2,1,0:T(8,128)(2,1)S(1)}, bf16[1,512,512]{2,1,0:T(8,128)(2,1)}, u32[]{:S(2)}, u32[]{:S(2)}) collective-permute-start(bf16[1,512,512]{2,1,0:T(8,128)(2,1)S(1)} %slice.7), channel_id=1, source_target_pairs={{0,96},{8,104},{16,112},{24,120},{32,0},{40,8},{48,16},{56,24},{64... | collective-permute-start | bytes 1572872 | tf_op jit(solution)/shard_map/ppermute | solution.py:335
  99.6 26.6 %collective-permute-start.22 = (bf16[256,2048]{1,0:T(8,128)(2,1)}, bf16[256,2048]{1,0:T(8,128)(2,1)}, u32[]{:S(2)}, u32[]{:S(2)}) collective-permute-start(bf16[256,2048]{1,0:T(8,128)(2,1)} %copy-done.4), channel_id=1, source_target_pairs={{0,4},{1,5},{2,6},{3,7},{4,0},{5,1},{6,2},{7,3},{8,12},{9,13},{10,... | collective-permute-start | bytes 3145736 | tf_op jit(solution)/shard_map/ppermute | solution.py:338
  100.5 2.3 %collective-permute-start.17 = (bf16[1,512,512]{2,1,0:T(8,128)(2,1)}, bf16[1,512,512]{2,1,0:T(8,128)(2,1)}, u32[]{:S(2)}, u32[]{:S(2)}) collective-permute-start(bf16[1,512,512]{2,1,0:T(8,128)(2,1)} %collective-permute-done.11.refs_2_), channel_id=1, source_target_pairs={{0,8},{8,0},{16,24},{24,16},{32,40},{40,32},{48,56},{56,48},{64,72... | collective-permute-start | bytes 1572872 | tf_op jit(solution)/shard_map/ppermute | solution.py:335
  100.5 3.7 %collective-permute-start.18 = (bf16[1,512,512]{2,1,0:T(8,128)(2,1)}, bf16[1,512,512]{2,1,0:T(8,128)(2,1)}, u32[]{:S(2)}, u32[]{:S(2)}) collective-permute-start(bf16[1,512,512]{2,1,0:T(8,128)(2,1)} %collective-permute-done.12.refs_3_), channel_id=1, source_target_pairs={{0,8},{8,0},{16,24},{24,16},{32,40},{40,32},{48,56},{56,48},{64,72... | collective-permute-start | bytes 1572872 | tf_op jit(solution)/shard_map/ppermute | solution.py:335
  101.0 37.8 %collective-permute-start.23 = (bf16[256,2048]{1,0:T(8,128)(2,1)S(1)}, bf16[256,2048]{1,0:T(8,128)(2,1)}, u32[]{:S(2)}, u32[]{:S(2)}) collective-permute-start(bf16[256,2048]{1,0:T(8,128)(2,1)S(1)} %get-tuple-element.47.refs_4_), channel_id=1, source_target_pairs={{0,8},{8,0},{16,24},{24,16},{32,40},{40,32},{48,56},{56,48},{64,72... | collective-permute-start | bytes 3145736 | tf_op jit(solution)/shard_map/ppermute | solution.py:335
  101.1 40.1 %collective-permute-start.24 = (bf16[256,2048]{1,0:T(8,128)(2,1)S(1)}, bf16[256,2048]{1,0:T(8,128)(2,1)}, u32[]{:S(2)}, u32[]{:S(2)}) collective-permute-start(bf16[256,2048]{1,0:T(8,128)(2,1)S(1)} %collective-permute-done.10.refs_5_), channel_id=1, source_target_pairs={{0,8},{8,0},{16,24},{24,16},{32,40},{40,32},{48,56},{56,48},{64,72... | collective-permute-start | bytes 3145736 | tf_op jit(solution)/shard_map/ppermute | solution.py:335
  112.9 23.9 %all-to-all-start.1 = ((bf16[16,272,128]{2,1,0:T(8,128)(2,1)}), bf16[16,272,128]{2,1,0:T(8,128)(2,1)S(1)}, u32[]{:S(2)}, u32[]{:S(2)}) async-start(bf16[16,272,128]{2,1,0:T(8,128)(2,1)} %attend.1), calls=%async_computation.1 | async-start | bytes 2228224 | tf_op jit(solution)/shard_map/all_to_all | solution.py:383
  118.1 24.6 %collective-permute-start.25 = (bf16[256,2048]{1,0:T(8,128)(2,1)}, bf16[256,2048]{1,0:T(8,128)(2,1)}, u32[]{:S(2)}, u32[]{:S(2)}) collective-permute-start(bf16[256,2048]{1,0:T(8,128)(2,1)} %collective-permute-done.16.refs_6_), channel_id=1, source_target_pairs={{0,8},{8,0},{16,24},{24,16},{32,40},{40,32},{48,56},{56,48},{64,72... | collective-permute-start | bytes 3145736 | tf_op jit(solution)/shard_map/ppermute | solution.py:335
  126.2 26.6 %collective-permute-start.26 = (bf16[256,2048]{1,0:T(8,128)(2,1)}, bf16[256,2048]{1,0:T(8,128)(2,1)}, u32[]{:S(2)}, u32[]{:S(2)}) collective-permute-start(bf16[256,2048]{1,0:T(8,128)(2,1)} %collective-permute-done.22.refs_7_), channel_id=1, source_target_pairs={{0,8},{8,0},{16,24},{24,16},{32,40},{40,32},{48,56},{56,48},{64,72... | collective-permute-start | bytes 3145736 | tf_op jit(solution)/shard_map/ppermute | solution.py:335
  137.8 10.2 %collective-permute-start.19 = (bf16[256,512]{1,0:T(8,128)(2,1)S(1)}, bf16[256,512]{1,0:T(8,128)(2,1)S(1)}, u32[]{:S(2)}, u32[]{:S(2)}) collective-permute-start(bf16[256,512]{1,0:T(8,128)(2,1)S(1)} %combine.1.refs_0_), channel_id=1, source_target_pairs={{0,2},{1,3},{2,4},{3,5},{4,6},{5,7},{6,0},{7,1},{8,10},{9,11},{10,... | collective-permute-start | bytes 786440 | tf_op jit(solution)/shard_map/ppermute | solution.py:338
  138.8 13.0 %collective-permute-start.20 = (bf16[256,512]{1,0:T(8,128)(2,1)S(1)}, bf16[256,512]{1,0:T(8,128)(2,1)S(1)}, u32[]{:S(2)}, u32[]{:S(2)}) collective-permute-start(bf16[256,512]{1,0:T(8,128)(2,1)S(1)} %combine.1.refs_0_), channel_id=1, source_target_pairs={{0,6},{1,7},{2,0},{3,1},{4,2},{5,3},{6,4},{7,5},{8,14},{9,15},{10,... | collective-permute-start | bytes 786440 | tf_op jit(solution)/shard_map/ppermute | solution.py:338
  141.1 11.7 %collective-permute-start.21 = (bf16[256,512]{1,0:T(8,128)(2,1)S(1)}, bf16[256,512]{1,0:T(8,128)(2,1)S(1)}, u32[]{:S(2)}, u32[]{:S(2)}) collective-permute-start(bf16[256,512]{1,0:T(8,128)(2,1)S(1)} %combine.1.refs_0_), channel_id=1, source_target_pairs={{0,4},{1,5},{2,6},{3,7},{4,0},{5,1},{6,2},{7,3},{8,12},{9,13},{10,... | collective-permute-start | bytes 786440 | tf_op jit(solution)/shard_map/ppermute | solution.py:338
  156.4 12.6 %collective-permute-start.27 = (bf16[256,1024]{1,0:T(8,128)(2,1)S(1)}, bf16[256,1024]{1,0:T(8,128)(2,1)S(1)}, u32[]{:S(2)}, u32[]{:S(2)}) collective-permute-start(bf16[256,1024]{1,0:T(8,128)(2,1)S(1)} %mix.3), channel_id=1, source_target_pairs={{0,1},{1,0},{2,3},{3,2},{4,5},{5,4},{6,7},{7,6},{8,9},{9,8},{10,11... | collective-permute-start | bytes 1572872 | tf_op jit(solution)/shard_map/ppermute | solution.py:390

commit v5 on v4

--- a/solution.py
+++ b/solution.py
@@ -229,8 +229,8 @@
     )(places, *operands, total, query_blocks)
 
 
-def combine_kernel(holder, parts, out):
-    rows, columns = out.shape
+def combine_kernel(lead, holder, parts, out):
+    rows, columns = out.shape[0] + lead, out.shape[1]
     heads, stretches = columns // HD, rows // M
     shares = []
     for u in range(stretches):
@@ -257,15 +257,15 @@
         flat.append(jnp.concatenate(pieces, axis=1))
     shifted = pltpu.roll(jnp.concatenate(flat, axis=0), M - 1, 0)
     row = lax.broadcasted_iota(jnp.int32, (rows, columns), 0)
-    out[...] = jnp.where(row >= M - 1, shifted, 0.0).astype(BF)
-
-
-def combine(holder, parts, rows, columns):
-    return pl.pallas_call(
-        combine_kernel,
+    out[...] = jnp.where(row >= M - 1, shifted, 0.0)[lead:].astype(BF)
+
+
+def combine(holder, parts, rows, columns, lead):
+    return pl.pallas_call(
+        functools.partial(combine_kernel, lead),
         in_specs=[pl.BlockSpec(memory_space=pltpu.SMEM)] + vmem_specs(1),
         out_specs=pl.BlockSpec(memory_space=pltpu.VMEM),
-        out_shape=jax.ShapeDtypeStruct((rows, columns), BF),
+        out_shape=jax.ShapeDtypeStruct((rows - lead, columns), BF),
         compiler_params=pltpu.CompilerParams(vmem_limit_bytes=VMEM_LIMIT),
         name="combine",
     )(holder, parts)
@@ -381,7 +381,8 @@
     mix_far = across_x(to_far, 2)
     parts = attend(encoded, with_twin(2, 1, far_keys, far_values), total, owner, query_blocks)
     returned = lax.all_to_all(parts, "dp", 0, 0, tiled=True)
-    attended = combine(holder, returned, *queries.shape)
+    lead = (M - 1) // 16 * 16
+    attended = combine(holder, returned, *queries.shape, lead)
 
     near = [attended, across_x(attended, 1), across_x(attended, -1), across_x(attended, 2)]
     mine = [mix_own, mix_last, mix_next, mix_far]
@@ -389,7 +390,8 @@
     theirs = mix(jnp.stack([1 - y_lo, core]), near, mine, other, BF)
     arrived = lax.ppermute(theirs, "tensor", tensor_pairs(0, 1))
     ours = mix(jnp.stack([y_lo, core]), near, mine, other, F32)
-    return (ours + arrived.astype(F32)).astype(BF)
+    mixed = (ours + arrived.astype(F32)).astype(BF)
+    return jnp.concatenate([jnp.zeros((lead, mixed.shape[1]), BF), mixed], axis=0)
 
 
 def solution(mesh):

time: 171 us -> 166 us (0.971)
  waiting for transfers between devices: 68.8 us -> 64.8 us
    ppermute x6, waiting for transfers between devices: 27.1 us -> 25 us  [across_x(): return lax.ppermute(block, 'tensor', tensor_pairs(step, 0))]
    ppermute x1, waiting for transfers between devices: 8.07 us -> 6.18 us  [body(): arrived = lax.ppermute(theirs, 'tensor', tensor_pairs(0, 1))]
  transfers between devices with their start and end apart: 30 -> 30, of which waited for: 12 -> 12; matrix products, arithmetic and copies ran while one was open for 2% -> 2% of each run, Pallas kernels for 30% -> 31%
where the time goes in v5:
time: 166 us
  waiting for transfers between devices  64.8 us (39%)
  Pallas kernels  54.8 us (33%)
  starting transfers between devices  38.7 us (23%)
  local copies, waits for them, and re-layouts  6.45 us (4%)
    pallas_call x3, Pallas kernels, project(): pl.pallas_call(functools.partial(project_kernel, [len(w) for _, w in piec...  32.1 us
    ppermute x6, waiting for transfers between devices, across_x(): return lax.ppermute(block, 'tensor', tensor_pairs(step, 0))  25 us
    ppermute x21, waiting for transfers between devices, send(): return lax.ppermute(block, 'dp', pairs)  23 us
    ppermute x21, starting transfers between devices, send(): return lax.ppermute(block, 'dp', pairs)  18.6 us
    all_to_all x1, waiting for transfers between devices, body(): returned = lax.all_to_all(parts, 'dp', 0, 0, tiled=True)  10.6 us
    ppermute x6, starting transfers between devices, across_x(): return lax.ppermute(block, 'tensor', tensor_pairs(step, 0))  8.75 us
    pallas_call x1, Pallas kernels, attend(): pl.pallas_call(functools.partial(attend_kernel, [len(w) for _, w in piece...  8.65 us
    pallas_call x2, Pallas kernels, mix(): pl.pallas_call(mix_kernel, grid_spec=pltpu.PrefetchScalarGridSpec(num_sca...  6.77 us
  transfers between devices with their start and end apart: 30, of which 12 were waited for; matrix products, arithmetic and copies ran while one was open for 2% of the time, Pallas kernels for 31%

profile of v5, /device:TPU:0, one launch (start us, length us, event | category | flops | bytes accessed | tf_op | source)
XLA Modules:
  0.0 165.5 jit_solution(11769692544708551157)
XLA Ops:
  0.0 2.0 %collective-permute-start = (bf16[2,512,512]{2,1,0:T(8,128)(2,1)}, bf16[2,512,512]{2,1,0:T(8,128)(2,1)S(1)}, u32[]{:S(2)}, u32[]{:S(2)}) collective-permute-start(bf16[2,512,512]{2,1,0:T(8,128)(2,1)} %refs_2_.2), channel_id=1, source_target_pairs={{0,32},{8,40},{16,48},{24,56},{32,64},{40,72},{48,80},{56,88},{64,... | collective-permute-start | bytes 3145736 | tf_op jit(solution)/shard_map/ppermute | solution.py:335
  2.0 2.2 %collective-permute-start.1 = (bf16[2,512,512]{2,1,0:T(8,128)(2,1)}, bf16[2,512,512]{2,1,0:T(8,128)(2,1)S(1)}, u32[]{:S(2)}, u32[]{:S(2)}) collective-permute-start(bf16[2,512,512]{2,1,0:T(8,128)(2,1)} %refs_2_.2), channel_id=1, source_target_pairs={{0,96},{8,104},{16,112},{24,120},{32,0},{40,8},{48,16},{56,24},{64... | collective-permute-start | bytes 3145736 | tf_op jit(solution)/shard_map/ppermute | solution.py:335
  4.2 3.2 %collective-permute-start.2 = (bf16[2,512,512]{2,1,0:T(8,128)(2,1)}, bf16[2,512,512]{2,1,0:T(8,128)(2,1)}, u32[]{:S(2)}, u32[]{:S(2)}) collective-permute-start(bf16[2,512,512]{2,1,0:T(8,128)(2,1)} %refs_2_.2), channel_id=1, source_target_pairs={{0,16},{8,24},{16,0},{24,8},{32,48},{40,56},{48,32},{56,40},{64,80... | collective-permute-start | bytes 3145736 | tf_op jit(solution)/shard_map/ppermute | solution.py:335
  7.5 4.6 %split_rows.1 = (bf16[256,2048]{1,0:T(8,128)(2,1)S(1)}, bf16[256,2048]{1,0:T(8,128)(2,1)S(1)}, bf16[256,2048]{1,0:T(8,128)(2,1)}, bf16[256,2048]{1,0:T(8,128)(2,1)S(1)}) custom-call(s32[5]{0:T(128)S(1)} %stack.101.place, bf16[512,8192]{1,0:T(8,128)(2,1)} %refs_3_.1, bf16[512,8192]{1,0:T(8,128)(2,1)} %refs_3_.1, bf16[512,8192]{1,0:T(8,128)(2,1)} %refs_3_.1, ...), custom_call_target="tpu_custom_call" | custom-call | bytes 65536 | tf_op jit(solution)/shard_map/split_rows/pallas_call | solution.py:117
  12.1 1.0 copy-done.5
  13.1 6.6 %project.3.refs_12_ = f32[1024,1024]{1,0:T(8,128)} custom-call(s32[2]{0:T(128)S(1)} %pad_add_fusion.2.idx, bf16[1024,8192]{1,0:T(8,128)(2,1)} %bitcast.26, bf16[1024,8192]{1,0:T(8,128)(2,1)} %bitcast.27, bf16[2,512,512]{2,1,0:T(8,128)(2,1)S(1)} %copy-done.2, bf16[2,512,512]{2,1,0:T(8,128)(2,1)} %collective-permute-done.3.refs_3_), custom_call_target="tpu_custom_call" | custom-call | flops 2147483648 | bytes 4194304 | tf_op jit(solution)/shard_map/project/pallas_call | solution.py:90
  19.8 8.4 %collective-permute-done.refs_6_ = bf16[2,512,512]{2,1,0:T(8,128)(2,1)S(1)} collective-permute-done((bf16[2,512,512]{2,1,0:T(8,128)(2,1)}, bf16[2,512,512]{2,1,0:T(8,128)(2,1)S(1)}, u32[]{:S(2)}, u32[]{:S(2)}) %collective-permute-start) | collective-permute-done | bytes 1048608 | tf_op jit(solution)/shard_map/ppermute | solution.py:335
  28.2 3.1 %collective-permute-done.2.refs_10_ = bf16[2,512,512]{2,1,0:T(8,128)(2,1)} collective-permute-done((bf16[2,512,512]{2,1,0:T(8,128)(2,1)}, bf16[2,512,512]{2,1,0:T(8,128)(2,1)}, u32[]{:S(2)}, u32[]{:S(2)}) %collective-permute-start.2) | collective-permute-done | bytes 1048608 | tf_op jit(solution)/shard_map/ppermute | solution.py:335
  31.3 1.0 copy-done
  32.2 0.5 collective-permute-start.8
  33.0 1.8 %collective-permute-start.4 = (bf16[2,512,512]{2,1,0:T(8,128)(2,1)S(1)}, bf16[2,512,512]{2,1,0:T(8,128)(2,1)}, u32[]{:S(2)}, u32[]{:S(2)}) collective-permute-start(bf16[2,512,512]{2,1,0:T(8,128)(2,1)S(1)} %collective-permute-done.1.refs_8_), channel_id=1, source_target_pairs={{0,96},{8,104},{16,112},{24,120},{32,0},{40,8},{48,16},{56,24},{64... | collective-permute-start | bytes 3145736 | tf_op jit(solution)/shard_map/ppermute | solution.py:335
  35.1 3.2 %collective-permute-start.6 = (bf16[2,512,512]{2,1,0:T(8,128)(2,1)S(1)}, bf16[2,512,512]{2,1,0:T(8,128)(2,1)}, u32[]{:S(2)}, u32[]{:S(2)}) collective-permute-start(bf16[2,512,512]{2,1,0:T(8,128)(2,1)S(1)} %collective-permute-done.1.refs_8_), channel_id=1, source_target_pairs={{0,16},{8,24},{16,0},{24,8},{32,48},{40,56},{48,32},{56,40},{64,80... | collective-permute-start | bytes 3145736 | tf_op jit(solution)/shard_map/ppermute | solution.py:335
  38.3 1.5 collective-permute-start.10
  39.8 1.2 copy-done.1
  41.0 12.4 %project.4.refs_12_ = f32[1024,1024]{1,0:T(8,128)} custom-call(s32[6]{0:T(128)S(1)} %stack.108.idx, bf16[1024,8192]{1,0:T(8,128)(2,1)} %bitcast.28, bf16[1024,8192]{1,0:T(8,128)(2,1)} %bitcast.29, bf16[1024,8192]{1,0:T(8,128)(2,1)} %bitcast.30, bf16[1024,8192]{1,0:T(8,128)(2,1)} %bitcast.31, bf16[1024,8192]{1,0:T(8,128)(2,1)} %bitcast.32, ...), custom_call_target="tpu_custom_call" | custom-call | flops 6442450944 | bytes 12582912 | tf_op jit(solution)/shard_map/project/pallas_call | solution.py:90
  53.4 1.6 pack_queries.1
  55.1 9.3 %collective-permute-done.10.refs_5_ = bf16[256,2048]{1,0:T(8,128)(2,1)S(1)} collective-permute-done((bf16[256,2048]{1,0:T(8,128)(2,1)}, bf16[256,2048]{1,0:T(8,128)(2,1)S(1)}, u32[]{:S(2)}, u32[]{:S(2)}) %collective-permute-start.10) | collective-permute-done | bytes 1048608 | tf_op jit(solution)/shard_map/ppermute | solution.py:338
  64.5 0.5 collective-permute-start.14
  65.1 1.5 collective-permute-start.16
  66.7 5.3 %all-to-all-start = ((bf16[16,272,128]{2,1,0:T(8,128)(2,1)}), bf16[16,272,128]{2,1,0:T(8,128)(2,1)S(1)}, u32[]{:S(2)}, u32[]{:S(2)}) async-start(bf16[16,272,128]{2,1,0:T(8,128)(2,1)} %pack_queries.1), calls=%async_computation | async-start | bytes 2228224 | tf_op jit(solution)/shard_map/all_to_all | solution.py:365
  72.1 1.1 slice.6
  73.2 1.1 slice.7
  74.2 2.0 %collective-permute-start.11 = (bf16[1,512,512]{2,1,0:T(8,128)(2,1)S(1)}, bf16[1,512,512]{2,1,0:T(8,128)(2,1)}, u32[]{:S(2)}, u32[]{:S(2)}) collective-permute-start(bf16[1,512,512]{2,1,0:T(8,128)(2,1)S(1)} %slice.6), channel_id=1, source_target_pairs={{0,32},{8,40},{16,48},{24,56},{32,64},{40,72},{48,80},{56,88},{64,... | collective-permute-start | bytes 1572872 | tf_op jit(solution)/shard_map/ppermute | solution.py:335
  76.2 1.4 collective-permute-start.12
  77.6 13.1 %project.5.refs_6_ = f32[1024,1024]{1,0:T(8,128)} custom-call(s32[6]{0:T(128)S(1)} %stack.115.idx, bf16[1024,8192]{1,0:T(8,128)(2,1)} %bitcast.34, bf16[1024,8192]{1,0:T(8,128)(2,1)} %bitcast.35, bf16[1024,8192]{1,0:T(8,128)(2,1)} %bitcast.36, bf16[1024,8192]{1,0:T(8,128)(2,1)} %bitcast.37, bf16[1024,8192]{1,0:T(8,128)(2,1)} %bitcast.38, ...), custom_call_target="tpu_custom_call" | custom-call | flops 6442450944 | bytes 12582912 | tf_op jit(solution)/shard_map/project/pallas_call | solution.py:90
  90.7 8.9 %collective-permute-done.11.refs_2_ = bf16[1,512,512]{2,1,0:T(8,128)(2,1)} collective-permute-done((bf16[1,512,512]{2,1,0:T(8,128)(2,1)S(1)}, bf16[1,512,512]{2,1,0:T(8,128)(2,1)}, u32[]{:S(2)}, u32[]{:S(2)}) %collective-permute-start.11) | collective-permute-done | bytes 524320 | tf_op jit(solution)/shard_map/ppermute | solution.py:335
  99.6 0.9 collective-permute-start.22
  100.5 0.5 collective-permute-start.18
  101.1 0.5 collective-permute-start.24
  101.7 1.1 collective-permute-done.17.refs_4_
  102.7 1.5 collective-permute-done.18.refs_5_
  104.2 8.6 %attend.1 = bf16[16,272,128]{2,1,0:T(8,128)(2,1)} custom-call(s32[10]{0:T(128)S(1)} %pad_add_fusion.1.idx, bf16[1024,8192]{1,0:T(8,128)(2,1)} %bitcast.40, bf16[1024,8192]{1,0:T(8,128)(2,1)} %bitcast.41, bf16[1,512,512]{2,1,0:T(8,128)(2,1)} %collective-permute-done.11.refs_2_, bf16[1,512,512]{2,1,0:T(8,128)(2,1)} %collective-permute-done.12.refs_3_, ...), custom_call_target="tpu_custom_call" | custom-call | tf_op jit(solution)/shard_map/attend/pallas_call | solution.py:213
  112.9 5.2 %all-to-all-start.1 = ((bf16[16,272,128]{2,1,0:T(8,128)(2,1)}), bf16[16,272,128]{2,1,0:T(8,128)(2,1)S(1)}, u32[]{:S(2)}, u32[]{:S(2)}) async-start(bf16[16,272,128]{2,1,0:T(8,128)(2,1)} %attend.1), calls=%async_computation.1 | async-start | bytes 2228224 | tf_op jit(solution)/shard_map/all_to_all | solution.py:383
  118.1 0.4 collective-permute-start.25
  118.5 7.7 %collective-permute-done.22.refs_7_ = bf16[256,2048]{1,0:T(8,128)(2,1)} collective-permute-done((bf16[256,2048]{1,0:T(8,128)(2,1)}, bf16[256,2048]{1,0:T(8,128)(2,1)}, u32[]{:S(2)}, u32[]{:S(2)}) %collective-permute-start.22) | collective-permute-done | bytes 1048608 | tf_op jit(solution)/shard_map/ppermute | solution.py:338
  126.2 10.6 %all-to-all-done.1.parts = bf16[16,272,128]{2,1,0:T(8,128)(2,1)S(1)} async-done(((bf16[16,272,128]{2,1,0:T(8,128)(2,1)}), bf16[16,272,128]{2,1,0:T(8,128)(2,1)S(1)}, u32[]{:S(2)}, u32[]{:S(2)}) %all-to-all-start.1) | async-done | bytes 1114144 | tf_op jit(solution)/shard_map/all_to_all | solution.py:383
  136.8 1.0 combine.1.refs_0_
  137.8 1.0 collective-permute-start.19
  138.8 2.4 %collective-permute-start.20 = (bf16[208,512]{1,0:T(8,128)(2,1)S(1)}, bf16[208,512]{1,0:T(8,128)(2,1)S(1)}, u32[]{:S(2)}, u32[]{:S(2)}) collective-permute-start(bf16[208,512]{1,0:T(8,128)(2,1)S(1)} %combine.1.refs_0_), channel_id=1, source_target_pairs={{0,6},{1,7},{2,0},{3,1},{4,2},{5,3},{6,4},{7,5},{8,14},{9,15},{10,... | collective-permute-start | bytes 638984 | tf_op jit(solution)/shard_map/ppermute | solution.py:338
  141.1 1.5 collective-permute-start.21
  142.7 4.2 %collective-permute-done.19.refs_1_ = bf16[208,512]{1,0:T(8,128)(2,1)S(1)} collective-permute-done((bf16[208,512]{1,0:T(8,128)(2,1)S(1)}, bf16[208,512]{1,0:T(8,128)(2,1)S(1)}, u32[]{:S(2)}, u32[]{:S(2)}) %collective-permute-start.19) | collective-permute-done | bytes 213024 | tf_op jit(solution)/shard_map/ppermute | solution.py:338
  147.0 2.7 %collective-permute-done.20.refs_2_ = bf16[208,512]{1,0:T(8,128)(2,1)S(1)} collective-permute-done((bf16[208,512]{1,0:T(8,128)(2,1)S(1)}, bf16[208,512]{1,0:T(8,128)(2,1)S(1)}, u32[]{:S(2)}, u32[]{:S(2)}) %collective-permute-start.20) | collective-permute-done | bytes 213024 | tf_op jit(solution)/shard_map/ppermute | solution.py:338
  149.7 1.0 collective-permute-done.21.refs_3_
  150.7 3.4 %mix.3 = bf16[208,1024]{1,0:T(8,128)(2,1)S(1)} custom-call(s32[2]{0:T(128)S(1)} %pad_add_fusion.3.place, bf16[208,512]{1,0:T(8,128)(2,1)S(1)} %combine.1.refs_0_, bf16[208,512]{1,0:T(8,128)(2,1)S(1)} %collective-permute-done.19.refs_1_, bf16[208,512]{1,0:T(8,128)(2,1)S(1)} %collective-permute-done.20.refs_2_, ...), custom_call_target="tpu_custom_call" | custom-call | flops 872415232 | bytes 4194304 | tf_op jit(solution)/shard_map/mix/pallas_call | solution.py:292
  154.1 0.8 collective-permute-start.27
  155.0 3.4 %mix.2 = f32[208,1024]{1,0:T(8,128)S(1)} custom-call(s32[2]{0:T(128)S(1)} %pad_add_fusion.place, bf16[208,512]{1,0:T(8,128)(2,1)S(1)} %combine.1.refs_0_, bf16[208,512]{1,0:T(8,128)(2,1)S(1)} %collective-permute-done.19.refs_1_, bf16[208,512]{1,0:T(8,128)(2,1)S(1)} %collective-permute-done.20.refs_2_, bf16[208,512]{1,0:T(8,128)(2,1)S(1)} %collective-permute-done.21.refs_3_, ...), custom_call_target="tpu_custom_call" | custom-call | flops 872415232 | bytes 4194304 | tf_op jit(solution)/shard_map/mix/pallas_call | solution.py:292
  158.4 6.2 %collective-permute-done.27 = bf16[208,1024]{1,0:T(8,128)(2,1)S(1)} collective-permute-done((bf16[208,1024]{1,0:T(8,128)(2,1)S(1)}, bf16[208,1024]{1,0:T(8,128)(2,1)S(1)}, u32[]{:S(2)}, u32[]{:S(2)}) %collective-permute-start.27) | collective-permute-done | bytes 426016 | tf_op jit(solution)/shard_map/ppermute | solution.py:391
  164.7 0.9 concatenate.7
  (53 shorter events, 1.5 us)
Async XLA Ops:
  0.0 13.1 %collective-permute-start.3 = (bf16[2,512,512]{2,1,0:T(8,128)(2,1)}, bf16[2,512,512]{2,1,0:T(8,128)(2,1)}, u32[]{:S(2)}, u32[]{:S(2)}) collective-permute-start(bf16[2,512,512]{2,1,0:T(8,128)(2,1)} %refs_2_.2), channel_id=1, source_target_pairs={{0,8},{8,0},{16,24},{24,16},{32,40},{40,32},{48,56},{56,48},{64,72... | collective-permute-start | bytes 3145736 | tf_op jit(solution)/shard_map/ppermute | solution.py:335
  0.0 28.2 %collective-permute-start = (bf16[2,512,512]{2,1,0:T(8,128)(2,1)}, bf16[2,512,512]{2,1,0:T(8,128)(2,1)S(1)}, u32[]{:S(2)}, u32[]{:S(2)}) collective-permute-start(bf16[2,512,512]{2,1,0:T(8,128)(2,1)} %refs_2_.2), channel_id=1, source_target_pairs={{0,32},{8,40},{16,48},{24,56},{32,64},{40,72},{48,80},{56,88},{64,... | collective-permute-start | bytes 3145736 | tf_op jit(solution)/shard_map/ppermute | solution.py:335
  2.0 26.2 %collective-permute-start.1 = (bf16[2,512,512]{2,1,0:T(8,128)(2,1)}, bf16[2,512,512]{2,1,0:T(8,128)(2,1)S(1)}, u32[]{:S(2)}, u32[]{:S(2)}) collective-permute-start(bf16[2,512,512]{2,1,0:T(8,128)(2,1)} %refs_2_.2), channel_id=1, source_target_pairs={{0,96},{8,104},{16,112},{24,120},{32,0},{40,8},{48,16},{56,24},{64... | collective-permute-start | bytes 3145736 | tf_op jit(solution)/shard_map/ppermute | solution.py:335
  4.2 27.1 %collective-permute-start.2 = (bf16[2,512,512]{2,1,0:T(8,128)(2,1)}, bf16[2,512,512]{2,1,0:T(8,128)(2,1)}, u32[]{:S(2)}, u32[]{:S(2)}) collective-permute-start(bf16[2,512,512]{2,1,0:T(8,128)(2,1)} %refs_2_.2), channel_id=1, source_target_pairs={{0,16},{8,24},{16,0},{24,8},{32,48},{40,56},{48,32},{56,40},{64,80... | collective-permute-start | bytes 3145736 | tf_op jit(solution)/shard_map/ppermute | solution.py:335
  7.5 5.6 %copy-start.2 = (bf16[2,512,512]{2,1,0:T(8,128)(2,1)S(1)}, bf16[2,512,512]{2,1,0:T(8,128)(2,1)}, u32[]{:S(2)}) copy-start(bf16[2,512,512]{2,1,0:T(8,128)(2,1)} %refs_2_.2) | copy-start | bytes 3145732
  12.1 1.0 copy-start.5
  12.1 7.7 %copy-start.4 = (bf16[256,2048]{1,0:T(8,128)(2,1)}, bf16[256,2048]{1,0:T(8,128)(2,1)S(1)}, u32[]{:S(2)}) copy-start(bf16[256,2048]{1,0:T(8,128)(2,1)S(1)} %get-tuple-element.50) | copy-start | bytes 3145732
  13.1 19.7 %copy-start.7 = (s32[128]{0:T(128)S(1)}, s32[128]{0:T(128)}, u32[]{:S(2)}) copy-start(s32[128]{0:T(128)} %param.11) | copy-start | bytes 1540
  13.1 26.7 %copy-start.6 = (s32[1,4,2,128]{3,2,1,0:T(2,128)S(1)}, s32[1,4,2,128]{3,2,1,0:T(2,128)}, u32[]{:S(2)}) copy-start(s32[1,4,2,128]{3,2,1,0:T(2,128)} %param.10) | copy-start | bytes 12292
  31.3 3.8 %collective-permute-start.7 = (bf16[2,512,512]{2,1,0:T(8,128)(2,1)S(1)}, bf16[2,512,512]{2,1,0:T(8,128)(2,1)}, u32[]{:S(2)}, u32[]{:S(2)}) collective-permute-start(bf16[2,512,512]{2,1,0:T(8,128)(2,1)S(1)} %collective-permute-done.refs_6_), channel_id=1, source_target_pairs={{0,8},{8,0},{16,24},{24,16},{32,40},{40,32},{48,56},{56,48},{64,72... | collective-permute-start | bytes 3145736 | tf_op jit(solution)/shard_map/ppermute | solution.py:335
  31.3 1.0 copy-start
  32.2 6.1 %collective-permute-start.8 = (bf16[2,512,512]{2,1,0:T(8,128)(2,1)S(1)}, bf16[2,512,512]{2,1,0:T(8,128)(2,1)}, u32[]{:S(2)}, u32[]{:S(2)}) collective-permute-start(bf16[2,512,512]{2,1,0:T(8,128)(2,1)S(1)} %collective-permute-done.1.refs_8_), channel_id=1, source_target_pairs={{0,8},{8,0},{16,24},{24,16},{32,40},{40,32},{48,56},{56,48},{64,72... | collective-permute-start | bytes 3145736 | tf_op jit(solution)/shard_map/ppermute | solution.py:335
  32.7 7.1 %collective-permute-start.9 = (bf16[2,512,512]{2,1,0:T(8,128)(2,1)}, bf16[2,512,512]{2,1,0:T(8,128)(2,1)}, u32[]{:S(2)}, u32[]{:S(2)}) collective-permute-start(bf16[2,512,512]{2,1,0:T(8,128)(2,1)} %collective-permute-done.2.refs_10_), channel_id=1, source_target_pairs={{0,8},{8,0},{16,24},{24,16},{32,40},{40,32},{48,56},{56,48},{64,72... | collective-permute-start | bytes 3145736 | tf_op jit(solution)/shard_map/ppermute | solution.py:335
  33.0 31.4 %collective-permute-start.4 = (bf16[2,512,512]{2,1,0:T(8,128)(2,1)S(1)}, bf16[2,512,512]{2,1,0:T(8,128)(2,1)}, u32[]{:S(2)}, u32[]{:S(2)}) collective-permute-start(bf16[2,512,512]{2,1,0:T(8,128)(2,1)S(1)} %collective-permute-done.1.refs_8_), channel_id=1, source_target_pairs={{0,96},{8,104},{16,112},{24,120},{32,0},{40,8},{48,16},{56,24},{64... | collective-permute-start | bytes 3145736 | tf_op jit(solution)/shard_map/ppermute | solution.py:335
  34.8 29.6 %collective-permute-start.5 = (bf16[2,512,512]{2,1,0:T(8,128)(2,1)}, bf16[2,512,512]{2,1,0:T(8,128)(2,1)}, u32[]{:S(2)}, u32[]{:S(2)}) collective-permute-start(bf16[2,512,512]{2,1,0:T(8,128)(2,1)} %collective-permute-done.2.refs_10_), channel_id=1, source_target_pairs={{0,32},{8,40},{16,48},{24,56},{32,64},{40,72},{48,80},{56,88},{64,... | collective-permute-start | bytes 3145736 | tf_op jit(solution)/shard_map/ppermute | solution.py:335
  35.1 29.3 %collective-permute-start.6 = (bf16[2,512,512]{2,1,0:T(8,128)(2,1)S(1)}, bf16[2,512,512]{2,1,0:T(8,128)(2,1)}, u32[]{:S(2)}, u32[]{:S(2)}) collective-permute-start(bf16[2,512,512]{2,1,0:T(8,128)(2,1)S(1)} %collective-permute-done.1.refs_8_), channel_id=1, source_target_pairs={{0,16},{8,24},{16,0},{24,8},{32,48},{40,56},{48,32},{56,40},{64,80... | collective-permute-start | bytes 3145736 | tf_op jit(solution)/shard_map/ppermute | solution.py:335
  38.3 26.2 %collective-permute-start.10 = (bf16[256,2048]{1,0:T(8,128)(2,1)}, bf16[256,2048]{1,0:T(8,128)(2,1)S(1)}, u32[]{:S(2)}, u32[]{:S(2)}) collective-permute-start(bf16[256,2048]{1,0:T(8,128)(2,1)} %copy-done.5), channel_id=1, source_target_pairs={{0,2},{1,3},{2,4},{3,5},{4,6},{5,7},{6,0},{7,1},{8,10},{9,11},{10,... | collective-permute-start | bytes 3145736 | tf_op jit(solution)/shard_map/ppermute | solution.py:338
  39.8 1.2 copy-start.1
  41.0 12.4 %copy-start.3 = (bf16[256,512]{1,0:T(8,128)(2,1)S(1)}, bf16[256,512]{1,0:T(8,128)(2,1)}, u32[]{:S(2)}) copy-start(bf16[256,512]{1,0:T(8,128)(2,1)} %query.1) | copy-start | bytes 786436
  64.5 11.7 %collective-permute-start.13 = (bf16[2,512,512]{2,1,0:T(8,128)(2,1)}, bf16[2,512,512]{2,1,0:T(8,128)(2,1)}, u32[]{:S(2)}, u32[]{:S(2)}) collective-permute-start(bf16[2,512,512]{2,1,0:T(8,128)(2,1)} %collective-permute-done.4.refs_6_), channel_id=1, source_target_pairs={{0,8},{8,0},{16,24},{24,16},{32,40},{40,32},{48,56},{56,48},{64,72... | collective-permute-start | bytes 3145736 | tf_op jit(solution)/shard_map/ppermute | solution.py:335
  64.5 13.0 %collective-permute-start.14 = (bf16[2,512,512]{2,1,0:T(8,128)(2,1)}, bf16[2,512,512]{2,1,0:T(8,128)(2,1)}, u32[]{:S(2)}, u32[]{:S(2)}) collective-permute-start(bf16[2,512,512]{2,1,0:T(8,128)(2,1)} %collective-permute-done.5.refs_8_), channel_id=1, source_target_pairs={{0,8},{8,0},{16,24},{24,16},{32,40},{40,32},{48,56},{56,48},{64,72... | collective-permute-start | bytes 3145736 | tf_op jit(solution)/shard_map/ppermute | solution.py:335
  65.0 12.5 %collective-permute-start.15 = (bf16[2,512,512]{2,1,0:T(8,128)(2,1)}, bf16[2,512,512]{2,1,0:T(8,128)(2,1)}, u32[]{:S(2)}, u32[]{:S(2)}) collective-permute-start(bf16[2,512,512]{2,1,0:T(8,128)(2,1)} %collective-permute-done.6.refs_10_), channel_id=1, source_target_pairs={{0,8},{8,0},{16,24},{24,16},{32,40},{40,32},{48,56},{56,48},{64,72... | collective-permute-start | bytes 3145736 | tf_op jit(solution)/shard_map/ppermute | solution.py:335
  65.1 34.4 %collective-permute-start.16 = (bf16[256,2048]{1,0:T(8,128)(2,1)}, bf16[256,2048]{1,0:T(8,128)(2,1)}, u32[]{:S(2)}, u32[]{:S(2)}) collective-permute-start(bf16[256,2048]{1,0:T(8,128)(2,1)} %get-tuple-element.41), channel_id=1, source_target_pairs={{0,6},{1,7},{2,0},{3,1},{4,2},{5,3},{6,4},{7,5},{8,14},{9,15},{10,... | collective-permute-start | bytes 3145736 | tf_op jit(solution)/shard_map/ppermute | solution.py:338
  66.7 32.9 %all-to-all-start = ((bf16[16,272,128]{2,1,0:T(8,128)(2,1)}), bf16[16,272,128]{2,1,0:T(8,128)(2,1)S(1)}, u32[]{:S(2)}, u32[]{:S(2)}) async-start(bf16[16,272,128]{2,1,0:T(8,128)(2,1)} %pack_queries.1), calls=%async_computation | async-start | bytes 2228224 | tf_op jit(solution)/shard_map/all_to_all | solution.py:365
  74.2 25.3 %collective-permute-start.11 = (bf16[1,512,512]{2,1,0:T(8,128)(2,1)S(1)}, bf16[1,512,512]{2,1,0:T(8,128)(2,1)}, u32[]{:S(2)}, u32[]{:S(2)}) collective-permute-start(bf16[1,512,512]{2,1,0:T(8,128)(2,1)S(1)} %slice.6), channel_id=1, source_target_pairs={{0,32},{8,40},{16,48},{24,56},{32,64},{40,72},{48,80},{56,88},{64,... | collective-permute-start | bytes 1572872 | tf_op jit(solution)/shard_map/ppermute | solution.py:335
  76.2 23.4 %collective-permute-start.12 = (bf16[1,512,512]{2,1,0:T(8,128)(2,1)S(1)}, bf16[1,512,512]{2,1,0:T(8,128)(2,1)}, u32[]{:S(2)}, u32[]{:S(2)}) collective-permute-start(bf16[1,512,512]{2,1,0:T(8,128)(2,1)S(1)} %slice.7), channel_id=1, source_target_pairs={{0,96},{8,104},{16,112},{24,120},{32,0},{40,8},{48,16},{56,24},{64... | collective-permute-start | bytes 1572872 | tf_op jit(solution)/shard_map/ppermute | solution.py:335
  99.6 26.6 %collective-permute-start.22 = (bf16[256,2048]{1,0:T(8,128)(2,1)}, bf16[256,2048]{1,0:T(8,128)(2,1)}, u32[]{:S(2)}, u32[]{:S(2)}) collective-permute-start(bf16[256,2048]{1,0:T(8,128)(2,1)} %copy-done.4), channel_id=1, source_target_pairs={{0,4},{1,5},{2,6},{3,7},{4,0},{5,1},{6,2},{7,3},{8,12},{9,13},{10,... | collective-permute-start | bytes 3145736 | tf_op jit(solution)/shard_map/ppermute | solution.py:338
  100.5 2.3 %collective-permute-start.17 = (bf16[1,512,512]{2,1,0:T(8,128)(2,1)}, bf16[1,512,512]{2,1,0:T(8,128)(2,1)}, u32[]{:S(2)}, u32[]{:S(2)}) collective-permute-start(bf16[1,512,512]{2,1,0:T(8,128)(2,1)} %collective-permute-done.11.refs_2_), channel_id=1, source_target_pairs={{0,8},{8,0},{16,24},{24,16},{32,40},{40,32},{48,56},{56,48},{64,72... | collective-permute-start | bytes 1572872 | tf_op jit(solution)/shard_map/ppermute | solution.py:335
  100.5 3.7 %collective-permute-start.18 = (bf16[1,512,512]{2,1,0:T(8,128)(2,1)}, bf16[1,512,512]{2,1,0:T(8,128)(2,1)}, u32[]{:S(2)}, u32[]{:S(2)}) collective-permute-start(bf16[1,512,512]{2,1,0:T(8,128)(2,1)} %collective-permute-done.12.refs_3_), channel_id=1, source_target_pairs={{0,8},{8,0},{16,24},{24,16},{32,40},{40,32},{48,56},{56,48},{64,72... | collective-permute-start | bytes 1572872 | tf_op jit(solution)/shard_map/ppermute | solution.py:335
  101.0 37.8 %collective-permute-start.23 = (bf16[256,2048]{1,0:T(8,128)(2,1)S(1)}, bf16[256,2048]{1,0:T(8,128)(2,1)}, u32[]{:S(2)}, u32[]{:S(2)}) collective-permute-start(bf16[256,2048]{1,0:T(8,128)(2,1)S(1)} %get-tuple-element.47.refs_4_), channel_id=1, source_target_pairs={{0,8},{8,0},{16,24},{24,16},{32,40},{40,32},{48,56},{56,48},{64,72... | collective-permute-start | bytes 3145736 | tf_op jit(solution)/shard_map/ppermute | solution.py:335
  101.1 40.1 %collective-permute-start.24 = (bf16[256,2048]{1,0:T(8,128)(2,1)S(1)}, bf16[256,2048]{1,0:T(8,128)(2,1)}, u32[]{:S(2)}, u32[]{:S(2)}) collective-permute-start(bf16[256,2048]{1,0:T(8,128)(2,1)S(1)} %collective-permute-done.10.refs_5_), channel_id=1, source_target_pairs={{0,8},{8,0},{16,24},{24,16},{32,40},{40,32},{48,56},{56,48},{64,72... | collective-permute-start | bytes 3145736 | tf_op jit(solution)/shard_map/ppermute | solution.py:335
  112.9 23.9 %all-to-all-start.1 = ((bf16[16,272,128]{2,1,0:T(8,128)(2,1)}), bf16[16,272,128]{2,1,0:T(8,128)(2,1)S(1)}, u32[]{:S(2)}, u32[]{:S(2)}) async-start(bf16[16,272,128]{2,1,0:T(8,128)(2,1)} %attend.1), calls=%async_computation.1 | async-start | bytes 2228224 | tf_op jit(solution)/shard_map/all_to_all | solution.py:383
  118.1 24.7 %collective-permute-start.25 = (bf16[256,2048]{1,0:T(8,128)(2,1)}, bf16[256,2048]{1,0:T(8,128)(2,1)}, u32[]{:S(2)}, u32[]{:S(2)}) collective-permute-start(bf16[256,2048]{1,0:T(8,128)(2,1)} %collective-permute-done.16.refs_6_), channel_id=1, source_target_pairs={{0,8},{8,0},{16,24},{24,16},{32,40},{40,32},{48,56},{56,48},{64,72... | collective-permute-start | bytes 3145736 | tf_op jit(solution)/shard_map/ppermute | solution.py:335
  126.2 24.5 %collective-permute-start.26 = (bf16[256,2048]{1,0:T(8,128)(2,1)}, bf16[256,2048]{1,0:T(8,128)(2,1)}, u32[]{:S(2)}, u32[]{:S(2)}) collective-permute-start(bf16[256,2048]{1,0:T(8,128)(2,1)} %collective-permute-done.22.refs_7_), channel_id=1, source_target_pairs={{0,8},{8,0},{16,24},{24,16},{32,40},{40,32},{48,56},{56,48},{64,72... | collective-permute-start | bytes 3145736 | tf_op jit(solution)/shard_map/ppermute | solution.py:335
  137.8 9.2 %collective-permute-start.19 = (bf16[208,512]{1,0:T(8,128)(2,1)S(1)}, bf16[208,512]{1,0:T(8,128)(2,1)S(1)}, u32[]{:S(2)}, u32[]{:S(2)}) collective-permute-start(bf16[208,512]{1,0:T(8,128)(2,1)S(1)} %combine.1.refs_0_), channel_id=1, source_target_pairs={{0,2},{1,3},{2,4},{3,5},{4,6},{5,7},{6,0},{7,1},{8,10},{9,11},{10,... | collective-permute-start | bytes 638984 | tf_op jit(solution)/shard_map/ppermute | solution.py:338
  138.8 10.9 %collective-permute-start.20 = (bf16[208,512]{1,0:T(8,128)(2,1)S(1)}, bf16[208,512]{1,0:T(8,128)(2,1)S(1)}, u32[]{:S(2)}, u32[]{:S(2)}) collective-permute-start(bf16[208,512]{1,0:T(8,128)(2,1)S(1)} %combine.1.refs_0_), channel_id=1, source_target_pairs={{0,6},{1,7},{2,0},{3,1},{4,2},{5,3},{6,4},{7,5},{8,14},{9,15},{10,... | collective-permute-start | bytes 638984 | tf_op jit(solution)/shard_map/ppermute | solution.py:338
  141.1 9.6 %collective-permute-start.21 = (bf16[208,512]{1,0:T(8,128)(2,1)S(1)}, bf16[208,512]{1,0:T(8,128)(2,1)S(1)}, u32[]{:S(2)}, u32[]{:S(2)}) collective-permute-start(bf16[208,512]{1,0:T(8,128)(2,1)S(1)} %combine.1.refs_0_), channel_id=1, source_target_pairs={{0,4},{1,5},{2,6},{3,7},{4,0},{5,1},{6,2},{7,3},{8,12},{9,13},{10,... | collective-permute-start | bytes 638984 | tf_op jit(solution)/shard_map/ppermute | solution.py:338
  154.1 10.5 %collective-permute-start.27 = (bf16[208,1024]{1,0:T(8,128)(2,1)S(1)}, bf16[208,1024]{1,0:T(8,128)(2,1)S(1)}, u32[]{:S(2)}, u32[]{:S(2)}) collective-permute-start(bf16[208,1024]{1,0:T(8,128)(2,1)S(1)} %mix.3), channel_id=1, source_target_pairs={{0,1},{1,0},{2,3},{3,2},{4,5},{5,4},{6,7},{7,6},{8,9},{9,8},{10,11... | collective-permute-start | bytes 1277960 | tf_op jit(solution)/shard_map/ppermute | solution.py:391

commit v6 on v5

--- a/solution.py
+++ b/solution.py
@@ -12,7 +12,7 @@
 M = 64
 BF = jnp.bfloat16
 F32 = jnp.float32
-ATTEND_SLOTS = 2
+ATTEND_SLOTS = 4
 VMEM_LIMIT = 48 * 1024 * 1024
 
 
@@ -349,9 +349,7 @@
         core, [x, (x + 1) % 4, (x + 3) % 4, (x + 2) % 4], out_weight
     )
     total = project(encoded, with_twin(0, 0, own), None)
-    below, above, across, total, to_next = lax.optimization_barrier(
-        (below, above, across, total, to_next)
-    )
+    below, above, total, to_next = lax.optimization_barrier((below, above, total, to_next))
 
     far, across_below, across_above = send(above, Z_DOWN), send(across, Z_UP), send(above, Y_SWAP)
     mix_last = across_x(to_next, 1)
@@ -363,8 +361,8 @@
     total, late_holder = lax.optimization_barrier((total, holder))
     outgoing = pack_queries(queries, valid, late_holder, groups)
     query_blocks = lax.all_to_all(outgoing, "dp", 0, 0, tiled=True)
-    far, across_below, across_above, total, mix_last, to_last, outgoing = lax.optimization_barrier(
-        (far, across_below, across_above, total, mix_last, to_last, outgoing)
+    across_below, across_above, total, mix_last, to_last, outgoing = lax.optimization_barrier(
+        (across_below, across_above, total, mix_last, to_last, outgoing)
     )
 
     far_keys, far_values = send(across_below[:1], Z_UP), send(across_above[1:], Z_DOWN)

time: 166 us -> 165 us (level)
    ppermute x6, waiting for transfers between devices: 25 us -> 20 us  [across_x(): return lax.ppermute(block, 'tensor', tensor_pairs(step, 0))]
    ppermute x21, waiting for transfers between devices: 23 us -> 27.8 us  [send(): return lax.ppermute(block, 'dp', pairs)]
where the time goes in v6:
time: 165 us; the launch traced here: 164 us
  waiting for transfers between devices  65 us (39%)
  Pallas kernels  54.3 us (33%)
  starting transfers between devices  37.2 us (23%)
  local copies, waits for them, and re-layouts  6.44 us (4%)
    pallas_call x3, Pallas kernels, project(): pl.pallas_call(functools.partial(project_kernel, [len(w) for _, w in piec...  32.1 us
    ppermute x21, waiting for transfers between devices, send(): return lax.ppermute(block, 'dp', pairs)  27.8 us
    ppermute x6, waiting for transfers between devices, across_x(): return lax.ppermute(block, 'tensor', tensor_pairs(step, 0))  20 us
    ppermute x21, starting transfers between devices, send(): return lax.ppermute(block, 'dp', pairs)  18.6 us
    all_to_all x1, waiting for transfers between devices, body(): returned = lax.all_to_all(parts, 'dp', 0, 0, tiled=True)  11.2 us
    ppermute x6, starting transfers between devices, across_x(): return lax.ppermute(block, 'tensor', tensor_pairs(step, 0))  8.94 us
    pallas_call x1, Pallas kernels, attend(): pl.pallas_call(functools.partial(attend_kernel, [len(w) for _, w in piece...  8.2 us
    pallas_call x2, Pallas kernels, mix(): pl.pallas_call(mix_kernel, grid_spec=pltpu.PrefetchScalarGridSpec(num_sca...  6.79 us
  transfers between devices with their start and end apart: 30, of which 12 were waited for; matrix products, arithmetic and copies ran while one was open for 2% of the time, Pallas kernels for 31%

profile of v6, /device:TPU:0, one launch (start us, length us, event | category | flops | bytes accessed | tf_op | source)
XLA Modules:
  0.0 163.8 jit_solution(13769516409860595347)
XLA Ops:
  0.0 2.0 %collective-permute-start.2 = (bf16[2,512,512]{2,1,0:T(8,128)(2,1)}, bf16[2,512,512]{2,1,0:T(8,128)(2,1)S(1)}, u32[]{:S(2)}, u32[]{:S(2)}) collective-permute-start(bf16[2,512,512]{2,1,0:T(8,128)(2,1)} %refs_2_.2), channel_id=1, source_target_pairs={{0,32},{8,40},{16,48},{24,56},{32,64},{40,72},{48,80},{56,88},{64,... | collective-permute-start | bytes 3145736 | tf_op jit(solution)/shard_map/ppermute | solution.py:335
  2.0 2.2 %collective-permute-start.3 = (bf16[2,512,512]{2,1,0:T(8,128)(2,1)}, bf16[2,512,512]{2,1,0:T(8,128)(2,1)S(1)}, u32[]{:S(2)}, u32[]{:S(2)}) collective-permute-start(bf16[2,512,512]{2,1,0:T(8,128)(2,1)} %refs_2_.2), channel_id=1, source_target_pairs={{0,96},{8,104},{16,112},{24,120},{32,0},{40,8},{48,16},{56,24},{64... | collective-permute-start | bytes 3145736 | tf_op jit(solution)/shard_map/ppermute | solution.py:335
  4.2 3.2 %collective-permute-start = (bf16[2,512,512]{2,1,0:T(8,128)(2,1)}, bf16[2,512,512]{2,1,0:T(8,128)(2,1)}, u32[]{:S(2)}, u32[]{:S(2)}) collective-permute-start(bf16[2,512,512]{2,1,0:T(8,128)(2,1)} %refs_2_.2), channel_id=1, source_target_pairs={{0,16},{8,24},{16,0},{24,8},{32,48},{40,56},{48,32},{56,40},{64,80... | collective-permute-start | bytes 3145736 | tf_op jit(solution)/shard_map/ppermute | solution.py:335
  7.5 4.6 %split_rows.1 = (bf16[256,2048]{1,0:T(8,128)(2,1)S(1)}, bf16[256,2048]{1,0:T(8,128)(2,1)S(1)}, bf16[256,2048]{1,0:T(8,128)(2,1)}, bf16[256,2048]{1,0:T(8,128)(2,1)S(1)}) custom-call(s32[5]{0:T(128)S(1)} %stack.101.place, bf16[512,8192]{1,0:T(8,128)(2,1)} %refs_3_.1, bf16[512,8192]{1,0:T(8,128)(2,1)} %refs_3_.1, bf16[512,8192]{1,0:T(8,128)(2,1)} %refs_3_.1, ...), custom_call_target="tpu_custom_call" | custom-call | bytes 65536 | tf_op jit(solution)/shard_map/split_rows/pallas_call | solution.py:117
  12.1 1.0 copy-done.5
  13.1 6.6 %project.3.refs_12_ = f32[1024,1024]{1,0:T(8,128)} custom-call(s32[2]{0:T(128)S(1)} %pad_add_fusion.2.idx, bf16[1024,8192]{1,0:T(8,128)(2,1)} %bitcast.26, bf16[1024,8192]{1,0:T(8,128)(2,1)} %bitcast.27, bf16[2,512,512]{2,1,0:T(8,128)(2,1)S(1)} %copy-done.2, bf16[2,512,512]{2,1,0:T(8,128)(2,1)} %collective-permute-done.4.refs_3_), custom_call_target="tpu_custom_call" | custom-call | flops 2147483648 | bytes 4194304 | tf_op jit(solution)/shard_map/project/pallas_call | solution.py:90
  19.8 8.4 %collective-permute-done.2.refs_6_ = bf16[2,512,512]{2,1,0:T(8,128)(2,1)S(1)} collective-permute-done((bf16[2,512,512]{2,1,0:T(8,128)(2,1)}, bf16[2,512,512]{2,1,0:T(8,128)(2,1)S(1)}, u32[]{:S(2)}, u32[]{:S(2)}) %collective-permute-start.2) | collective-permute-done | bytes 1048608 | tf_op jit(solution)/shard_map/ppermute | solution.py:335
  28.2 1.0 copy-done
  29.2 0.5 collective-permute-start.7
  29.6 1.6 collective-permute-done.refs_10_
  31.5 3.2 %collective-permute-start.5 = (bf16[2,512,512]{2,1,0:T(8,128)(2,1)S(1)}, bf16[2,512,512]{2,1,0:T(8,128)(2,1)}, u32[]{:S(2)}, u32[]{:S(2)}) collective-permute-start(bf16[2,512,512]{2,1,0:T(8,128)(2,1)S(1)} %collective-permute-done.3.refs_8_), channel_id=1, source_target_pairs={{0,16},{8,24},{16,0},{24,8},{32,48},{40,56},{48,32},{56,40},{64,80... | collective-permute-start | bytes 3145736 | tf_op jit(solution)/shard_map/ppermute | solution.py:335
  34.8 1.7 %collective-permute-start.12 = (bf16[2,512,512]{2,1,0:T(8,128)(2,1)S(1)}, bf16[2,512,512]{2,1,0:T(8,128)(2,1)}, u32[]{:S(2)}, u32[]{:S(2)}) collective-permute-start(bf16[2,512,512]{2,1,0:T(8,128)(2,1)S(1)} %collective-permute-done.3.refs_8_), channel_id=1, source_target_pairs={{0,96},{8,104},{16,112},{24,120},{32,0},{40,8},{48,16},{56,24},{64... | collective-permute-start | bytes 3145736 | tf_op jit(solution)/shard_map/ppermute | solution.py:335
  36.5 1.5 collective-permute-start.9
  38.4 1.2 copy-done.1
  39.6 12.4 %project.4.refs_12_ = f32[1024,1024]{1,0:T(8,128)} custom-call(s32[6]{0:T(128)S(1)} %stack.108.idx, bf16[1024,8192]{1,0:T(8,128)(2,1)} %bitcast.28, bf16[1024,8192]{1,0:T(8,128)(2,1)} %bitcast.29, bf16[1024,8192]{1,0:T(8,128)(2,1)} %bitcast.30, bf16[1024,8192]{1,0:T(8,128)(2,1)} %bitcast.31, bf16[1024,8192]{1,0:T(8,128)(2,1)} %bitcast.32, ...), custom_call_target="tpu_custom_call" | custom-call | flops 6442450944 | bytes 12582912 | tf_op jit(solution)/shard_map/project/pallas_call | solution.py:90
  52.0 1.6 %pack_queries.1 = bf16[16,272,128]{2,1,0:T(8,128)(2,1)} custom-call(s32[8]{0:T(128)S(1)} %and_select_fusion.1.holder, bf16[256,512]{1,0:T(8,128)(2,1)S(1)} %copy-done.3, f32[8,128]{1,0:T(8,128)S(1)} %bitcast.25), custom_call_target="tpu_custom_call" | custom-call | tf_op jit(solution)/shard_map/pack_queries/pallas_call | solution.py:151
  53.6 5.2 %collective-permute-done.5.refs_10_ = bf16[2,512,512]{2,1,0:T(8,128)(2,1)} collective-permute-done((bf16[2,512,512]{2,1,0:T(8,128)(2,1)S(1)}, bf16[2,512,512]{2,1,0:T(8,128)(2,1)}, u32[]{:S(2)}, u32[]{:S(2)}) %collective-permute-start.5) | collective-permute-done | bytes 1048608 | tf_op jit(solution)/shard_map/ppermute | solution.py:335
  58.8 4.2 %collective-permute-done.9.refs_5_ = bf16[256,2048]{1,0:T(8,128)(2,1)S(1)} collective-permute-done((bf16[256,2048]{1,0:T(8,128)(2,1)}, bf16[256,2048]{1,0:T(8,128)(2,1)S(1)}, u32[]{:S(2)}, u32[]{:S(2)}) %collective-permute-start.9) | collective-permute-done | bytes 1048608 | tf_op jit(solution)/shard_map/ppermute | solution.py:338
  63.0 1.3 collective-permute-done.1.refs_8_
  64.3 0.5 collective-permute-start.15
  64.8 1.7 %collective-permute-start.16 = (bf16[256,2048]{1,0:T(8,128)(2,1)}, bf16[256,2048]{1,0:T(8,128)(2,1)}, u32[]{:S(2)}, u32[]{:S(2)}) collective-permute-start(bf16[256,2048]{1,0:T(8,128)(2,1)} %get-tuple-element.37), channel_id=1, source_target_pairs={{0,6},{1,7},{2,0},{3,1},{4,2},{5,3},{6,4},{7,5},{8,14},{9,15},{10,... | collective-permute-start | bytes 3145736 | tf_op jit(solution)/shard_map/ppermute | solution.py:338
  66.5 3.7 %all-to-all-start = ((bf16[16,272,128]{2,1,0:T(8,128)(2,1)}), bf16[16,272,128]{2,1,0:T(8,128)(2,1)S(1)}, u32[]{:S(2)}, u32[]{:S(2)}) async-start(bf16[16,272,128]{2,1,0:T(8,128)(2,1)} %pack_queries.1), calls=%async_computation | async-start | bytes 2228224 | tf_op jit(solution)/shard_map/all_to_all | solution.py:363
  70.4 1.1 slice.6
  71.5 1.1 slice.7
  72.5 1.9 %collective-permute-start.10 = (bf16[1,512,512]{2,1,0:T(8,128)(2,1)S(1)}, bf16[1,512,512]{2,1,0:T(8,128)(2,1)}, u32[]{:S(2)}, u32[]{:S(2)}) collective-permute-start(bf16[1,512,512]{2,1,0:T(8,128)(2,1)S(1)} %slice.6), channel_id=1, source_target_pairs={{0,32},{8,40},{16,48},{24,56},{32,64},{40,72},{48,80},{56,88},{64,... | collective-permute-start | bytes 1572872 | tf_op jit(solution)/shard_map/ppermute | solution.py:335
  74.4 1.5 collective-permute-start.11
  75.9 13.1 %project.5.refs_6_ = f32[1024,1024]{1,0:T(8,128)} custom-call(s32[6]{0:T(128)S(1)} %stack.115.idx, bf16[1024,8192]{1,0:T(8,128)(2,1)} %bitcast.34, bf16[1024,8192]{1,0:T(8,128)(2,1)} %bitcast.35, bf16[1024,8192]{1,0:T(8,128)(2,1)} %bitcast.36, bf16[1024,8192]{1,0:T(8,128)(2,1)} %bitcast.37, bf16[1024,8192]{1,0:T(8,128)(2,1)} %bitcast.38, ...), custom_call_target="tpu_custom_call" | custom-call | flops 6442450944 | bytes 12582912 | tf_op jit(solution)/shard_map/project/pallas_call | solution.py:90
  88.9 8.9 %collective-permute-done.10.refs_2_ = bf16[1,512,512]{2,1,0:T(8,128)(2,1)} collective-permute-done((bf16[1,512,512]{2,1,0:T(8,128)(2,1)S(1)}, bf16[1,512,512]{2,1,0:T(8,128)(2,1)}, u32[]{:S(2)}, u32[]{:S(2)}) %collective-permute-start.10) | collective-permute-done | bytes 524320 | tf_op jit(solution)/shard_map/ppermute | solution.py:335
  97.8 1.9 %collective-permute-start.22 = (bf16[256,2048]{1,0:T(8,128)(2,1)}, bf16[256,2048]{1,0:T(8,128)(2,1)}, u32[]{:S(2)}, u32[]{:S(2)}) collective-permute-start(bf16[256,2048]{1,0:T(8,128)(2,1)} %copy-done.4), channel_id=1, source_target_pairs={{0,4},{1,5},{2,6},{3,7},{4,0},{5,1},{6,2},{7,3},{8,12},{9,13},{10,... | collective-permute-start | bytes 3145736 | tf_op jit(solution)/shard_map/ppermute | solution.py:338
  99.7 0.5 collective-permute-start.18
  100.3 0.7 collective-permute-start.24
  101.1 0.9 collective-permute-done.17.refs_4_
  102.0 1.5 collective-permute-done.18.refs_5_
  103.5 8.2 %attend.1 = bf16[16,272,128]{2,1,0:T(8,128)(2,1)} custom-call(s32[10]{0:T(128)S(1)} %pad_add_fusion.1.idx, bf16[1024,8192]{1,0:T(8,128)(2,1)} %bitcast.40, bf16[1024,8192]{1,0:T(8,128)(2,1)} %bitcast.41, bf16[1,512,512]{2,1,0:T(8,128)(2,1)} %collective-permute-done.10.refs_2_, bf16[1,512,512]{2,1,0:T(8,128)(2,1)} %collective-permute-done.11.refs_3_, ...), custom_call_target="tpu_custom_call" | custom-call | tf_op jit(solution)/shard_map/attend/pallas_call | solution.py:213
  111.7 5.2 %all-to-all-start.1 = ((bf16[16,272,128]{2,1,0:T(8,128)(2,1)}), bf16[16,272,128]{2,1,0:T(8,128)(2,1)S(1)}, u32[]{:S(2)}, u32[]{:S(2)}) async-start(bf16[16,272,128]{2,1,0:T(8,128)(2,1)} %attend.1), calls=%async_computation.1 | async-start | bytes 2228224 | tf_op jit(solution)/shard_map/all_to_all | solution.py:381
  116.9 0.4 collective-permute-start.25
  117.3 7.1 %collective-permute-done.22.refs_7_ = bf16[256,2048]{1,0:T(8,128)(2,1)} collective-permute-done((bf16[256,2048]{1,0:T(8,128)(2,1)}, bf16[256,2048]{1,0:T(8,128)(2,1)}, u32[]{:S(2)}, u32[]{:S(2)}) %collective-permute-start.22) | collective-permute-done | bytes 1048608 | tf_op jit(solution)/shard_map/ppermute | solution.py:338
  124.4 11.2 %all-to-all-done.1.parts = bf16[16,272,128]{2,1,0:T(8,128)(2,1)S(1)} async-done(((bf16[16,272,128]{2,1,0:T(8,128)(2,1)}), bf16[16,272,128]{2,1,0:T(8,128)(2,1)S(1)}, u32[]{:S(2)}, u32[]{:S(2)}) %all-to-all-start.1) | async-done | bytes 1114144 | tf_op jit(solution)/shard_map/all_to_all | solution.py:381
  135.6 1.0 combine.1.refs_0_
  136.6 0.7 collective-permute-start.19
  137.3 2.6 %collective-permute-start.20 = (bf16[208,512]{1,0:T(8,128)(2,1)S(1)}, bf16[208,512]{1,0:T(8,128)(2,1)S(1)}, u32[]{:S(2)}, u32[]{:S(2)}) collective-permute-start(bf16[208,512]{1,0:T(8,128)(2,1)S(1)} %combine.1.refs_0_), channel_id=1, source_target_pairs={{0,6},{1,7},{2,0},{3,1},{4,2},{5,3},{6,4},{7,5},{8,14},{9,15},{10,... | collective-permute-start | bytes 638984 | tf_op jit(solution)/shard_map/ppermute | solution.py:338
  139.9 0.5 collective-permute-start.21
  140.5 8.7 %collective-permute-done.19.refs_1_ = bf16[208,512]{1,0:T(8,128)(2,1)S(1)} collective-permute-done((bf16[208,512]{1,0:T(8,128)(2,1)S(1)}, bf16[208,512]{1,0:T(8,128)(2,1)S(1)}, u32[]{:S(2)}, u32[]{:S(2)}) %collective-permute-start.19) | collective-permute-done | bytes 213024 | tf_op jit(solution)/shard_map/ppermute | solution.py:338
  149.2 3.4 %mix.3 = bf16[208,1024]{1,0:T(8,128)(2,1)S(1)} custom-call(s32[2]{0:T(128)S(1)} %pad_add_fusion.3.place, bf16[208,512]{1,0:T(8,128)(2,1)S(1)} %combine.1.refs_0_, bf16[208,512]{1,0:T(8,128)(2,1)S(1)} %collective-permute-done.19.refs_1_, bf16[208,512]{1,0:T(8,128)(2,1)S(1)} %collective-permute-done.20.refs_2_, ...), custom_call_target="tpu_custom_call" | custom-call | flops 872415232 | bytes 4194304 | tf_op jit(solution)/shard_map/mix/pallas_call | solution.py:292
  152.6 0.8 collective-permute-start.27
  153.5 3.4 %mix.2 = f32[208,1024]{1,0:T(8,128)S(1)} custom-call(s32[2]{0:T(128)S(1)} %pad_add_fusion.place, bf16[208,512]{1,0:T(8,128)(2,1)S(1)} %combine.1.refs_0_, bf16[208,512]{1,0:T(8,128)(2,1)S(1)} %collective-permute-done.19.refs_1_, bf16[208,512]{1,0:T(8,128)(2,1)S(1)} %collective-permute-done.20.refs_2_, bf16[208,512]{1,0:T(8,128)(2,1)S(1)} %collective-permute-done.21.refs_3_, ...), custom_call_target="tpu_custom_call" | custom-call | flops 872415232 | bytes 4194304 | tf_op jit(solution)/shard_map/mix/pallas_call | solution.py:292
  156.9 6.0 %collective-permute-done.27 = bf16[208,1024]{1,0:T(8,128)(2,1)S(1)} collective-permute-done((bf16[208,1024]{1,0:T(8,128)(2,1)S(1)}, bf16[208,1024]{1,0:T(8,128)(2,1)S(1)}, u32[]{:S(2)}, u32[]{:S(2)}) %collective-permute-start.27) | collective-permute-done | bytes 426016 | tf_op jit(solution)/shard_map/ppermute | solution.py:389
  163.0 0.9 concatenate.7
  (53 shorter events, 1.3 us)
Async XLA Ops:
  0.0 13.1 %collective-permute-start.4 = (bf16[2,512,512]{2,1,0:T(8,128)(2,1)}, bf16[2,512,512]{2,1,0:T(8,128)(2,1)}, u32[]{:S(2)}, u32[]{:S(2)}) collective-permute-start(bf16[2,512,512]{2,1,0:T(8,128)(2,1)} %refs_2_.2), channel_id=1, source_target_pairs={{0,8},{8,0},{16,24},{24,16},{32,40},{40,32},{48,56},{56,48},{64,72... | collective-permute-start | bytes 3145736 | tf_op jit(solution)/shard_map/ppermute | solution.py:335
  0.0 28.2 %collective-permute-start.2 = (bf16[2,512,512]{2,1,0:T(8,128)(2,1)}, bf16[2,512,512]{2,1,0:T(8,128)(2,1)S(1)}, u32[]{:S(2)}, u32[]{:S(2)}) collective-permute-start(bf16[2,512,512]{2,1,0:T(8,128)(2,1)} %refs_2_.2), channel_id=1, source_target_pairs={{0,32},{8,40},{16,48},{24,56},{32,64},{40,72},{48,80},{56,88},{64,... | collective-permute-start | bytes 3145736 | tf_op jit(solution)/shard_map/ppermute | solution.py:335
  2.0 26.2 %collective-permute-start.3 = (bf16[2,512,512]{2,1,0:T(8,128)(2,1)}, bf16[2,512,512]{2,1,0:T(8,128)(2,1)S(1)}, u32[]{:S(2)}, u32[]{:S(2)}) collective-permute-start(bf16[2,512,512]{2,1,0:T(8,128)(2,1)} %refs_2_.2), channel_id=1, source_target_pairs={{0,96},{8,104},{16,112},{24,120},{32,0},{40,8},{48,16},{56,24},{64... | collective-permute-start | bytes 3145736 | tf_op jit(solution)/shard_map/ppermute | solution.py:335
  4.2 27.1 %collective-permute-start = (bf16[2,512,512]{2,1,0:T(8,128)(2,1)}, bf16[2,512,512]{2,1,0:T(8,128)(2,1)}, u32[]{:S(2)}, u32[]{:S(2)}) collective-permute-start(bf16[2,512,512]{2,1,0:T(8,128)(2,1)} %refs_2_.2), channel_id=1, source_target_pairs={{0,16},{8,24},{16,0},{24,8},{32,48},{40,56},{48,32},{56,40},{64,80... | collective-permute-start | bytes 3145736 | tf_op jit(solution)/shard_map/ppermute | solution.py:335
  7.5 5.6 %copy-start.2 = (bf16[2,512,512]{2,1,0:T(8,128)(2,1)S(1)}, bf16[2,512,512]{2,1,0:T(8,128)(2,1)}, u32[]{:S(2)}) copy-start(bf16[2,512,512]{2,1,0:T(8,128)(2,1)} %refs_2_.2) | copy-start | bytes 3145732
  12.1 1.0 copy-start.5
  12.1 7.7 %copy-start.4 = (bf16[256,2048]{1,0:T(8,128)(2,1)}, bf16[256,2048]{1,0:T(8,128)(2,1)S(1)}, u32[]{:S(2)}) copy-start(bf16[256,2048]{1,0:T(8,128)(2,1)S(1)} %get-tuple-element.46) | copy-start | bytes 3145732
  13.1 18.2 %copy-start.7 = (s32[128]{0:T(128)S(1)}, s32[128]{0:T(128)}, u32[]{:S(2)}) copy-start(s32[128]{0:T(128)} %param.11) | copy-start | bytes 1540
  13.1 25.2 %copy-start.6 = (s32[1,4,2,128]{3,2,1,0:T(2,128)S(1)}, s32[1,4,2,128]{3,2,1,0:T(2,128)}, u32[]{:S(2)}) copy-start(s32[1,4,2,128]{3,2,1,0:T(2,128)} %param.10) | copy-start | bytes 12292
  28.2 8.4 %collective-permute-start.6 = (bf16[2,512,512]{2,1,0:T(8,128)(2,1)S(1)}, bf16[2,512,512]{2,1,0:T(8,128)(2,1)}, u32[]{:S(2)}, u32[]{:S(2)}) collective-permute-start(bf16[2,512,512]{2,1,0:T(8,128)(2,1)S(1)} %collective-permute-done.2.refs_6_), channel_id=1, source_target_pairs={{0,8},{8,0},{16,24},{24,16},{32,40},{40,32},{48,56},{56,48},{64,72... | collective-permute-start | bytes 3145736 | tf_op jit(solution)/shard_map/ppermute | solution.py:335
  28.2 1.0 copy-start
  29.2 8.9 %collective-permute-start.7 = (bf16[2,512,512]{2,1,0:T(8,128)(2,1)S(1)}, bf16[2,512,512]{2,1,0:T(8,128)(2,1)}, u32[]{:S(2)}, u32[]{:S(2)}) collective-permute-start(bf16[2,512,512]{2,1,0:T(8,128)(2,1)S(1)} %collective-permute-done.3.refs_8_), channel_id=1, source_target_pairs={{0,8},{8,0},{16,24},{24,16},{32,40},{40,32},{48,56},{56,48},{64,72... | collective-permute-start | bytes 3145736 | tf_op jit(solution)/shard_map/ppermute | solution.py:335
  31.3 7.1 %collective-permute-start.8 = (bf16[2,512,512]{2,1,0:T(8,128)(2,1)}, bf16[2,512,512]{2,1,0:T(8,128)(2,1)}, u32[]{:S(2)}, u32[]{:S(2)}) collective-permute-start(bf16[2,512,512]{2,1,0:T(8,128)(2,1)} %collective-permute-done.refs_10_), channel_id=1, source_target_pairs={{0,8},{8,0},{16,24},{24,16},{32,40},{40,32},{48,56},{56,48},{64,72... | collective-permute-start | bytes 3145736 | tf_op jit(solution)/shard_map/ppermute | solution.py:335
  31.5 27.3 %collective-permute-start.5 = (bf16[2,512,512]{2,1,0:T(8,128)(2,1)S(1)}, bf16[2,512,512]{2,1,0:T(8,128)(2,1)}, u32[]{:S(2)}, u32[]{:S(2)}) collective-permute-start(bf16[2,512,512]{2,1,0:T(8,128)(2,1)S(1)} %collective-permute-done.3.refs_8_), channel_id=1, source_target_pairs={{0,16},{8,24},{16,0},{24,8},{32,48},{40,56},{48,32},{56,40},{64,80... | collective-permute-start | bytes 3145736 | tf_op jit(solution)/shard_map/ppermute | solution.py:335
  34.8 30.0 %collective-permute-start.12 = (bf16[2,512,512]{2,1,0:T(8,128)(2,1)S(1)}, bf16[2,512,512]{2,1,0:T(8,128)(2,1)}, u32[]{:S(2)}, u32[]{:S(2)}) collective-permute-start(bf16[2,512,512]{2,1,0:T(8,128)(2,1)S(1)} %collective-permute-done.3.refs_8_), channel_id=1, source_target_pairs={{0,96},{8,104},{16,112},{24,120},{32,0},{40,8},{48,16},{56,24},{64... | collective-permute-start | bytes 3145736 | tf_op jit(solution)/shard_map/ppermute | solution.py:335
  36.5 26.4 %collective-permute-start.9 = (bf16[256,2048]{1,0:T(8,128)(2,1)}, bf16[256,2048]{1,0:T(8,128)(2,1)S(1)}, u32[]{:S(2)}, u32[]{:S(2)}) collective-permute-start(bf16[256,2048]{1,0:T(8,128)(2,1)} %copy-done.5), channel_id=1, source_target_pairs={{0,2},{1,3},{2,4},{3,5},{4,6},{5,7},{6,0},{7,1},{8,10},{9,11},{10,... | collective-permute-start | bytes 3145736 | tf_op jit(solution)/shard_map/ppermute | solution.py:338
  38.0 26.3 %collective-permute-start.1 = (bf16[2,512,512]{2,1,0:T(8,128)(2,1)}, bf16[2,512,512]{2,1,0:T(8,128)(2,1)}, u32[]{:S(2)}, u32[]{:S(2)}) collective-permute-start(bf16[2,512,512]{2,1,0:T(8,128)(2,1)} %collective-permute-done.refs_10_), channel_id=1, source_target_pairs={{0,32},{8,40},{16,48},{24,56},{32,64},{40,72},{48,80},{56,88},{64,... | collective-permute-start | bytes 3145736 | tf_op jit(solution)/shard_map/ppermute | solution.py:335
  38.3 1.2 copy-start.1
  39.6 12.4 %copy-start.3 = (bf16[256,512]{1,0:T(8,128)(2,1)S(1)}, bf16[256,512]{1,0:T(8,128)(2,1)}, u32[]{:S(2)}) copy-start(bf16[256,512]{1,0:T(8,128)(2,1)} %query.1) | copy-start | bytes 786436
  64.3 10.1 %collective-permute-start.14 = (bf16[2,512,512]{2,1,0:T(8,128)(2,1)}, bf16[2,512,512]{2,1,0:T(8,128)(2,1)}, u32[]{:S(2)}, u32[]{:S(2)}) collective-permute-start(bf16[2,512,512]{2,1,0:T(8,128)(2,1)} %collective-permute-done.1.refs_8_), channel_id=1, source_target_pairs={{0,8},{8,0},{16,24},{24,16},{32,40},{40,32},{48,56},{56,48},{64,72... | collective-permute-start | bytes 3145736 | tf_op jit(solution)/shard_map/ppermute | solution.py:335
  64.3 11.6 %collective-permute-start.15 = (bf16[2,512,512]{2,1,0:T(8,128)(2,1)}, bf16[2,512,512]{2,1,0:T(8,128)(2,1)}, u32[]{:S(2)}, u32[]{:S(2)}) collective-permute-start(bf16[2,512,512]{2,1,0:T(8,128)(2,1)} %collective-permute-done.5.refs_10_), channel_id=1, source_target_pairs={{0,8},{8,0},{16,24},{24,16},{32,40},{40,32},{48,56},{56,48},{64,72... | collective-permute-start | bytes 3145736 | tf_op jit(solution)/shard_map/ppermute | solution.py:335
  64.8 11.1 %collective-permute-start.13 = (bf16[2,512,512]{2,1,0:T(8,128)(2,1)}, bf16[2,512,512]{2,1,0:T(8,128)(2,1)}, u32[]{:S(2)}, u32[]{:S(2)}) collective-permute-start(bf16[2,512,512]{2,1,0:T(8,128)(2,1)} %collective-permute-done.12.refs_6_), channel_id=1, source_target_pairs={{0,8},{8,0},{16,24},{24,16},{32,40},{40,32},{48,56},{56,48},{64,72... | collective-permute-start | bytes 3145736 | tf_op jit(solution)/shard_map/ppermute | solution.py:335
  64.8 33.0 %collective-permute-start.16 = (bf16[256,2048]{1,0:T(8,128)(2,1)}, bf16[256,2048]{1,0:T(8,128)(2,1)}, u32[]{:S(2)}, u32[]{:S(2)}) collective-permute-start(bf16[256,2048]{1,0:T(8,128)(2,1)} %get-tuple-element.37), channel_id=1, source_target_pairs={{0,6},{1,7},{2,0},{3,1},{4,2},{5,3},{6,4},{7,5},{8,14},{9,15},{10,... | collective-permute-start | bytes 3145736 | tf_op jit(solution)/shard_map/ppermute | solution.py:338
  66.5 31.3 %all-to-all-start = ((bf16[16,272,128]{2,1,0:T(8,128)(2,1)}), bf16[16,272,128]{2,1,0:T(8,128)(2,1)S(1)}, u32[]{:S(2)}, u32[]{:S(2)}) async-start(bf16[16,272,128]{2,1,0:T(8,128)(2,1)} %pack_queries.1), calls=%async_computation | async-start | bytes 2228224 | tf_op jit(solution)/shard_map/all_to_all | solution.py:363
  72.5 25.3 %collective-permute-start.10 = (bf16[1,512,512]{2,1,0:T(8,128)(2,1)S(1)}, bf16[1,512,512]{2,1,0:T(8,128)(2,1)}, u32[]{:S(2)}, u32[]{:S(2)}) collective-permute-start(bf16[1,512,512]{2,1,0:T(8,128)(2,1)S(1)} %slice.6), channel_id=1, source_target_pairs={{0,32},{8,40},{16,48},{24,56},{32,64},{40,72},{48,80},{56,88},{64,... | collective-permute-start | bytes 1572872 | tf_op jit(solution)/shard_map/ppermute | solution.py:335
  74.4 23.4 %collective-permute-start.11 = (bf16[1,512,512]{2,1,0:T(8,128)(2,1)S(1)}, bf16[1,512,512]{2,1,0:T(8,128)(2,1)}, u32[]{:S(2)}, u32[]{:S(2)}) collective-permute-start(bf16[1,512,512]{2,1,0:T(8,128)(2,1)S(1)} %slice.7), channel_id=1, source_target_pairs={{0,96},{8,104},{16,112},{24,120},{32,0},{40,8},{48,16},{56,24},{64... | collective-permute-start | bytes 1572872 | tf_op jit(solution)/shard_map/ppermute | solution.py:335
  97.8 26.6 %collective-permute-start.22 = (bf16[256,2048]{1,0:T(8,128)(2,1)}, bf16[256,2048]{1,0:T(8,128)(2,1)}, u32[]{:S(2)}, u32[]{:S(2)}) collective-permute-start(bf16[256,2048]{1,0:T(8,128)(2,1)} %copy-done.4), channel_id=1, source_target_pairs={{0,4},{1,5},{2,6},{3,7},{4,0},{5,1},{6,2},{7,3},{8,12},{9,13},{10,... | collective-permute-start | bytes 3145736 | tf_op jit(solution)/shard_map/ppermute | solution.py:338
  99.7 2.3 %collective-permute-start.17 = (bf16[1,512,512]{2,1,0:T(8,128)(2,1)}, bf16[1,512,512]{2,1,0:T(8,128)(2,1)}, u32[]{:S(2)}, u32[]{:S(2)}) collective-permute-start(bf16[1,512,512]{2,1,0:T(8,128)(2,1)} %collective-permute-done.10.refs_2_), channel_id=1, source_target_pairs={{0,8},{8,0},{16,24},{24,16},{32,40},{40,32},{48,56},{56,48},{64,72... | collective-permute-start | bytes 1572872 | tf_op jit(solution)/shard_map/ppermute | solution.py:335
  99.7 3.7 %collective-permute-start.18 = (bf16[1,512,512]{2,1,0:T(8,128)(2,1)}, bf16[1,512,512]{2,1,0:T(8,128)(2,1)}, u32[]{:S(2)}, u32[]{:S(2)}) collective-permute-start(bf16[1,512,512]{2,1,0:T(8,128)(2,1)} %collective-permute-done.11.refs_3_), channel_id=1, source_target_pairs={{0,8},{8,0},{16,24},{24,16},{32,40},{40,32},{48,56},{56,48},{64,72... | collective-permute-start | bytes 1572872 | tf_op jit(solution)/shard_map/ppermute | solution.py:335
  100.2 37.0 %collective-permute-start.23 = (bf16[256,2048]{1,0:T(8,128)(2,1)S(1)}, bf16[256,2048]{1,0:T(8,128)(2,1)}, u32[]{:S(2)}, u32[]{:S(2)}) collective-permute-start(bf16[256,2048]{1,0:T(8,128)(2,1)S(1)} %get-tuple-element.43.refs_4_), channel_id=1, source_target_pairs={{0,8},{8,0},{16,24},{24,16},{32,40},{40,32},{48,56},{56,48},{64,72... | collective-permute-start | bytes 3145736 | tf_op jit(solution)/shard_map/ppermute | solution.py:335
  100.3 39.6 %collective-permute-start.24 = (bf16[256,2048]{1,0:T(8,128)(2,1)S(1)}, bf16[256,2048]{1,0:T(8,128)(2,1)}, u32[]{:S(2)}, u32[]{:S(2)}) collective-permute-start(bf16[256,2048]{1,0:T(8,128)(2,1)S(1)} %collective-permute-done.9.refs_5_), channel_id=1, source_target_pairs={{0,8},{8,0},{16,24},{24,16},{32,40},{40,32},{48,56},{56,48},{64,72... | collective-permute-start | bytes 3145736 | tf_op jit(solution)/shard_map/ppermute | solution.py:335
  111.7 23.9 %all-to-all-start.1 = ((bf16[16,272,128]{2,1,0:T(8,128)(2,1)}), bf16[16,272,128]{2,1,0:T(8,128)(2,1)S(1)}, u32[]{:S(2)}, u32[]{:S(2)}) async-start(bf16[16,272,128]{2,1,0:T(8,128)(2,1)} %attend.1), calls=%async_computation.1 | async-start | bytes 2228224 | tf_op jit(solution)/shard_map/all_to_all | solution.py:381
  116.9 23.6 %collective-permute-start.25 = (bf16[256,2048]{1,0:T(8,128)(2,1)}, bf16[256,2048]{1,0:T(8,128)(2,1)}, u32[]{:S(2)}, u32[]{:S(2)}) collective-permute-start(bf16[256,2048]{1,0:T(8,128)(2,1)} %collective-permute-done.16.refs_6_), channel_id=1, source_target_pairs={{0,8},{8,0},{16,24},{24,16},{32,40},{40,32},{48,56},{56,48},{64,72... | collective-permute-start | bytes 3145736 | tf_op jit(solution)/shard_map/ppermute | solution.py:335
  124.4 24.8 %collective-permute-start.26 = (bf16[256,2048]{1,0:T(8,128)(2,1)}, bf16[256,2048]{1,0:T(8,128)(2,1)}, u32[]{:S(2)}, u32[]{:S(2)}) collective-permute-start(bf16[256,2048]{1,0:T(8,128)(2,1)} %collective-permute-done.22.refs_7_), channel_id=1, source_target_pairs={{0,8},{8,0},{16,24},{24,16},{32,40},{40,32},{48,56},{56,48},{64,72... | collective-permute-start | bytes 3145736 | tf_op jit(solution)/shard_map/ppermute | solution.py:335
  136.6 12.6 %collective-permute-start.19 = (bf16[208,512]{1,0:T(8,128)(2,1)S(1)}, bf16[208,512]{1,0:T(8,128)(2,1)S(1)}, u32[]{:S(2)}, u32[]{:S(2)}) collective-permute-start(bf16[208,512]{1,0:T(8,128)(2,1)S(1)} %combine.1.refs_0_), channel_id=1, source_target_pairs={{0,2},{1,3},{2,4},{3,5},{4,6},{5,7},{6,0},{7,1},{8,10},{9,11},{10,... | collective-permute-start | bytes 638984 | tf_op jit(solution)/shard_map/ppermute | solution.py:338
  137.3 11.9 %collective-permute-start.20 = (bf16[208,512]{1,0:T(8,128)(2,1)S(1)}, bf16[208,512]{1,0:T(8,128)(2,1)S(1)}, u32[]{:S(2)}, u32[]{:S(2)}) collective-permute-start(bf16[208,512]{1,0:T(8,128)(2,1)S(1)} %combine.1.refs_0_), channel_id=1, source_target_pairs={{0,6},{1,7},{2,0},{3,1},{4,2},{5,3},{6,4},{7,5},{8,14},{9,15},{10,... | collective-permute-start | bytes 638984 | tf_op jit(solution)/shard_map/ppermute | solution.py:338
  139.9 9.3 %collective-permute-start.21 = (bf16[208,512]{1,0:T(8,128)(2,1)S(1)}, bf16[208,512]{1,0:T(8,128)(2,1)S(1)}, u32[]{:S(2)}, u32[]{:S(2)}) collective-permute-start(bf16[208,512]{1,0:T(8,128)(2,1)S(1)} %combine.1.refs_0_), channel_id=1, source_target_pairs={{0,4},{1,5},{2,6},{3,7},{4,0},{5,1},{6,2},{7,3},{8,12},{9,13},{10,... | collective-permute-start | bytes 638984 | tf_op jit(solution)/shard_map/ppermute | solution.py:338
  152.6 10.3 %collective-permute-start.27 = (bf16[208,1024]{1,0:T(8,128)(2,1)S(1)}, bf16[208,1024]{1,0:T(8,128)(2,1)S(1)}, u32[]{:S(2)}, u32[]{:S(2)}) collective-permute-start(bf16[208,1024]{1,0:T(8,128)(2,1)S(1)} %mix.3), channel_id=1, source_target_pairs={{0,1},{1,0},{2,3},{3,2},{4,5},{5,4},{6,7},{7,6},{8,9},{9,8},{10,11... | collective-permute-start | bytes 1277960 | tf_op jit(solution)/shard_map/ppermute | solution.py:389

commit v7 on v6

--- a/solution.py
+++ b/solution.py
@@ -349,10 +349,12 @@
         core, [x, (x + 1) % 4, (x + 3) % 4, (x + 2) % 4], out_weight
     )
     total = project(encoded, with_twin(0, 0, own), None)
-    below, above, total, to_next = lax.optimization_barrier((below, above, total, to_next))
+    below, above, total, to_next, to_last = lax.optimization_barrier(
+        (below, above, total, to_next, to_last)
+    )
 
     far, across_below, across_above = send(above, Z_DOWN), send(across, Z_UP), send(above, Y_SWAP)
-    mix_last = across_x(to_next, 1)
+    mix_last, mix_next = across_x(to_next, 1), across_x(to_last, -1)
     total = project(
         encoded,
         with_twin(-1, 0, below) + with_twin(1, 0, above) + with_twin(0, 1, across),
@@ -361,22 +363,23 @@
     total, late_holder = lax.optimization_barrier((total, holder))
     outgoing = pack_queries(queries, valid, late_holder, groups)
     query_blocks = lax.all_to_all(outgoing, "dp", 0, 0, tiled=True)
-    across_below, across_above, total, mix_last, to_last, outgoing = lax.optimization_barrier(
-        (across_below, across_above, total, mix_last, to_last, outgoing)
+    across_below, across_above, total, mix_last, mix_next, to_far, outgoing = (
+        lax.optimization_barrier(
+            (across_below, across_above, total, mix_last, mix_next, to_far, outgoing)
+        )
     )
 
     far_keys, far_values = send(across_below[:1], Z_UP), send(across_above[1:], Z_DOWN)
-    mix_next = across_x(to_last, -1)
+    mix_far = across_x(to_far, 2)
     total = project(
         encoded,
         with_twin(2, 0, far) + with_twin(-1, 1, across_below) + with_twin(1, 1, across_above),
         total,
     )
-    far_keys, far_values, total, mix_next, to_far, query_blocks = lax.optimization_barrier(
-        (far_keys, far_values, total, mix_next, to_far, query_blocks)
-    )
-
-    mix_far = across_x(to_far, 2)
+    far_keys, far_values, total, mix_far, query_blocks = lax.optimization_barrier(
+        (far_keys, far_values, total, mix_far, query_blocks)
+    )
+
     parts = attend(encoded, with_twin(2, 1, far_keys, far_values), total, owner, query_blocks)
     returned = lax.all_to_all(parts, "dp", 0, 0, tiled=True)
     lead = (M - 1) // 16 * 16

time: 165 us -> 164 us (level)
    all_to_all x1, waiting for transfers between devices: 11.2 us -> 18.1 us  [body(): returned = lax.all_to_all(parts, 'dp', 0, 0, tiled=True)]
    ppermute x21, waiting for transfers between devices: 27.8 us -> 21.4 us  [send(): return lax.ppermute(block, 'dp', pairs)]
  transfers between devices with their start and end apart: 30 -> 30, of which waited for: 12 -> 11; matrix products, arithmetic and copies ran while one was open for 2% -> 2% of each run, Pallas kernels for 31% -> 31%
where the time goes in v7:
time: 164 us
  waiting for transfers between devices  64.6 us (39%)
  Pallas kernels  54.2 us (33%)
  starting transfers between devices  37.4 us (23%)
  local copies, waits for them, and re-layouts  6.45 us (4%)
    pallas_call x3, Pallas kernels, project(): pl.pallas_call(functools.partial(project_kernel, [len(w) for _, w in piec...  32.1 us
    ppermute x21, waiting for transfers between devices, send(): return lax.ppermute(block, 'dp', pairs)  21.4 us
    ppermute x6, waiting for transfers between devices, across_x(): return lax.ppermute(block, 'tensor', tensor_pairs(step, 0))  19.1 us
    ppermute x21, starting transfers between devices, send(): return lax.ppermute(block, 'dp', pairs)  18.9 us
    all_to_all x1, waiting for transfers between devices, body(): returned = lax.all_to_all(parts, 'dp', 0, 0, tiled=True)  18.1 us
    ppermute x6, starting transfers between devices, across_x(): return lax.ppermute(block, 'tensor', tensor_pairs(step, 0))  8.73 us
    pallas_call x1, Pallas kernels, attend(): pl.pallas_call(functools.partial(attend_kernel, [len(w) for _, w in piece...  8.16 us
    pallas_call x2, Pallas kernels, mix(): pl.pallas_call(mix_kernel, grid_spec=pltpu.PrefetchScalarGridSpec(num_sca...  6.74 us
  transfers between devices with their start and end apart: 30, of which 11 were waited for; matrix products, arithmetic and copies ran while one was open for 2% of the time, Pallas kernels for 31%

profile of v7, /device:TPU:0, one launch (start us, length us, event | category | flops | bytes accessed | tf_op | source)
XLA Modules:
  0.0 163.5 jit_solution(16423382613528566668)
XLA Ops:
  0.0 2.0 %collective-permute-start.2 = (bf16[2,512,512]{2,1,0:T(8,128)(2,1)}, bf16[2,512,512]{2,1,0:T(8,128)(2,1)S(1)}, u32[]{:S(2)}, u32[]{:S(2)}) collective-permute-start(bf16[2,512,512]{2,1,0:T(8,128)(2,1)} %refs_2_.2), channel_id=1, source_target_pairs={{0,32},{8,40},{16,48},{24,56},{32,64},{40,72},{48,80},{56,88},{64,... | collective-permute-start | bytes 3145736 | tf_op jit(solution)/shard_map/ppermute | solution.py:335
  2.0 2.2 %collective-permute-start.3 = (bf16[2,512,512]{2,1,0:T(8,128)(2,1)}, bf16[2,512,512]{2,1,0:T(8,128)(2,1)S(1)}, u32[]{:S(2)}, u32[]{:S(2)}) collective-permute-start(bf16[2,512,512]{2,1,0:T(8,128)(2,1)} %refs_2_.2), channel_id=1, source_target_pairs={{0,96},{8,104},{16,112},{24,120},{32,0},{40,8},{48,16},{56,24},{64... | collective-permute-start | bytes 3145736 | tf_op jit(solution)/shard_map/ppermute | solution.py:335
  4.2 3.2 %collective-permute-start = (bf16[2,512,512]{2,1,0:T(8,128)(2,1)}, bf16[2,512,512]{2,1,0:T(8,128)(2,1)}, u32[]{:S(2)}, u32[]{:S(2)}) collective-permute-start(bf16[2,512,512]{2,1,0:T(8,128)(2,1)} %refs_2_.2), channel_id=1, source_target_pairs={{0,16},{8,24},{16,0},{24,8},{32,48},{40,56},{48,32},{56,40},{64,80... | collective-permute-start | bytes 3145736 | tf_op jit(solution)/shard_map/ppermute | solution.py:335
  7.5 4.6 %split_rows.1 = (bf16[256,2048]{1,0:T(8,128)(2,1)S(1)}, bf16[256,2048]{1,0:T(8,128)(2,1)S(1)}, bf16[256,2048]{1,0:T(8,128)(2,1)S(1)}, bf16[256,2048]{1,0:T(8,128)(2,1)}) custom-call(s32[5]{0:T(128)S(1)} %stack.101.place, bf16[512,8192]{1,0:T(8,128)(2,1)} %refs_3_.1, bf16[512,8192]{1,0:T(8,128)(2,1)} %refs_3_.1, bf16[512,8192]{1,0:T(8,128)(2,1)} %refs_3_.1, ...), custom_call_target="tpu_custom_call" | custom-call | bytes 65536 | tf_op jit(solution)/shard_map/split_rows/pallas_call | solution.py:117
  12.0 1.0 copy-done.4
  13.1 6.6 %project.3.refs_12_ = f32[1024,1024]{1,0:T(8,128)} custom-call(s32[2]{0:T(128)S(1)} %pad_add_fusion.2.idx, bf16[1024,8192]{1,0:T(8,128)(2,1)} %bitcast.26, bf16[1024,8192]{1,0:T(8,128)(2,1)} %bitcast.27, bf16[2,512,512]{2,1,0:T(8,128)(2,1)S(1)} %copy-done.2, bf16[2,512,512]{2,1,0:T(8,128)(2,1)} %collective-permute-done.4.refs_3_), custom_call_target="tpu_custom_call" | custom-call | flops 2147483648 | bytes 4194304 | tf_op jit(solution)/shard_map/project/pallas_call | solution.py:90
  19.8 8.4 %collective-permute-done.2.refs_6_ = bf16[2,512,512]{2,1,0:T(8,128)(2,1)S(1)} collective-permute-done((bf16[2,512,512]{2,1,0:T(8,128)(2,1)}, bf16[2,512,512]{2,1,0:T(8,128)(2,1)S(1)}, u32[]{:S(2)}, u32[]{:S(2)}) %collective-permute-start.2) | collective-permute-done | bytes 1048608 | tf_op jit(solution)/shard_map/ppermute | solution.py:335
  28.2 1.0 copy-done
  29.2 0.5 collective-permute-start.7
  29.6 1.6 collective-permute-done.refs_10_
  31.4 0.2 select_reduce_fusion
  31.5 3.2 %collective-permute-start.5 = (bf16[2,512,512]{2,1,0:T(8,128)(2,1)S(1)}, bf16[2,512,512]{2,1,0:T(8,128)(2,1)}, u32[]{:S(2)}, u32[]{:S(2)}) collective-permute-start(bf16[2,512,512]{2,1,0:T(8,128)(2,1)S(1)} %collective-permute-done.3.refs_8_), channel_id=1, source_target_pairs={{0,16},{8,24},{16,0},{24,8},{32,48},{40,56},{48,32},{56,40},{64,80... | collective-permute-start | bytes 3145736 | tf_op jit(solution)/shard_map/ppermute | solution.py:335
  34.8 1.7 %collective-permute-start.13 = (bf16[2,512,512]{2,1,0:T(8,128)(2,1)S(1)}, bf16[2,512,512]{2,1,0:T(8,128)(2,1)}, u32[]{:S(2)}, u32[]{:S(2)}) collective-permute-start(bf16[2,512,512]{2,1,0:T(8,128)(2,1)S(1)} %collective-permute-done.3.refs_8_), channel_id=1, source_target_pairs={{0,96},{8,104},{16,112},{24,120},{32,0},{40,8},{48,16},{56,24},{64... | collective-permute-start | bytes 3145736 | tf_op jit(solution)/shard_map/ppermute | solution.py:335
  36.5 2.8 %collective-permute-start.10 = (bf16[256,2048]{1,0:T(8,128)(2,1)}, bf16[256,2048]{1,0:T(8,128)(2,1)S(1)}, u32[]{:S(2)}, u32[]{:S(2)}) collective-permute-start(bf16[256,2048]{1,0:T(8,128)(2,1)} %copy-done.5), channel_id=1, source_target_pairs={{0,6},{1,7},{2,0},{3,1},{4,2},{5,3},{6,4},{7,5},{8,14},{9,15},{10,... | collective-permute-start | bytes 3145736 | tf_op jit(solution)/shard_map/ppermute | solution.py:338
  39.3 0.4 collective-permute-start.1
  39.7 1.2 copy-done.1
  40.9 12.4 %project.4.refs_12_ = f32[1024,1024]{1,0:T(8,128)} custom-call(s32[6]{0:T(128)S(1)} %stack.108.idx, bf16[1024,8192]{1,0:T(8,128)(2,1)} %bitcast.28, bf16[1024,8192]{1,0:T(8,128)(2,1)} %bitcast.29, bf16[1024,8192]{1,0:T(8,128)(2,1)} %bitcast.30, bf16[1024,8192]{1,0:T(8,128)(2,1)} %bitcast.31, bf16[1024,8192]{1,0:T(8,128)(2,1)} %bitcast.32, ...), custom_call_target="tpu_custom_call" | custom-call | flops 6442450944 | bytes 12582912 | tf_op jit(solution)/shard_map/project/pallas_call | solution.py:90
  53.3 1.6 %pack_queries.1 = bf16[16,272,128]{2,1,0:T(8,128)(2,1)} custom-call(s32[8]{0:T(128)S(1)} %and_select_fusion.1.holder, bf16[256,512]{1,0:T(8,128)(2,1)S(1)} %copy-done.3, f32[8,128]{1,0:T(8,128)S(1)} %bitcast.25), custom_call_target="tpu_custom_call" | custom-call | tf_op jit(solution)/shard_map/pack_queries/pallas_call | solution.py:151
  55.0 7.2 %collective-permute-done.10.refs_6_ = bf16[256,2048]{1,0:T(8,128)(2,1)S(1)} collective-permute-done((bf16[256,2048]{1,0:T(8,128)(2,1)}, bf16[256,2048]{1,0:T(8,128)(2,1)S(1)}, u32[]{:S(2)}, u32[]{:S(2)}) %collective-permute-start.10) | collective-permute-done | bytes 1048608 | tf_op jit(solution)/shard_map/ppermute | solution.py:338
  62.1 3.4 %collective-permute-done.9.refs_5_ = bf16[256,2048]{1,0:T(8,128)(2,1)} collective-permute-done((bf16[256,2048]{1,0:T(8,128)(2,1)}, bf16[256,2048]{1,0:T(8,128)(2,1)}, u32[]{:S(2)}, u32[]{:S(2)}) %collective-permute-start.9) | collective-permute-done | bytes 1048608 | tf_op jit(solution)/shard_map/ppermute | solution.py:338
  65.6 0.5 collective-permute-start.16
  66.1 1.9 %collective-permute-start.17 = (bf16[256,2048]{1,0:T(8,128)(2,1)}, bf16[256,2048]{1,0:T(8,128)(2,1)}, u32[]{:S(2)}, u32[]{:S(2)}) collective-permute-start(bf16[256,2048]{1,0:T(8,128)(2,1)} %get-tuple-element.40), channel_id=1, source_target_pairs={{0,4},{1,5},{2,6},{3,7},{4,0},{5,1},{6,2},{7,3},{8,12},{9,13},{10,... | collective-permute-start | bytes 3145736 | tf_op jit(solution)/shard_map/ppermute | solution.py:338
  68.1 3.7 %all-to-all-start = ((bf16[16,272,128]{2,1,0:T(8,128)(2,1)}), bf16[16,272,128]{2,1,0:T(8,128)(2,1)S(1)}, u32[]{:S(2)}, u32[]{:S(2)}) async-start(bf16[16,272,128]{2,1,0:T(8,128)(2,1)} %pack_queries.1), calls=%async_computation | async-start | bytes 2228224 | tf_op jit(solution)/shard_map/all_to_all | solution.py:365
  71.9 1.1 slice.6
  73.0 1.1 slice.7
  74.1 1.9 %collective-permute-start.11 = (bf16[1,512,512]{2,1,0:T(8,128)(2,1)S(1)}, bf16[1,512,512]{2,1,0:T(8,128)(2,1)}, u32[]{:S(2)}, u32[]{:S(2)}) collective-permute-start(bf16[1,512,512]{2,1,0:T(8,128)(2,1)S(1)} %slice.6), channel_id=1, source_target_pairs={{0,32},{8,40},{16,48},{24,56},{32,64},{40,72},{48,80},{56,88},{64,... | collective-permute-start | bytes 1572872 | tf_op jit(solution)/shard_map/ppermute | solution.py:335
  75.9 1.5 collective-permute-start.12
  77.4 13.1 %project.5.refs_6_ = f32[1024,1024]{1,0:T(8,128)} custom-call(s32[6]{0:T(128)S(1)} %stack.115.idx, bf16[1024,8192]{1,0:T(8,128)(2,1)} %bitcast.34, bf16[1024,8192]{1,0:T(8,128)(2,1)} %bitcast.35, bf16[1024,8192]{1,0:T(8,128)(2,1)} %bitcast.36, bf16[1024,8192]{1,0:T(8,128)(2,1)} %bitcast.37, bf16[1024,8192]{1,0:T(8,128)(2,1)} %bitcast.38, ...), custom_call_target="tpu_custom_call" | custom-call | flops 6442450944 | bytes 12582912 | tf_op jit(solution)/shard_map/project/pallas_call | solution.py:90
  90.5 8.9 %collective-permute-done.11.refs_2_ = bf16[1,512,512]{2,1,0:T(8,128)(2,1)} collective-permute-done((bf16[1,512,512]{2,1,0:T(8,128)(2,1)S(1)}, bf16[1,512,512]{2,1,0:T(8,128)(2,1)}, u32[]{:S(2)}, u32[]{:S(2)}) %collective-permute-start.11) | collective-permute-done | bytes 524320 | tf_op jit(solution)/shard_map/ppermute | solution.py:335
  99.5 0.5 collective-permute-start.19
  100.1 0.6 collective-permute-start.24
  100.8 0.9 collective-permute-done.18.refs_4_
  101.7 1.5 collective-permute-done.19.refs_5_
  103.2 8.2 %attend.1 = bf16[16,272,128]{2,1,0:T(8,128)(2,1)} custom-call(s32[10]{0:T(128)S(1)} %pad_add_fusion.1.idx, bf16[1024,8192]{1,0:T(8,128)(2,1)} %bitcast.40, bf16[1024,8192]{1,0:T(8,128)(2,1)} %bitcast.41, bf16[1,512,512]{2,1,0:T(8,128)(2,1)} %collective-permute-done.11.refs_2_, bf16[1,512,512]{2,1,0:T(8,128)(2,1)} %collective-permute-done.12.refs_3_, ...), custom_call_target="tpu_custom_call" | custom-call | tf_op jit(solution)/shard_map/attend/pallas_call | solution.py:213
  111.4 5.2 %all-to-all-start.1 = ((bf16[16,272,128]{2,1,0:T(8,128)(2,1)}), bf16[16,272,128]{2,1,0:T(8,128)(2,1)S(1)}, u32[]{:S(2)}, u32[]{:S(2)}) async-start(bf16[16,272,128]{2,1,0:T(8,128)(2,1)} %attend.1), calls=%async_computation.1 | async-start | bytes 2228224 | tf_op jit(solution)/shard_map/all_to_all | solution.py:384
  116.6 0.4 collective-permute-start.25
  117.0 0.2 collective-permute-start.26
  117.2 18.1 %all-to-all-done.1.parts = bf16[16,272,128]{2,1,0:T(8,128)(2,1)S(1)} async-done(((bf16[16,272,128]{2,1,0:T(8,128)(2,1)}), bf16[16,272,128]{2,1,0:T(8,128)(2,1)S(1)}, u32[]{:S(2)}, u32[]{:S(2)}) %all-to-all-start.1) | async-done | bytes 1114144 | tf_op jit(solution)/shard_map/all_to_all | solution.py:384
  135.3 1.0 combine.1.refs_0_
  136.3 1.9 %collective-permute-start.20 = (bf16[208,512]{1,0:T(8,128)(2,1)S(1)}, bf16[208,512]{1,0:T(8,128)(2,1)S(1)}, u32[]{:S(2)}, u32[]{:S(2)}) collective-permute-start(bf16[208,512]{1,0:T(8,128)(2,1)S(1)} %combine.1.refs_0_), channel_id=1, source_target_pairs={{0,2},{1,3},{2,4},{3,5},{4,6},{5,7},{6,0},{7,1},{8,10},{9,11},{10,... | collective-permute-start | bytes 638984 | tf_op jit(solution)/shard_map/ppermute | solution.py:338
  138.2 1.4 collective-permute-start.21
  139.7 0.7 collective-permute-start.22
  140.5 8.5 %collective-permute-done.20.refs_1_ = bf16[208,512]{1,0:T(8,128)(2,1)S(1)} collective-permute-done((bf16[208,512]{1,0:T(8,128)(2,1)S(1)}, bf16[208,512]{1,0:T(8,128)(2,1)S(1)}, u32[]{:S(2)}, u32[]{:S(2)}) %collective-permute-start.20) | collective-permute-done | bytes 213024 | tf_op jit(solution)/shard_map/ppermute | solution.py:338
  149.0 3.4 %mix.3 = bf16[208,1024]{1,0:T(8,128)(2,1)S(1)} custom-call(s32[2]{0:T(128)S(1)} %pad_add_fusion.3.place, bf16[208,512]{1,0:T(8,128)(2,1)S(1)} %combine.1.refs_0_, bf16[208,512]{1,0:T(8,128)(2,1)S(1)} %collective-permute-done.20.refs_1_, bf16[208,512]{1,0:T(8,128)(2,1)S(1)} %collective-permute-done.21.refs_2_, ...), custom_call_target="tpu_custom_call" | custom-call | flops 872415232 | bytes 4194304 | tf_op jit(solution)/shard_map/mix/pallas_call | solution.py:292
  152.3 0.8 collective-permute-start.27
  153.2 3.4 %mix.2 = f32[208,1024]{1,0:T(8,128)S(1)} custom-call(s32[2]{0:T(128)S(1)} %pad_add_fusion.place, bf16[208,512]{1,0:T(8,128)(2,1)S(1)} %combine.1.refs_0_, bf16[208,512]{1,0:T(8,128)(2,1)S(1)} %collective-permute-done.20.refs_1_, bf16[208,512]{1,0:T(8,128)(2,1)S(1)} %collective-permute-done.21.refs_2_, bf16[208,512]{1,0:T(8,128)(2,1)S(1)} %collective-permute-done.22.refs_3_, ...), custom_call_target="tpu_custom_call" | custom-call | flops 872415232 | bytes 4194304 | tf_op jit(solution)/shard_map/mix/pallas_call | solution.py:292
  156.6 6.0 %collective-permute-done.27 = bf16[208,1024]{1,0:T(8,128)(2,1)S(1)} collective-permute-done((bf16[208,1024]{1,0:T(8,128)(2,1)S(1)}, bf16[208,1024]{1,0:T(8,128)(2,1)S(1)}, u32[]{:S(2)}, u32[]{:S(2)}) %collective-permute-start.27) | collective-permute-done | bytes 426016 | tf_op jit(solution)/shard_map/ppermute | solution.py:392
  162.7 0.9 concatenate.7
  (53 shorter events, 1.1 us)
Async XLA Ops:
  0.0 13.1 %collective-permute-start.4 = (bf16[2,512,512]{2,1,0:T(8,128)(2,1)}, bf16[2,512,512]{2,1,0:T(8,128)(2,1)}, u32[]{:S(2)}, u32[]{:S(2)}) collective-permute-start(bf16[2,512,512]{2,1,0:T(8,128)(2,1)} %refs_2_.2), channel_id=1, source_target_pairs={{0,8},{8,0},{16,24},{24,16},{32,40},{40,32},{48,56},{56,48},{64,72... | collective-permute-start | bytes 3145736 | tf_op jit(solution)/shard_map/ppermute | solution.py:335
  0.0 28.2 %collective-permute-start.2 = (bf16[2,512,512]{2,1,0:T(8,128)(2,1)}, bf16[2,512,512]{2,1,0:T(8,128)(2,1)S(1)}, u32[]{:S(2)}, u32[]{:S(2)}) collective-permute-start(bf16[2,512,512]{2,1,0:T(8,128)(2,1)} %refs_2_.2), channel_id=1, source_target_pairs={{0,32},{8,40},{16,48},{24,56},{32,64},{40,72},{48,80},{56,88},{64,... | collective-permute-start | bytes 3145736 | tf_op jit(solution)/shard_map/ppermute | solution.py:335
  2.0 26.2 %collective-permute-start.3 = (bf16[2,512,512]{2,1,0:T(8,128)(2,1)}, bf16[2,512,512]{2,1,0:T(8,128)(2,1)S(1)}, u32[]{:S(2)}, u32[]{:S(2)}) collective-permute-start(bf16[2,512,512]{2,1,0:T(8,128)(2,1)} %refs_2_.2), channel_id=1, source_target_pairs={{0,96},{8,104},{16,112},{24,120},{32,0},{40,8},{48,16},{56,24},{64... | collective-permute-start | bytes 3145736 | tf_op jit(solution)/shard_map/ppermute | solution.py:335
  4.2 27.1 %collective-permute-start = (bf16[2,512,512]{2,1,0:T(8,128)(2,1)}, bf16[2,512,512]{2,1,0:T(8,128)(2,1)}, u32[]{:S(2)}, u32[]{:S(2)}) collective-permute-start(bf16[2,512,512]{2,1,0:T(8,128)(2,1)} %refs_2_.2), channel_id=1, source_target_pairs={{0,16},{8,24},{16,0},{24,8},{32,48},{40,56},{48,32},{56,40},{64,80... | collective-permute-start | bytes 3145736 | tf_op jit(solution)/shard_map/ppermute | solution.py:335
  7.5 5.6 %copy-start.2 = (bf16[2,512,512]{2,1,0:T(8,128)(2,1)S(1)}, bf16[2,512,512]{2,1,0:T(8,128)(2,1)}, u32[]{:S(2)}) copy-start(bf16[2,512,512]{2,1,0:T(8,128)(2,1)} %refs_2_.2) | copy-start | bytes 3145732
  12.0 1.0 copy-start.4
  12.0 7.7 %copy-start.5 = (bf16[256,2048]{1,0:T(8,128)(2,1)}, bf16[256,2048]{1,0:T(8,128)(2,1)S(1)}, u32[]{:S(2)}) copy-start(bf16[256,2048]{1,0:T(8,128)(2,1)S(1)} %get-tuple-element.34) | copy-start | bytes 3145732
  13.1 18.2 %copy-start.7 = (s32[128]{0:T(128)S(1)}, s32[128]{0:T(128)}, u32[]{:S(2)}) copy-start(s32[128]{0:T(128)} %param.11) | copy-start | bytes 1540
  13.1 26.6 %copy-start.6 = (s32[1,4,2,128]{3,2,1,0:T(2,128)S(1)}, s32[1,4,2,128]{3,2,1,0:T(2,128)}, u32[]{:S(2)}) copy-start(s32[1,4,2,128]{3,2,1,0:T(2,128)} %param.10) | copy-start | bytes 12292
  28.2 8.4 %collective-permute-start.6 = (bf16[2,512,512]{2,1,0:T(8,128)(2,1)S(1)}, bf16[2,512,512]{2,1,0:T(8,128)(2,1)}, u32[]{:S(2)}, u32[]{:S(2)}) collective-permute-start(bf16[2,512,512]{2,1,0:T(8,128)(2,1)S(1)} %collective-permute-done.2.refs_6_), channel_id=1, source_target_pairs={{0,8},{8,0},{16,24},{24,16},{32,40},{40,32},{48,56},{56,48},{64,72... | collective-permute-start | bytes 3145736 | tf_op jit(solution)/shard_map/ppermute | solution.py:335
  28.2 1.0 copy-start
  29.2 10.1 %collective-permute-start.7 = (bf16[2,512,512]{2,1,0:T(8,128)(2,1)S(1)}, bf16[2,512,512]{2,1,0:T(8,128)(2,1)}, u32[]{:S(2)}, u32[]{:S(2)}) collective-permute-start(bf16[2,512,512]{2,1,0:T(8,128)(2,1)S(1)} %collective-permute-done.3.refs_8_), channel_id=1, source_target_pairs={{0,8},{8,0},{16,24},{24,16},{32,40},{40,32},{48,56},{56,48},{64,72... | collective-permute-start | bytes 3145736 | tf_op jit(solution)/shard_map/ppermute | solution.py:335
  31.3 8.0 %collective-permute-start.8 = (bf16[2,512,512]{2,1,0:T(8,128)(2,1)}, bf16[2,512,512]{2,1,0:T(8,128)(2,1)}, u32[]{:S(2)}, u32[]{:S(2)}) collective-permute-start(bf16[2,512,512]{2,1,0:T(8,128)(2,1)} %collective-permute-done.refs_10_), channel_id=1, source_target_pairs={{0,8},{8,0},{16,24},{24,16},{32,40},{40,32},{48,56},{56,48},{64,72... | collective-permute-start | bytes 3145736 | tf_op jit(solution)/shard_map/ppermute | solution.py:335
  31.5 30.6 %collective-permute-start.5 = (bf16[2,512,512]{2,1,0:T(8,128)(2,1)S(1)}, bf16[2,512,512]{2,1,0:T(8,128)(2,1)}, u32[]{:S(2)}, u32[]{:S(2)}) collective-permute-start(bf16[2,512,512]{2,1,0:T(8,128)(2,1)S(1)} %collective-permute-done.3.refs_8_), channel_id=1, source_target_pairs={{0,16},{8,24},{16,0},{24,8},{32,48},{40,56},{48,32},{56,40},{64,80... | collective-permute-start | bytes 3145736 | tf_op jit(solution)/shard_map/ppermute | solution.py:335
  34.8 31.4 %collective-permute-start.13 = (bf16[2,512,512]{2,1,0:T(8,128)(2,1)S(1)}, bf16[2,512,512]{2,1,0:T(8,128)(2,1)}, u32[]{:S(2)}, u32[]{:S(2)}) collective-permute-start(bf16[2,512,512]{2,1,0:T(8,128)(2,1)S(1)} %collective-permute-done.3.refs_8_), channel_id=1, source_target_pairs={{0,96},{8,104},{16,112},{24,120},{32,0},{40,8},{48,16},{56,24},{64... | collective-permute-start | bytes 3145736 | tf_op jit(solution)/shard_map/ppermute | solution.py:335
  36.5 25.6 %collective-permute-start.10 = (bf16[256,2048]{1,0:T(8,128)(2,1)}, bf16[256,2048]{1,0:T(8,128)(2,1)S(1)}, u32[]{:S(2)}, u32[]{:S(2)}) collective-permute-start(bf16[256,2048]{1,0:T(8,128)(2,1)} %copy-done.5), channel_id=1, source_target_pairs={{0,6},{1,7},{2,0},{3,1},{4,2},{5,3},{6,4},{7,5},{8,14},{9,15},{10,... | collective-permute-start | bytes 3145736 | tf_op jit(solution)/shard_map/ppermute | solution.py:338
  39.3 26.3 %collective-permute-start.9 = (bf16[256,2048]{1,0:T(8,128)(2,1)}, bf16[256,2048]{1,0:T(8,128)(2,1)}, u32[]{:S(2)}, u32[]{:S(2)}) collective-permute-start(bf16[256,2048]{1,0:T(8,128)(2,1)} %copy-done.4), channel_id=1, source_target_pairs={{0,2},{1,3},{2,4},{3,5},{4,6},{5,7},{6,0},{7,1},{8,10},{9,11},{10,... | collective-permute-start | bytes 3145736 | tf_op jit(solution)/shard_map/ppermute | solution.py:338
  39.3 26.3 %collective-permute-start.1 = (bf16[2,512,512]{2,1,0:T(8,128)(2,1)}, bf16[2,512,512]{2,1,0:T(8,128)(2,1)}, u32[]{:S(2)}, u32[]{:S(2)}) collective-permute-start(bf16[2,512,512]{2,1,0:T(8,128)(2,1)} %collective-permute-done.refs_10_), channel_id=1, source_target_pairs={{0,32},{8,40},{16,48},{24,56},{32,64},{40,72},{48,80},{56,88},{64,... | collective-permute-start | bytes 3145736 | tf_op jit(solution)/shard_map/ppermute | solution.py:335
  39.7 1.2 copy-start.1
  40.9 12.4 %copy-start.3 = (bf16[256,512]{1,0:T(8,128)(2,1)S(1)}, bf16[256,512]{1,0:T(8,128)(2,1)}, u32[]{:S(2)}) copy-start(bf16[256,512]{1,0:T(8,128)(2,1)} %query.1) | copy-start | bytes 786436
  65.6 10.3 %collective-permute-start.15 = (bf16[2,512,512]{2,1,0:T(8,128)(2,1)}, bf16[2,512,512]{2,1,0:T(8,128)(2,1)}, u32[]{:S(2)}, u32[]{:S(2)}) collective-permute-start(bf16[2,512,512]{2,1,0:T(8,128)(2,1)} %collective-permute-done.1.refs_8_), channel_id=1, source_target_pairs={{0,8},{8,0},{16,24},{24,16},{32,40},{40,32},{48,56},{56,48},{64,72... | collective-permute-start | bytes 3145736 | tf_op jit(solution)/shard_map/ppermute | solution.py:335
  65.6 11.8 %collective-permute-start.16 = (bf16[2,512,512]{2,1,0:T(8,128)(2,1)}, bf16[2,512,512]{2,1,0:T(8,128)(2,1)}, u32[]{:S(2)}, u32[]{:S(2)}) collective-permute-start(bf16[2,512,512]{2,1,0:T(8,128)(2,1)} %collective-permute-done.5.refs_10_), channel_id=1, source_target_pairs={{0,8},{8,0},{16,24},{24,16},{32,40},{40,32},{48,56},{56,48},{64,72... | collective-permute-start | bytes 3145736 | tf_op jit(solution)/shard_map/ppermute | solution.py:335
  66.1 11.3 %collective-permute-start.14 = (bf16[2,512,512]{2,1,0:T(8,128)(2,1)}, bf16[2,512,512]{2,1,0:T(8,128)(2,1)}, u32[]{:S(2)}, u32[]{:S(2)}) collective-permute-start(bf16[2,512,512]{2,1,0:T(8,128)(2,1)} %collective-permute-done.13.refs_6_), channel_id=1, source_target_pairs={{0,8},{8,0},{16,24},{24,16},{32,40},{40,32},{48,56},{56,48},{64,72... | collective-permute-start | bytes 3145736 | tf_op jit(solution)/shard_map/ppermute | solution.py:335
  66.1 33.2 %collective-permute-start.17 = (bf16[256,2048]{1,0:T(8,128)(2,1)}, bf16[256,2048]{1,0:T(8,128)(2,1)}, u32[]{:S(2)}, u32[]{:S(2)}) collective-permute-start(bf16[256,2048]{1,0:T(8,128)(2,1)} %get-tuple-element.40), channel_id=1, source_target_pairs={{0,4},{1,5},{2,6},{3,7},{4,0},{5,1},{6,2},{7,3},{8,12},{9,13},{10,... | collective-permute-start | bytes 3145736 | tf_op jit(solution)/shard_map/ppermute | solution.py:338
  68.1 31.3 %all-to-all-start = ((bf16[16,272,128]{2,1,0:T(8,128)(2,1)}), bf16[16,272,128]{2,1,0:T(8,128)(2,1)S(1)}, u32[]{:S(2)}, u32[]{:S(2)}) async-start(bf16[16,272,128]{2,1,0:T(8,128)(2,1)} %pack_queries.1), calls=%async_computation | async-start | bytes 2228224 | tf_op jit(solution)/shard_map/all_to_all | solution.py:365
  74.1 25.3 %collective-permute-start.11 = (bf16[1,512,512]{2,1,0:T(8,128)(2,1)S(1)}, bf16[1,512,512]{2,1,0:T(8,128)(2,1)}, u32[]{:S(2)}, u32[]{:S(2)}) collective-permute-start(bf16[1,512,512]{2,1,0:T(8,128)(2,1)S(1)} %slice.6), channel_id=1, source_target_pairs={{0,32},{8,40},{16,48},{24,56},{32,64},{40,72},{48,80},{56,88},{64,... | collective-permute-start | bytes 1572872 | tf_op jit(solution)/shard_map/ppermute | solution.py:335
  75.9 23.4 %collective-permute-start.12 = (bf16[1,512,512]{2,1,0:T(8,128)(2,1)S(1)}, bf16[1,512,512]{2,1,0:T(8,128)(2,1)}, u32[]{:S(2)}, u32[]{:S(2)}) collective-permute-start(bf16[1,512,512]{2,1,0:T(8,128)(2,1)S(1)} %slice.7), channel_id=1, source_target_pairs={{0,96},{8,104},{16,112},{24,120},{32,0},{40,8},{48,16},{56,24},{64... | collective-permute-start | bytes 1572872 | tf_op jit(solution)/shard_map/ppermute | solution.py:335
  99.4 2.3 %collective-permute-start.18 = (bf16[1,512,512]{2,1,0:T(8,128)(2,1)}, bf16[1,512,512]{2,1,0:T(8,128)(2,1)}, u32[]{:S(2)}, u32[]{:S(2)}) collective-permute-start(bf16[1,512,512]{2,1,0:T(8,128)(2,1)} %collective-permute-done.11.refs_2_), channel_id=1, source_target_pairs={{0,8},{8,0},{16,24},{24,16},{32,40},{40,32},{48,56},{56,48},{64,72... | collective-permute-start | bytes 1572872 | tf_op jit(solution)/shard_map/ppermute | solution.py:335
  99.5 3.7 %collective-permute-start.19 = (bf16[1,512,512]{2,1,0:T(8,128)(2,1)}, bf16[1,512,512]{2,1,0:T(8,128)(2,1)}, u32[]{:S(2)}, u32[]{:S(2)}) collective-permute-start(bf16[1,512,512]{2,1,0:T(8,128)(2,1)} %collective-permute-done.12.refs_3_), channel_id=1, source_target_pairs={{0,8},{8,0},{16,24},{24,16},{32,40},{40,32},{48,56},{56,48},{64,72... | collective-permute-start | bytes 1572872 | tf_op jit(solution)/shard_map/ppermute | solution.py:335
  100.0 38.3 %collective-permute-start.23 = (bf16[256,2048]{1,0:T(8,128)(2,1)S(1)}, bf16[256,2048]{1,0:T(8,128)(2,1)}, u32[]{:S(2)}, u32[]{:S(2)}) collective-permute-start(bf16[256,2048]{1,0:T(8,128)(2,1)S(1)} %get-tuple-element.45.refs_4_), channel_id=1, source_target_pairs={{0,8},{8,0},{16,24},{24,16},{32,40},{40,32},{48,56},{56,48},{64,72... | collective-permute-start | bytes 3145736 | tf_op jit(solution)/shard_map/ppermute | solution.py:335
  100.1 39.5 %collective-permute-start.24 = (bf16[256,2048]{1,0:T(8,128)(2,1)}, bf16[256,2048]{1,0:T(8,128)(2,1)}, u32[]{:S(2)}, u32[]{:S(2)}) collective-permute-start(bf16[256,2048]{1,0:T(8,128)(2,1)} %collective-permute-done.9.refs_5_), channel_id=1, source_target_pairs={{0,8},{8,0},{16,24},{24,16},{32,40},{40,32},{48,56},{56,48},{64,72... | collective-permute-start | bytes 3145736 | tf_op jit(solution)/shard_map/ppermute | solution.py:335
  111.4 24.0 %all-to-all-start.1 = ((bf16[16,272,128]{2,1,0:T(8,128)(2,1)}), bf16[16,272,128]{2,1,0:T(8,128)(2,1)S(1)}, u32[]{:S(2)}, u32[]{:S(2)}) async-start(bf16[16,272,128]{2,1,0:T(8,128)(2,1)} %attend.1), calls=%async_computation.1 | async-start | bytes 2228224 | tf_op jit(solution)/shard_map/all_to_all | solution.py:384
  116.6 23.9 %collective-permute-start.25 = (bf16[256,2048]{1,0:T(8,128)(2,1)S(1)}, bf16[256,2048]{1,0:T(8,128)(2,1)}, u32[]{:S(2)}, u32[]{:S(2)}) collective-permute-start(bf16[256,2048]{1,0:T(8,128)(2,1)S(1)} %collective-permute-done.10.refs_6_), channel_id=1, source_target_pairs={{0,8},{8,0},{16,24},{24,16},{32,40},{40,32},{48,56},{56,48},{64,72... | collective-permute-start | bytes 3145736 | tf_op jit(solution)/shard_map/ppermute | solution.py:335
  117.0 23.4 %collective-permute-start.26 = (bf16[256,2048]{1,0:T(8,128)(2,1)}, bf16[256,2048]{1,0:T(8,128)(2,1)}, u32[]{:S(2)}, u32[]{:S(2)}) collective-permute-start(bf16[256,2048]{1,0:T(8,128)(2,1)} %collective-permute-done.17.refs_7_), channel_id=1, source_target_pairs={{0,8},{8,0},{16,24},{24,16},{32,40},{40,32},{48,56},{56,48},{64,72... | collective-permute-start | bytes 3145736 | tf_op jit(solution)/shard_map/ppermute | solution.py:335
  136.3 12.6 %collective-permute-start.20 = (bf16[208,512]{1,0:T(8,128)(2,1)S(1)}, bf16[208,512]{1,0:T(8,128)(2,1)S(1)}, u32[]{:S(2)}, u32[]{:S(2)}) collective-permute-start(bf16[208,512]{1,0:T(8,128)(2,1)S(1)} %combine.1.refs_0_), channel_id=1, source_target_pairs={{0,2},{1,3},{2,4},{3,5},{4,6},{5,7},{6,0},{7,1},{8,10},{9,11},{10,... | collective-permute-start | bytes 638984 | tf_op jit(solution)/shard_map/ppermute | solution.py:338
  138.2 10.7 %collective-permute-start.21 = (bf16[208,512]{1,0:T(8,128)(2,1)S(1)}, bf16[208,512]{1,0:T(8,128)(2,1)S(1)}, u32[]{:S(2)}, u32[]{:S(2)}) collective-permute-start(bf16[208,512]{1,0:T(8,128)(2,1)S(1)} %combine.1.refs_0_), channel_id=1, source_target_pairs={{0,6},{1,7},{2,0},{3,1},{4,2},{5,3},{6,4},{7,5},{8,14},{9,15},{10,... | collective-permute-start | bytes 638984 | tf_op jit(solution)/shard_map/ppermute | solution.py:338
  139.7 9.3 %collective-permute-start.22 = (bf16[208,512]{1,0:T(8,128)(2,1)S(1)}, bf16[208,512]{1,0:T(8,128)(2,1)S(1)}, u32[]{:S(2)}, u32[]{:S(2)}) collective-permute-start(bf16[208,512]{1,0:T(8,128)(2,1)S(1)} %combine.1.refs_0_), channel_id=1, source_target_pairs={{0,4},{1,5},{2,6},{3,7},{4,0},{5,1},{6,2},{7,3},{8,12},{9,13},{10,... | collective-permute-start | bytes 638984 | tf_op jit(solution)/shard_map/ppermute | solution.py:338
  152.3 10.3 %collective-permute-start.27 = (bf16[208,1024]{1,0:T(8,128)(2,1)S(1)}, bf16[208,1024]{1,0:T(8,128)(2,1)S(1)}, u32[]{:S(2)}, u32[]{:S(2)}) collective-permute-start(bf16[208,1024]{1,0:T(8,128)(2,1)S(1)} %mix.3), channel_id=1, source_target_pairs={{0,1},{1,0},{2,3},{3,2},{4,5},{5,4},{6,7},{7,6},{8,9},{9,8},{10,11... | collective-permute-start | bytes 1277960 | tf_op jit(solution)/shard_map/ppermute | solution.py:392
